TPU v7x, 32 devices: a whole 2x2x4 slice. The times are simulated.
32 devices in a mesh: seq: 32 (over z, y, x, core).
Axes of the slice: x: 2, y: 2, z: 4, core: 2. Of those that a mesh axis runs over, the one named last changes fastest.
Arguments:
- hidden: bfloat16 [65536, 1024], P('seq'), may hold values from -6 to 6
- scene_lengths: int32 [16], replicated, may hold values from 1 to 32768, 65536 in all
- norm_gain: float32 [1024], replicated, may hold values from 0.1 to 1.9
- w_in: bfloat16 [1024, 4384], replicated, may hold values from -0.1875 to 0.1875
- conv_weight: float32 [4, 2304], replicated, may hold values from -3 to 3
- conv_bias: float32 [2304], replicated, may hold values from -2 to 2
- dt_bias: float32 [32], replicated, may hold values from -4.5 to -3.5
- a_log: float32 [32], replicated, may hold values from -11 to 0.7
- d_skip: float32 [32], replicated, may hold values from 0.5 to 1.5
- gate_gain: float32 [2048], replicated, may hold values from 0.1 to 1.9
- w_out: bfloat16 [2048, 1024], replicated, may hold values from -0.125 to 0.125
- out_grad: bfloat16 [65536, 1024], P('seq'), may hold values from -6 to 6
Outputs:
- mixed_out: bfloat16 [65536, 1024], P('seq')
- hidden_grad: float32 [65536, 1024], P('seq')
- norm_gain_grad: float32 [1024], replicated
- w_in_grad: float32 [1024, 4384], P('seq')
- conv_weight_grad: float32 [4, 2304], replicated
- conv_bias_grad: float32 [2304], replicated
- dt_bias_grad: float32 [32], replicated
- a_log_grad: float32 [32], replicated
- d_skip_grad: float32 [32], replicated
- gate_gain_grad: float32 [2048], replicated
- w_out_grad: float32 [2048, 1024], P(None, 'seq')
Inputs may be any that keep to these rules, and one draw needn't show every extreme that they name: `scene_lengths`: scenes follow each other in the stream; they sum to 65536 tokens and the longest has exactly 32768.
All inputs are finite; a program needn't handle non-finite values.
Results may differ from a plain program's by a relative error of at most 0.0014.
The roundings to bfloat16 on the way count: a program that leaves them out, or rounds other values in their place, can miss the bound.
Values may be sent and summed in bfloat16 or wider, within the bound.
No kernel may reach another device: no remote copies, remote signals or barrier semaphores. Data moves between devices by JAX's collectives and lax.ppermute only.
A program may use at most 1.0625 GiB of HBM per device.

v0:
```python
import jax
import jax.numpy as jnp
from jax import lax
from jax.sharding import PartitionSpec as P

QB = 256


norm_eps = 1e-05
highest = lax.Precision.HIGHEST


def from_behind(value, axis, steps):
    count = lax.axis_size(axis)
    first, last = (max(0, -steps), min(count, count - steps))
    return lax.ppermute(value, axis, [(source, source + steps) for source in range(first, last)])


def entering_2(value, axis, join, neutral, backward):
    count, mine = (lax.axis_size(axis), lax.axis_index(axis))
    pieces = jax.tree.map(lambda part: lax.all_gather(part, axis), value)
    if backward:
        pieces = jax.tree.map(lambda part: part[::-1], pieces)
        mine = count - 1 - mine
    subtotal = jax.tree.map(
        lambda part, zero: jnp.full_like(part, 0) + jnp.asarray(zero, part.dtype), value, neutral
    )

    def turn(position, subtotal):
        longer = join(subtotal, jax.tree.map(lambda part: part[position], pieces))
        return jax.tree.map(lambda new, old: jnp.where(position < mine, new, old), longer, subtotal)

    return lax.fori_loop(0, count - 1, turn, subtotal)


def scene_marks(starts, position):
    before = starts[None, :] <= position[:, None]
    begins = jnp.max(jnp.where(before, starts[None, :], 0), axis=1)
    resets = jnp.any(starts[None, :] == position[:, None], axis=1)
    return (begins, resets)


def rms_scale(values, gain_row):
    return (
        values * lax.rsqrt(jnp.mean(values * values, axis=1, keepdims=True) + norm_eps) * gain_row
    )


def combine_states(earlier, later_part):
    return (earlier[0] * later_part[0], later_part[0][:, None, None] * earlier[1] + later_part[1])


def body(
    hidden,
    scene_lengths,
    norm_gain,
    w_in,
    conv_weight,
    conv_bias,
    dt_bias,
    a_log,
    d_skip,
    gate_gain,
    w_out,
    out_grad,
):
    local_rows = hidden.shape[0]
    head_count = a_log.shape[0]
    inner_width = gate_gain.shape[0]
    channel_count = conv_bias.shape[0]
    state_width = (channel_count - inner_width) // 2
    head_width = inner_width // head_count
    conv_taps = conv_weight.shape[0]
    rim_width = conv_taps - 1
    block_count = local_rows // QB
    position = lax.axis_index("seq") * local_rows + jnp.arange(local_rows, dtype=jnp.int32)
    starts = jnp.cumsum(scene_lengths) - scene_lengths
    begins, resets = scene_marks(starts, position)
    segment = jnp.cumsum(resets.astype(jnp.int32).reshape(block_count, QB), axis=1)
    ordering = jnp.arange(QB)
    same_scene = (segment[:, :, None] == segment[:, None, :]) & (
        ordering[:, None] >= ordering[None, :]
    )[None]
    carry_live = (segment == 0).astype(jnp.float32)
    tail_live = (segment == segment[:, -1:]).astype(jnp.float32)
    opened = (segment[:, -1] == 0).astype(jnp.float32)
    valid_taps = [
        (position - (rim_width - tap_index) >= begins).astype(jnp.float32)[:, None]
        for tap_index in range(conv_taps)
    ]

    def prepare(extended, conv_weight, conv_bias, dt_raw, dt_bias, a_log):
        conv_sum = jnp.zeros((local_rows, channel_count), jnp.float32) + conv_bias
        for tap_index in range(conv_taps):
            conv_sum = (
                conv_sum
                + conv_weight[tap_index]
                * extended[tap_index : tap_index + local_rows]
                * valid_taps[tap_index]
            )
        activated = jax.nn.silu(conv_sum)
        x_heads = activated[:, :inner_width].reshape(block_count, QB, head_count, head_width)
        b_rows = activated[:, inner_width : inner_width + state_width].reshape(
            block_count, QB, state_width
        )
        c_rows = activated[:, inner_width + state_width :].reshape(block_count, QB, state_width)
        step_size = jax.nn.softplus(dt_raw + dt_bias).reshape(block_count, QB, head_count)
        log_decay = jnp.cumsum(step_size * -jnp.exp(a_log), axis=1)
        tail_weight = jnp.exp(log_decay[:, -1:, :] - log_decay) * tail_live[:, :, None] * step_size
        block_state = jnp.einsum(
            "cshp,csn->chpn", tail_weight[..., None] * x_heads, b_rows, precision=highest
        )
        block_decay = jnp.exp(log_decay[:, -1, :]) * opened[:, None]

        def fold_block(running, element):
            return (
                (running[0] * element[1][:, None, None] + element[0], running[1] * element[1]),
                None,
            )

        start_pair = (
            jnp.zeros((head_count, head_width, state_width), jnp.float32),
            jnp.ones((head_count,), jnp.float32),
        )
        (dev_state, dev_decay), _ = lax.scan(fold_block, start_pair, (block_state, block_decay))
        return (
            x_heads,
            b_rows,
            c_rows,
            step_size,
            log_decay,
            block_state,
            block_decay,
            dev_state,
            dev_decay,
        )

    def finish(
        x_heads,
        b_rows,
        c_rows,
        step_size,
        log_decay,
        block_state,
        block_decay,
        state_in,
        gate_z,
        d_skip,
        gate_gain,
    ):

        def advance(running, element):
            return (running * element[1][:, None, None] + element[0], running)

        _, entering = lax.scan(advance, state_in, (block_state, block_decay))
        scores = jnp.einsum("ctn,csn->cts", c_rows, b_rows, precision=highest)
        decay_gaps = log_decay[:, :, None, :] - log_decay[:, None, :, :]
        weights = jnp.exp(jnp.where(same_scene[..., None], decay_gaps, -jnp.inf))
        mixing = scores[..., None] * weights * step_size[:, None, :, :]
        inside = jnp.einsum("ctsh,cshp->cthp", mixing, x_heads, precision=highest)
        carried = (
            jnp.einsum("ctn,chpn->cthp", c_rows, entering, precision=highest)
            * (jnp.exp(log_decay) * carry_live[..., None])[..., None]
        )
        ssd_out = inside + carried + d_skip[:, None] * x_heads
        gated = ssd_out.reshape(local_rows, inner_width) * jax.nn.silu(gate_z)
        return rms_scale(gated, gate_gain)

    hidden_wide = hidden.astype(jnp.float32)
    normed, norm_back = jax.vjp(rms_scale, hidden_wide, norm_gain)
    normed_low = normed.astype(jnp.bfloat16)
    projected = jnp.dot(normed_low, w_in, preferred_element_type=jnp.float32)
    gate_z = projected[:, :inner_width]
    xbc_low = projected[:, inner_width : inner_width + channel_count].astype(jnp.bfloat16)
    dt_raw = projected[:, inner_width + channel_count :]
    rim_rows = from_behind(xbc_low[local_rows - rim_width :], "seq", 1)
    extended = jnp.concatenate([rim_rows, xbc_low], axis=0).astype(jnp.float32)
    prepared, prepare_back = jax.vjp(
        prepare, extended, conv_weight, conv_bias, dt_raw, dt_bias, a_log
    )
    (
        x_heads,
        b_rows,
        c_rows,
        step_size,
        log_decay,
        block_state,
        block_decay,
        dev_state,
        dev_decay,
    ) = prepared
    identity_pair = (jnp.ones_like(dev_decay), jnp.zeros_like(dev_state))
    _, state_in = entering_2((dev_decay, dev_state), "seq", combine_states, identity_pair, False)
    gate_norm, finish_back = jax.vjp(
        finish,
        x_heads,
        b_rows,
        c_rows,
        step_size,
        log_decay,
        block_state,
        block_decay,
        state_in,
        gate_z,
        d_skip,
        gate_gain,
    )
    gate_low = gate_norm.astype(jnp.bfloat16)
    mixed_out = (hidden_wide + jnp.dot(gate_low, w_out, preferred_element_type=jnp.float32)).astype(
        jnp.bfloat16
    )
    grad_gate = jnp.einsum("td,id->ti", out_grad, w_out, preferred_element_type=jnp.float32)
    (
        x_heads_grad,
        b_rows_grad,
        c_rows_grad,
        step_grad,
        decay_log_grad,
        block_state_grad,
        block_decay_grad,
        state_in_grad,
        gate_z_grad,
        d_skip_grad,
        gate_gain_grad,
    ) = finish_back(grad_gate)
    _, state_out_grad = entering_2(
        (dev_decay, state_in_grad), "seq", combine_states, identity_pair, True
    )
    dev_decay_grad = jnp.sum(state_out_grad * state_in, axis=(1, 2))
    extended_grad, conv_weight_grad, conv_bias_grad, dt_raw_grad, dt_bias_grad, a_log_grad = (
        prepare_back(
            (
                x_heads_grad,
                b_rows_grad,
                c_rows_grad,
                step_grad,
                decay_log_grad,
                block_state_grad,
                block_decay_grad,
                state_out_grad,
                dev_decay_grad,
            )
        )
    )
    rim_grad = from_behind(extended_grad[:rim_width], "seq", -1)
    xbc_grad = extended_grad[rim_width:] + jnp.pad(rim_grad, ((local_rows - rim_width, 0), (0, 0)))
    projected_grad = jnp.concatenate([gate_z_grad, xbc_grad, dt_raw_grad], axis=1).astype(
        jnp.bfloat16
    )
    normed_grad = jnp.einsum("te,de->td", projected_grad, w_in, preferred_element_type=jnp.float32)
    hidden_part, norm_gain_grad = norm_back(normed_grad)
    hidden_grad = out_grad.astype(jnp.float32) + hidden_part
    w_in_grad = lax.psum_scatter(
        jnp.einsum("tk,te->ke", normed_low, projected_grad, preferred_element_type=jnp.float32),
        "seq",
        scatter_dimension=0,
        tiled=True,
    )
    w_out_grad = lax.psum_scatter(
        jnp.einsum("tk,ti->ki", out_grad, gate_low, preferred_element_type=jnp.float32),
        "seq",
        scatter_dimension=0,
        tiled=True,
    ).T
    summed = lax.psum(
        (
            norm_gain_grad,
            conv_weight_grad,
            conv_bias_grad,
            dt_bias_grad,
            a_log_grad,
            d_skip_grad,
            gate_gain_grad,
        ),
        "seq",
    )
    return (
        mixed_out,
        hidden_grad,
        summed[0],
        w_in_grad,
        summed[1],
        summed[2],
        summed[3],
        summed[4],
        summed[5],
        summed[6],
        w_out_grad,
    )


def solution(mesh):
    return jax.shard_map(
        body,
        mesh=mesh,
        in_specs=(P("seq", None), P(), P(), P(), P(), P(), P(), P(), P(), P(), P(), P("seq", None)),
        out_specs=(
            P("seq", None),
            P("seq", None),
            P(),
            P("seq", None),
            P(),
            P(),
            P(),
            P(),
            P(),
            P(),
            P(None, "seq"),
        ),
        check_vma=False,
    )
```

profile of v0, /device:TPU:0, one launch (start us, length us, event | category | flops | bytes accessed | tf_op | source)
XLA Modules:
  0.0 1615.0 jit_solution(9347187744961002551)
XLA Ops:
  10.9 29.3 %fusion.135 = (bf16[2048,4384]{0,1:T(8,128)(2,1)}, f32[2048,4384]{0,1:T(8,128)}) fusion(bf16[1024,4384]{0,1:T(8,128)(2,1)} %param.27, bf16[2048,1024]{1,0:T(8,128)(2,1)} %param.24, f32[1024]{0:T(1024)} %param.26, f32[2048]{0:T(1024)S(1)} %fusion.122), kind=kOutput, calls=%fused_computation.223 | convolution fusion | flops 18405195776 | bytes 67055616 | tf_op jit(solution)/shard_map/dot_general | solution.py:172
  79.2 47.0 %fusion.40 = (f32[2048,2304]{0,1:T(8,128)}, f32[2048,2304]{0,1:T(8,128)}) fusion(f32[2048]{0:T(1024)S(1)} %get-tuple-element.904, f32[2051,2304]{0,1:T(8,128)} %maximum_convert_fusion, f32[2304]{0:T(1024)S(1)} %get-tuple-element.783, f32[2048]{0:T(1024)S(1)} %get-tuple-element.905, f32[2304]{0:T(1024)S(1)} %get-tuple-element.784, ...), kind=kLoop, calls=%fused_computation.76 | loop fusion | flops 75497472 | bytes 113325056 | tf_op jit(solution)/shard_map/jvp(jit(silu))/mul | solution.py:101
  147.6 26.3 %fusion.56 = f32[8,32,64,128]{3,2,1,0:T(8,128)} fusion(f32[8,256,128,1]{2,1,3,0:T(8,128)S(1)} %copy.273, f32[8,256,32,64]{1,0,3,2:T(8,128)} %bitcast.311, f32[8,256,32]{1,2,0:T(8,128)} %get-tuple-element.902), kind=kOutput, calls=%fused_computation.113 | convolution fusion | flops 6446645248 | bytes 26476544 | tf_op jit(solution)/shard_map/jvp(cshp,csn->chpn)/dot_general | solution.py:110
  202.4 43.6 %all-reduce.14 = f32[1024]{0:T(1024)S(1)} all-reduce(f32[1024]{0:T(1024)S(1)} %dynamic-update-slice), channel_id=2, replica_groups=mesh['seq'=32] {'seq'}, use_global_device_ids=true, to_apply=%add.14 | all-reduce | flops 1024 | bytes 8192
  257.7 141.1 %all-gather.6.cloned.1.call-done = f32[1024,64,128]{2,1,0:T(8,128)} async-done(((f32[32,64,128]{2,1,0:T(8,128)}), f32[1024,64,128]{2,1,0:T(8,128)}) %all-gather.6.cloned.1.call-update) | async-done | bytes 33554448 | tf_op jit(solution)/shard_map/all_gather | solution.py:21
  398.8 46.5 %while.103 = (s32[]{:T(128)}, f32[32,64,128]{2,1,0:T(8,128)S(1)}, s32[]{:T(128)}, f32[32,32]{1,0:T(8,128)S(1)}, f32[32,32,64,128]{3,2,1,0:T(8,128)}, /*index=5*/s32[]{:T(128)}, s32[]{:T(128)}) while((s32[]{:T(128)}, f32[32,64,128]{2,1,0:T(8,128)S(1)}, s32[]{:T(128)}, f32[32,32]{1,0:T(8,128)S(1)}, ...), condition=%wide.region_11.12_spmd.clone, body=%wide.region_10.11_spmd.clone.sunk | while | flops 1048580 | bytes 3146217 | solution.py:33
  488.8 88.6 %fusion.48 = f32[8,256,32,64]{1,3,2,0:T(8,128)} fusion(f32[8,256,32,64]{1,3,2,0:T(8,128)} %fusion.137, f32[8,256,32,64]{1,0,3,2:T(8,128)} %bitcast.312, f32[8,256,32]{1,2,0:T(8,128)S(1)} %bitcast.347, f32[8,256,32]{1,2,0:T(8,128)S(1)} %copy-done.26, f32[8,256,256]{2,1,0:T(8,128)S(1)} %copy-done.23, pred[8,256,256]{2,1,0:T(8,128)(4,1)S(1)} %copy-done.28, ...), kind=kOutput, calls=%fused_computation.92 | convolution fusion | flops 12968787968 | bytes 53739648 | tf_op jit(solution)/shard_map/jvp(ctsh,cshp->cthp)/dot_general | solution.py:160
  644.4 36.5 %multiply_reduce_fusion.6 = (f32[2048]{0:T(1024)}, f32[2048,2048]{0,1:T(8,128)}, bf16[2048,2048]{0,1:T(8,128)(2,1)}) fusion(f32[2048,2304]{0,1:T(8,128)} %get-tuple-element.883, f32[2048,4384]{0,1:T(8,128)} %get-tuple-element.908, f32[2048,2048]{0,1:T(8,128)} %get-tuple-element.880, f32[2048]{0:T(1024)S(1)} %multiply_multiply_fusion.7, ...), kind=kLoop, calls=%fused_computation.94 | loop fusion | flops 83884032 | bytes 109084672 | tf_op jit(solution)/shard_map/transpose(jvp())/reduce_sum | solution.py:165
  715.7 24.2 %while.104 = (s32[]{:T(128)}, f32[32,64,128]{2,1,0:T(8,128)S(1)}, f32[8,32,64,128]{3,2,1,0:T(8,128)}, f32[8,32]{1,0:T(8,128)S(1)}, f32[8,32,64,128]{3,2,1,0:T(8,...) while((s32[]{:T(128)}, f32[32,64,128]{2,1,0:T(8,128)S(1)}, ...), condition=%wide.region_19.20_spmd.clone, body=%wide.region_17.19_spmd.clone.sunk | while | flops 1572836 | bytes 6292364 | solution.py:155
  741.0 36.4 %fusion.98 = f32[8,256,128]{2,1,0:T(8,128)S(1)} fusion(f32[8,32,64,128]{3,2,1,0:T(8,128)} %get-tuple-element.1346, f32[8,256,32,64]{1,0,3,2:T(8,128)} %bitcast.317, f32[8,256,32]{1,2,0:T(8,128)S(1)} %copy-done.22), kind=kOutput, calls=%fused_computation.147 | convolution fusion | flops 6446645248 | bytes 26476544 | tf_op jit(solution)/shard_map/transpose(jvp(ctn,chpn->cthp))/dot_general | solution.py:162
  777.5 114.8 %fusion.24 = (f32[8,256,32]{1,2,0:T(8,128)}, f32[8,256,32]{1,2,0:T(8,128)}, f32[8,256,32]{1,2,0:T(8,128)}, f32[8,256,256]{2,1,0:T(8,128)S(1)}) fusion(f32[8,256,32]{1,2,0:T(8,128)S(1)} %bitcast.348, f32[8,256,32]{1,2,0:T(8,128)S(1)} %copy-done.27, f32[8,256,256]{2,1,0:T(8,128)} %fusion.136, pred[8,256,256]{2,1,0:T(8,128)(4,1)S(1)} %copy-done.29, ...), kind=kOutput, calls=%fused_computation.50 | convolution fusion | flops 13102284800 | bytes 39583744 | tf_op jit(solution)/shard_map/transpose(jvp(ctsh,cshp->cthp))/dot_general | solution.py:160
  936.1 23.6 %rev.7 = f32[32,32,64,128]{3,2,1,0:T(8,128)} reverse(f32[32,32,64,128]{3,2,1,0:T(8,128)} %bitcast.328), dimensions={0} | reverse | bytes 67108864 | tf_op jit(solution)/shard_map/rev | solution.py:23
  959.7 46.8 %while.105 = (s32[]{:T(128)}, f32[32,64,128]{2,1,0:T(8,128)S(1)}, s32[]{:T(128)}, f32[32,32]{1,0:T(8,128)S(1)}, f32[32,32,64,128]{3,2,1,0:T(8,128)}, /*index=5*/s32[]{:T(128)}, s32[]{:T(128)}) while((s32[]{:T(128)}, f32[32,64,128]{2,1,0:T(8,128)S(1)}, s32[]{:T(128)}, f32[32,32]{1,0:T(8,128)S(1)}, ...), condition=%wide.region_21.22_spmd.clone, body=%wide.region_20.21_spmd.clone.sunk | while | flops 1048580 | bytes 3146217 | solution.py:33
  1011.3 32.7 %while.101 = (s32[]{:T(128)}, f32[32,64,128]{2,1,0:T(8,128)S(1)}, f32[32]{0:T(128)S(1)}, f32[8,32,64,128]{3,2,1,0:T(8,128)}, f32[8,32]{1,0:T(8,128)S(1)}, /*inde...) while((s32[]{:T(128)}, f32[32,64,128]{2,1,0:T(8,128)S(1)}, ...), condition=%wide.region_25.26_spmd, body=%wide.region_23.25_spmd.sunk | while | flops 786499 | bytes 5244565 | solution.py:125
  1044.5 38.6 %fusion.93 = f32[8,256,128]{2,1,0:T(8,128)} fusion(f32[8,32,64,128]{3,2,1,0:T(8,128)} %get-tuple-element.606, f32[8,32,64,128]{3,2,1,0:T(8,128)} %get-tuple-element.612, f32[8,256,32,64]{1,0,3,2:T(8,128)} %bitcast.314, f32[8,256,32]{1,2,0:T(8,128)S(1)} %copy-done.21), kind=kOutput, calls=%fused_computation.146 | convolution fusion | flops 6448742400 | bytes 34865152 | tf_op jit(solution)/shard_map/transpose(jvp(cshp,csn->chpn))/dot_general | solution.py:110
  1083.2 29.7 %multiply_reduce_fusion.8 = (f32[8,256,32]{1,2,0:T(8,128)S(1)}, f32[8,256,32,64]{1,3,2,0:T(8,128)}) fusion(f32[8,256,32,64]{1,0,3,2:T(8,128)} %bitcast.315, f32[8,256,128,1]{2,1,3,0:T(8,128)S(1)} %copy-done.13, f32[8,32,64,128]{3,2,1,0:T(8,128)} %get-tuple-element.606, f32[8,32,64,128]{3,2,1,0:T(8,128)} %get-tuple-element.612), kind=kOutput, calls=%fused_computation.96 | convolution fusion | flops 6452871168 | bytes 51642368 | tf_op jit(solution)/shard_map/transpose(jvp(cshp,csn->chpn))/dot_general | solution.py:110
  1120.7 73.9 %fusion.44 = f32[8,256,32,64]{1,3,2,0:T(8,128)} fusion(f32[8,256,32,64]{1,3,2,0:T(8,128)} %get-tuple-element.911, f32[8,256,32]{1,2,0:T(8,128)} %bitcast.346, f32[8,256,32]{1,2,0:T(8,128)} %copy-done.25, f32[8,256,256]{2,1,0:T(8,128)} %fusion.136, pred[8,256,256]{2,1,0:T(8,128)(4,1)} %compare_and_fusion, f32[8,256,32,64]{1,0,3,2:T(8,128)} %bitcast.320, ...), kind=kOutput, calls=%fused_computation.87 | convolution fusion | flops 12968787968 | bytes 53739648 | tf_op jit(solution)/shard_map/transpose(jvp(ctsh,cshp->cthp))/dot_general | solution.py:160
  1223.7 47.1 %multiply_reduce_fusion.4 = (f32[2304]{0:T(1024)}, f32[2304]{0:T(1024)}, f32[2304]{0:T(1024)}, f32[2304]{0:T(1024)}, f32[2304]{0:T(1024)}, /*index=5*/f32[2048,2304]{0,1:T(8,128)}) fusion(f32[2051,2304]{0,1:T(8,128)} %maximum_convert_fusion, f32[2048]{0:T(1024)S(1)} %copy-done.44, f32[2048]{0:T(1024)S(1)} %copy-done.46, f32[2048]{0:T(1024)S(1)} %copy-done.48, ...), kind=kLoop, calls=%fused_computation.74 | loop fusion | flops 113234688 | bytes 132199424 | tf_op jit(solution)/shard_map/transpose(jvp())/reduce_sum | solution.py:97
  1270.8 30.9 %multiply_multiply_fusion.3 = (f32[2048,2304]{0,1:T(8,128)}, f32[2048,2304]{0,1:T(8,128)}, f32[2048,2304]{0,1:T(8,128)}, f32[2048,2304]{0,1:T(8,128)}) fusion(f32[2048,2304]{0,1:T(8,128)} %get-tuple-element.878, f32[2048]{0:T(1024)S(1)} %copy-done.44, f32[2304]{0:T(1024)S(1)} %copy-done.54, f32[2048]{0:T(1024)S(1)} %copy-done.42, f32[2304]{0:T(1024)S(1)} %copy-done.50, ...), kind=kLoop, calls=%fused_computation.82 | loop fusion | flops 37748736 | bytes 94441472 | tf_op jit(solution)/shard_map/transpose(jvp())/mul | solution.py:97
  1328.0 33.8 %pad_add_fusion = f32[2051,2304]{0,1:T(8,128)} fusion(f32[2048,2304]{0,1:T(8,128)} %get-tuple-element.894, f32[2048,2304]{0,1:T(8,128)} %get-tuple-element.895, f32[2048,2304]{0,1:T(8,128)} %get-tuple-element.896, f32[2048,2304]{0,1:T(8,128)} %get-tuple-element.893), kind=kLoop, calls=%fused_computation.66 | loop fusion | flops 14176512 | bytes 94399488 | tf_op jit(solution)/shard_map/transpose(jvp())/add_any | solution.py:98
  1378.7 29.9 %fusion.87 = f32[1024,4384]{1,0:T(8,128)} fusion(bf16[2048,32]{0,1:T(8,128)(2,1)S(1)} %get-tuple-element.877, bf16[2048,2304]{0,1:T(8,128)(2,1)} %fusion.39, bf16[2048,2048]{0,1:T(8,128)(2,1)} %get-tuple-element.892, bf16[2048,1024]{1,0:T(8,128)(2,1)} %param.24, f32[1024]{0:T(1024)S(1)} %copy-done.86, f32[2048]{0:T(1024)S(1)} %copy-done.71), kind=kOutput, calls=%fused_computation.138 | convolution fusion | flops 18450087936 | bytes 40120320 | tf_op jit(solution)/shard_map/tk,te->ke/dot_general | solution.py:254
  1427.7 27.6 %fusion.77 = (f32[1024]{0:T(1024)S(1)}, f32[2048]{0:T(1024)S(1)}, f32[2048,1024]{1,0:T(8,128)}) fusion(bf16[2048,1024]{1,0:T(8,128)(2,1)S(1)} %copy-done.7, f32[2048]{0:T(1024)S(1)} %copy-done.71, f32[1024]{0:T(1024)S(1)} %copy-done.86, bf16[1024,4384]{0,1:T(8,128)(2,1)} %param.27, bf16[2048,32]{0,1:T(8,128)(2,1)S(1)} %get-tuple-element.877, ...), kind=kOutput, calls=%fused_computation.128 | convolution fusion | flops 18456377344 | bytes 39542784 | tf_op jit(solution)/shard_map/te,de->td/dot_general | solution.py:250
  1455.3 44.6 %all-reduce.15 = (f32[1024]{0:T(1024)}, f32[4,2304]{1,0:T(4,128)}, f32[2304]{0:T(1024)}, f32[32]{0:T(128)}, f32[32]{0:T(128)}, /*index=5*/f32[32]{0:T(128)}, f32[2048]{0:T(1024)}) all-reduce(f32[1024]{0:T(1024)S(1)} %get-tuple-element.779, f32[4,2304]{1,0:T(4,128)S(1)} %pad_add_fusion.2, ...), channel_id=1, replica_groups=mesh['seq'=32] {'seq'}, use_global_device_ids=true, to_apply=%region_36.37 | all-reduce | flops 14688 | bytes 117504 | tf_op jit(solution)/shard_map/psum | solution.py:265
  1509.8 98.4 %reduce-scatter.5.cloned.1.call-done = f32[32,4384]{1,0:T(8,128)} async-done(((f32[1024,4384]{1,0:T(8,128)}), f32[32,4384]{1,0:T(8,128)}) %reduce-scatter.5.cloned.1.call-update) | async-done | bytes 561168 | tf_op jit(solution)/shard_map/reduce_scatter | solution.py:253
  (598 shorter events, 595.9 us)
Async XLA Ops:
  7.2 391.6 %all-gather.6.cloned.1.call-start = ((), (), s32[]{:S(2)}) async-start(), calls=%async_computation.3 | async-start | bytes 34603008 | tf_op jit(solution)/shard_map/all_gather | solution.py:21
  10.9 43.1 %copy-start.68 = (f32[4,2304]{1,0:T(4,128)S(1)}, f32[4,2304]{1,0:T(4,128)}, u32[]{:S(2)}) copy-start(f32[4,2304]{1,0:T(4,128)} %param.28) | copy-start | bytes 110596
  41.8 21.6 %collective-permute-start = (bf16[3,2304]{1,0:T(4,128)(2,1)S(1)}, bf16[3,2304]{1,0:T(4,128)(2,1)S(1)}, u32[]{:S(2)}, u32[]{:S(2)}) collective-permute-start(bf16[3,2304]{1,0:T(4,128)(2,1)S(1)} %copy.228), channel_id=1, source_target_pairs={{0,1},{1,2},{2,3},{3,4},{4,5},{5,6},{6,7},{7,8},{8,9},{9,10},{10,1... | collective-permute-start | bytes 41480 | tf_op jit(solution)/shard_map/ppermute | solution.py:16
  47.4 152.9 %copy-start.8 = (f32[2048,32]{0,1:T(8,128)}, f32[2048,32]{0,1:T(8,128)S(1)}, u32[]{:S(2)}) copy-start(f32[2048,32]{0,1:T(8,128)S(1)} %compare_select_fusion.2) | copy-start | bytes 786436
  199.2 250.6 %copy-start.87 = (f32[8,32,1,1]{1,3,2,0:T(1,128)}, f32[8,32,1,1]{1,3,2,0:T(1,128)S(1)}, u32[]{:S(2)}) copy-start(f32[8,32,1,1]{1,3,2,0:T(1,128)S(1)} %get-tuple-element.1307) | copy-start | bytes 3076
  200.2 735.9 %all-gather.8.cloned.1.call-start = ((), (), s32[]{:S(2)}) async-start(), calls=%async_computation.4 | async-start | bytes 34603008 | tf_op jit(solution)/shard_map/all_gather | solution.py:21
  250.3 195.1 %copy-start.14 = (f32[8,256,128]{2,1,0:T(8,128)}, f32[8,256,128]{2,1,0:T(8,128)S(1)}, u32[]{:S(2)}) copy-start(f32[8,256,128]{2,1,0:T(8,128)S(1)} %copy.231) | copy-start | bytes 3145732
  470.3 107.1 %copy-start.74 = (f32[8,32]{1,0:T(8,128)}, f32[8,32]{1,0:T(8,128)S(1)}, u32[]{:S(2)}) copy-start(f32[8,32]{1,0:T(8,128)S(1)} %get-tuple-element.1358) | copy-start | bytes 3076
  626.8 267.8 %copy-start.72 = (f32[2048]{0:T(1024)}, f32[2048]{0:T(1024)S(1)}, u32[]{:S(2)}) copy-start(f32[2048]{0:T(1024)S(1)} %fusion.123) | copy-start | bytes 24580
  740.0 37.5 %copy-start.27 = (f32[8,256,32]{1,2,0:T(8,128)S(1)}, f32[8,256,32]{1,2,0:T(8,128)}, u32[]{:S(2)}) copy-start(f32[8,256,32]{1,2,0:T(8,128)} %copy-done.25) | copy-start | bytes 786436
  740.0 37.5 %copy-start.29 = (pred[8,256,256]{2,1,0:T(8,128)(4,1)S(1)}, pred[8,256,256]{2,1,0:T(8,128)(4,1)}, u32[]{:S(2)}) copy-start(pred[8,256,256]{2,1,0:T(8,128)(4,1)} %compare_and_fusion) | copy-start | bytes 1572868
  740.9 768.9 %reduce-scatter.7.cloned.1.call-start = ((), (), s32[]{:S(2)}) async-start(), calls=%async_computation.5 | async-start | bytes 8650752
  777.5 114.8 %copy-start.16 = (f32[8,256,128]{2,1,0:T(8,128)S(1)}, f32[8,256,128]{2,1,0:T(8,128)}, u32[]{:S(2)}) copy-start(f32[8,256,128]{2,1,0:T(8,128)} %copy.232) | copy-start | bytes 3145732
  936.0 672.2 %reduce-scatter.5.cloned.1.call-start = ((), (), s32[]{:S(2)}) async-start(), calls=%async_computation.2 | async-start | bytes 18923520 | tf_op jit(solution)/shard_map/reduce_scatter | solution.py:253
  936.1 70.5 %copy-start.6 = (f32[32,64,128]{2,1,0:T(8,128)S(1)}, f32[32,64,128]{2,1,0:T(8,128)}, u32[]{:S(2)}) copy-start(f32[32,64,128]{2,1,0:T(8,128)} %copy-done.5) | copy-start | bytes 3145732
  1006.9 37.6 %copy-start.21 = (f32[8,256,32]{1,2,0:T(8,128)S(1)}, f32[8,256,32]{1,2,0:T(8,128)}, u32[]{:S(2)}) copy-start(f32[8,256,32]{1,2,0:T(8,128)} %get-tuple-element.902) | copy-start | bytes 786436
  1044.5 38.6 %copy-start.13 = (f32[8,256,128,1]{2,1,3,0:T(8,128)S(1)}, f32[8,256,128,1]{2,1,3,0:T(8,128)}, u32[]{:S(2)}) copy-start(f32[8,256,128,1]{2,1,3,0:T(8,128)} %copy-done.12) | copy-start | bytes 3145732
  1083.2 37.6 %copy-start.95 = (f32[32]{0:T(128)S(1)}, f32[32]{0:T(128)}, u32[]{:S(2)}) copy-start(f32[32]{0:T(128)} %param.32) | copy-start | bytes 388
  1223.7 47.1 %copy-start.50 = (f32[2304]{0:T(1024)S(1)}, f32[2304]{0:T(1024)}, u32[]{:S(2)}) copy-start(f32[2304]{0:T(1024)} %copy-done.49) | copy-start | bytes 27652
  1223.7 47.1 %copy-start.52 = (f32[2304]{0:T(1024)S(1)}, f32[2304]{0:T(1024)}, u32[]{:S(2)}) copy-start(f32[2304]{0:T(1024)} %copy-done.51) | copy-start | bytes 27652
  1223.7 47.1 %copy-start.54 = (f32[2304]{0:T(1024)S(1)}, f32[2304]{0:T(1024)}, u32[]{:S(2)}) copy-start(f32[2304]{0:T(1024)} %copy-done.53) | copy-start | bytes 27652
  1223.7 47.1 %copy-start.56 = (f32[2304]{0:T(1024)S(1)}, f32[2304]{0:T(1024)}, u32[]{:S(2)}) copy-start(f32[2304]{0:T(1024)} %copy-done.55) | copy-start | bytes 27652
  1305.0 58.2 %collective-permute-start.1 = (f32[3,2304]{1,0:T(4,128)S(1)}, f32[3,2304]{1,0:T(4,128)S(1)}, u32[]{:S(2)}, u32[]{:S(2)}) collective-permute-start(f32[3,2304]{1,0:T(4,128)S(1)} %copy.259), channel_id=1, source_target_pairs={{1,0},{2,1},{3,2},{4,3},{5,4},{6,5},{7,6},{8,7},{9,8},{10,9},{11,1... | collective-permute-start | bytes 82952 | tf_op jit(solution)/shard_map/ppermute | solution.py:16
  1427.7 72.2 %copy-start.60 = (f32[2048]{0:T(1024)S(1)}, f32[2048]{0:T(1024)}, u32[]{:S(2)}) copy-start(f32[2048]{0:T(1024)} %copy-done.59) | copy-start | bytes 24580
  (80 other events, 1204.4 us)
Sparse Core Ops, SparseCore 0:
  200.3 198.4 all-gather.5
  741.1 192.9 all-gather.7
  936.9 146.9 reduce-scatter.6
  1408.8 199.3 reduce-scatter.4
where the time goes:
time: 1630 us; the launch traced here: 1620 us
  matrix products  597 us (37%)
  other arithmetic  474 us (29%)
  waiting for transfers between devices  240 us (15%)
  local copies, waits for them, and re-layouts  194 us (12%)
  blocking collectives  88.2 us (5%)
    dot_general x3, matrix products, finish(): inside = jnp.einsum('ctsh,cshp->cthp', mixing, x_heads, precision=highest)  277 us
    all_gather x2, waiting for transfers between devices, entering_2(): pieces = jax.tree.map(lambda part: lax.all_gather(part, axis), value)  141 us
    reduce_scatter x1, waiting for transfers between devices, body(): lax.psum_scatter(jnp.einsum('tk,te->ke', normed_low, projected_grad, pref...  98.4 us
    dot_general x3, matrix products, prepare(): jnp.einsum('cshp,csn->chpn', tail_weight[..., None] * x_heads, b_rows, pr...  94.6 us
    select_n x62, other arithmetic, turn(): jnp.where(position < mine, new, old)  90.9 us
    dot_general x3, matrix products, finish(): jnp.einsum('ctn,chpn->cthp', c_rows, entering, precision=highest)  73.6 us
    unnamed x206, local copies, waits for them, and re-layouts  61.6 us
    reduce_sum x1, other arithmetic, prepare(): conv_weight[tap_index] * extended[tap_index:tap_index + local_rows]  47.1 us
  transfers between devices with their start and end apart: 6, of which 2 were waited for; matrix products, arithmetic and copies ran while one was open for 47% of the time, Pallas kernels for 0%

commit v1 on v0

v1 whole, which is shorter than its diff:
```python
import functools

import jax
import jax.numpy as jnp
from jax import lax
from jax.experimental import pallas as pl
from jax.experimental.pallas import tpu as pltpu
from jax.sharding import PartitionSpec as P

Q = 128
LANES = 128
EPS = 1e-05
LOG2E = 1.4426950408889634
f32 = jnp.float32
bf16 = jnp.bfloat16
VMEM_BYTES = 60 << 20


def mm(a, b):
    return lax.dot_general(a, b, (((1,), (0,)), ((), ())), preferred_element_type=f32)


def mm_nt(a, b):
    return lax.dot_general(a, b, (((1,), (1,)), ((), ())), preferred_element_type=f32)


def mm_tn(a, b):
    return lax.dot_general(a, b, (((0,), (0,)), ((), ())), preferred_element_type=f32)


def split2(v):
    hi = v.astype(bf16)
    return hi, (v - hi.astype(f32)).astype(bf16)


def sigmoid(v):
    return 1.0 / (1.0 + jnp.exp(-v))


def lane_iota(rows):
    return lax.broadcasted_iota(jnp.int32, (rows, LANES), 1)


def spread(v, heads):
    hi = v.astype(bf16).astype(f32)
    rest = v - hi
    mid = rest.astype(bf16).astype(f32)
    low = rest - mid
    lane = lane_iota(v.shape[0])
    kept = jnp.where(lane < heads, hi, jnp.where(lane < 2 * heads, mid, low))
    return jnp.where(lane < 3 * heads, kept, 0.0).astype(bf16)


def exact3(v):
    hi = v.astype(bf16)
    rest = v - hi.astype(f32)
    mid = rest.astype(bf16)
    return hi, mid, (rest - mid.astype(f32)).astype(bf16)


def mask_mm(mask, v):
    hi, mid, low = exact3(v)
    return mm(mask, hi) + mm(mask, mid) + mm(mask, low)


def prod3(a_hi, a_lo, b_hi, b_lo):
    left = jnp.concatenate([a_hi, a_lo], axis=1)
    return mm(left, jnp.concatenate([b_hi, b_hi], axis=0)) + mm(a_hi, b_lo)


def head_sums(v, red):
    hi, lo = split2(v)
    return mm(hi, red) + mm(lo, red)


def tri_masks(begin_col, begin_row):
    row = lax.broadcasted_iota(jnp.int32, (Q, Q), 0)
    col = lax.broadcasted_iota(jnp.int32, (Q, Q), 1)
    same = jnp.broadcast_to(begin_col, (Q, Q)) == jnp.broadcast_to(begin_row, (Q, Q))
    return same & (row >= col), same & (row <= col)


def project_kernel(
    heads, inner, state,
    hid, rim, gain, w_x, w_bc, w_dt, cw, cb, dtb, alog, meta, expm,
    nl_o, xbc_o, x_o, bc_o, dsil_o, step_o, sig_o, la_o, cum_o, sloc_o, dst_o, ddec_o,
    ext, srun, cum,
):
    rows = hid.shape[0]
    channels = inner + 2 * state
    step_id = pl.program_id(0)

    @pl.when(step_id == 0)
    def _():
        ext[0:8, :] = rim[...]
        srun[...] = jnp.zeros_like(srun)
        cum[...] = jnp.zeros_like(cum)

    hv = hid[...].astype(f32)
    mean = jnp.mean(hv * hv, axis=1, keepdims=True)
    nl = (hv * lax.rsqrt(mean + EPS) * gain[...]).astype(bf16)
    nl_o[...] = nl

    v = mm(nl, w_dt[...]) + dtb[...]
    step = jnp.maximum(v, 0.0) + jnp.log1p(jnp.exp(-jnp.abs(v)))
    step_o[...] = step
    sig_o[...] = sigmoid(v)
    rate = -step * (jnp.exp(alog[...]) * LOG2E)

    m1, m2, m3 = meta[:, 1:2], meta[:, 2:3], meta[:, 3:4]
    width = 256
    for g in range(channels // width):
        cols = slice(g * width, (g + 1) * width)
        weights = w_x[:, cols] if g * width < inner else w_bc[...]
        low = mm(nl, weights).astype(bf16)
        xbc_o[:, cols] = low
        ext[8 : 8 + rows, cols] = low.astype(f32)
        conv = cb[:, cols] + cw[3:4, cols] * ext[8 : 8 + rows, cols]
        conv = conv + cw[2:3, cols] * (ext[7 : 7 + rows, cols] * m1)
        conv = conv + cw[1:2, cols] * (ext[6 : 6 + rows, cols] * m2)
        conv = conv + cw[0:1, cols] * (ext[5 : 5 + rows, cols] * m3)
        gate = sigmoid(conv)
        act = conv * gate
        dsil_o[:, cols] = gate + act * (1.0 - gate)
        if g * width < inner:
            x_o[:, cols] = act
        else:
            bc_o[...] = act
    ext[0:8, :] = ext[rows : rows + 8, :]

    row = lax.broadcasted_iota(jnp.int32, (Q, Q), 0)
    col = lax.broadcasted_iota(jnp.int32, (Q, Q), 1)
    tri = (row >= col).astype(bf16)
    for c in range(rows // Q):
        rs = slice(c * Q, (c + 1) * Q)
        la = mask_mm(tri, rate[rs])
        la_o[rs, :] = la
        cum_o[c * 8 : (c + 1) * 8, :] = cum[...]
        last = la[Q - 1 : Q, :]
        cum[...] = cum[...] + last
        weight = jnp.exp2(last - la) * meta[rs, 7:8] * step[rs]
        decay = jnp.exp2(last) * meta[c * Q + Q - 1 : c * Q + Q, 8:9]
        decay_x = mm(spread(jnp.broadcast_to(decay, (8, LANES)), heads), expm[...])
        weight_s = spread(weight, heads)
        bt_hi, bt_lo = split2(bc_o[rs, :state].T)
        for g in range(inner // width):
            cols = slice(g * width, (g + 1) * width)
            wx = x_o[rs, cols] * mm(weight_s, expm[:, cols])
            hi, lo = split2(wx)
            new = prod3(bt_hi, bt_lo, hi, lo)
            old = srun[:, cols]
            sloc_o[c, :, cols] = old
            srun[:, cols] = old * decay_x[0:1, cols] + new
        if c == rows // Q - 1:
            @pl.when(step_id == pl.num_programs(0) - 1)
            def _():
                live = meta[c * Q + Q - 1 : c * Q + Q, 9:10]
                total = jnp.exp2(cum[...]) * live
                ddec_o[...] = mm(spread(total, heads), expm[...])
                dst_o[...] = srun[...]


def scan_kernel(
    heads, inner, state,
    x, bc, step, la_r, meta, brow, sloc, nl, w_z, expm,
    y_o, z_o,
    usc,
):
    la = la_r[...]
    la_t = la.T
    mask, _ = tri_masks(meta[:, 0:1], brow[0])
    b_hi, b_lo = split2(bc[:, :state])
    c_hi, c_lo = split2(bc[:, state:])
    c_cat = jnp.concatenate([c_hi, c_lo], axis=1)
    scores = mm_nt(c_cat, jnp.concatenate([b_hi, b_hi], axis=1)) + mm_nt(c_hi, b_lo)
    scores = jnp.where(mask, scores, 0.0)
    step_s = spread(step[...], heads)
    carry_s = spread(jnp.exp2(la) * meta[:, 8:9], heads)
    lane = lane_iota(Q)
    head_width = inner // heads
    for j in range(inner // LANES):
        cols = slice(j * LANES, (j + 1) * LANES)
        u_hi, u_lo = split2(x[:, cols] * mm(step_s, expm[:, cols]))
        u_cat = jnp.concatenate([u_hi, u_lo], axis=1)
        right = jnp.concatenate([u_cat, u_cat], axis=0)
        lefts = []
        for e in range(2):
            h = 2 * j + e
            gap = jnp.minimum(la[:, h : h + 1] - la_t[h : h + 1, :], 0.0)
            w_hi, w_lo = split2(scores * jnp.exp2(gap))
            lefts.append(jnp.concatenate([w_hi, w_lo], axis=1))
        both = mm(jnp.concatenate(lefts, axis=0), right)
        both = both[:, :LANES] + both[:, LANES:]
        y = jnp.where(lane < head_width, both[:Q], both[Q:])
        s_hi, s_lo = split2(sloc[0, :, cols])
        carried = mm(c_cat, jnp.concatenate([s_hi, s_hi], axis=0)) + mm(c_hi, s_lo)
        y_o[:, cols] = y + carried * mm(carry_s, expm[:, cols])
    nlv = nl[...]
    for g in range(inner // 256):
        cols = slice(g * 256, (g + 1) * 256)
        z_o[:, cols] = mm(nlv, w_z[:, cols])


def gate_kernel(
    heads, inner, state,
    yss, x, z, og, w_out, s_in, bc, la_r, cum, meta, dsk, gain, expm, red,
    gl_o, dy_o, gz_o, rowdot_o, sin_o, dgain_o, dskip_o,
    gsc, ysc, ggsc, ssc,
):
    step_id = pl.program_id(0)

    @pl.when(step_id == 0)
    def _():
        sin_o[...] = jnp.zeros_like(sin_o)
        dgain_o[...] = jnp.zeros_like(dgain_o)
        dskip_o[...] = jnp.zeros_like(dskip_o)
        hi, lo = split2(s_in[...])
        ssc[0:state, :] = hi
        ssc[state : 2 * state, :] = hi
        ssc[2 * state :, :] = lo

    c_hi, c_lo = split2(bc[:, state:])
    c_cat = jnp.concatenate([c_hi, c_lo], axis=1)
    ct_hi, ct_lo = split2(bc[:, state:].T)
    enter_s = spread(jnp.exp2(la_r[...] + cum[0:1, :]) * meta[:, 9:10], heads)
    ogv = og[...]
    width = 256
    sq = jnp.zeros((Q, LANES), f32)
    dotted = jnp.zeros((Q, LANES), f32)
    for g in range(inner // width):
        cols = slice(g * width, (g + 1) * width)
        gg = mm_nt(ogv, w_out[cols, :])
        carried = mm(c_cat, ssc[0 : 2 * state, cols]) + mm(c_hi, ssc[2 * state :, cols])
        y = yss[:, cols] + carried * mm(enter_s, expm[:, cols])
        ysc[:, cols] = y
        zv = z[:, cols]
        gated = (y + dsk[:, cols] * x[:, cols]) * (zv * sigmoid(zv))
        gsc[:, cols] = gated
        ggsc[:, cols] = gg
        s = gated * gated
        d = gg * gain[:, cols] * gated
        for k in range(width // LANES):
            sq = sq + s[:, k * LANES : (k + 1) * LANES]
            dotted = dotted + d[:, k * LANES : (k + 1) * LANES]
    mean = jnp.sum(sq, axis=1, keepdims=True) / inner
    r = lax.rsqrt(mean + EPS)
    m = jnp.sum(dotted, axis=1, keepdims=True) / inner
    coeff = r * r * r * m
    rowdot = jnp.zeros((Q, LANES), f32)
    for g in range(inner // width):
        cols = slice(g * width, (g + 1) * width)
        gated = gsc[:, cols]
        gg = ggsc[:, cols]
        gn = gated * r
        gl_o[:, cols] = (gn * gain[:, cols]).astype(bf16)
        dgain_o[0:1, cols] += jnp.sum(gg * gn, axis=0, keepdims=True)
        grad_gated = r * (gain[:, cols] * gg) - gated * coeff
        zv = z[:, cols]
        sg = sigmoid(zv)
        sz = zv * sg
        dy = grad_gated * sz
        dy_o[:, cols] = dy
        ys = ysc[:, cols]
        xv = x[:, cols]
        gz_o[:, cols] = (
            grad_gated * (ys + dsk[:, cols] * xv) * (sg + sz * (1.0 - sg))
        ).astype(bf16)
        rowdot = rowdot + head_sums(dy * ys, red[cols, :])
        dskip_o[0:1, cols] += jnp.sum(dy * xv, axis=0, keepdims=True)
        hi, lo = split2(dy * mm(enter_s, expm[:, cols]))
        sin_o[:, cols] += prod3(ct_hi, ct_lo, hi, lo)
    rowdot_o[...] = rowdot


def back_kernel(
    heads, inner, state,
    x, bc, step_r, sig, la_r, cum, meta, brow, sloc, s_in, dyr, rowdot, dsil, xbc,
    d_in, s_out, dsk, cw, alog, expm, red,
    pg_o, dt_o, first_o, tail_o, dcw_o, small_o,
    ds, cgx, xb, wgt,
):
    step_id = pl.program_id(0)
    channels = inner + 2 * state

    @pl.when(step_id == 0)
    def _():
        ds[...] = d_in[...]
        cgx[Q:, :] = jnp.zeros_like(cgx[Q:, :])
        dcw_o[...] = jnp.zeros_like(dcw_o)
        small_o[...] = jnp.zeros_like(small_o)
        total = jnp.sum(d_in[...] * s_out[...], axis=0, keepdims=True)
        xb[...] = head_sums(jnp.broadcast_to(total, (8, inner)), red[...])

    @pl.when(step_id > 0)
    def _():
        cgx[Q:, :] = cgx[0:8, :]

    la = la_r[...]
    la_t = la.T
    mask, mask_t = tri_masks(meta[:, 0:1], brow[0])
    b32, c32 = bc[:, :state], bc[:, state:]
    b_hi, b_lo = split2(b32)
    c_hi, c_lo = split2(c32)
    b_cat = jnp.concatenate([b_hi, b_lo], axis=1)
    ct_hi, ct_lo = split2(c32.T)
    scores_t = mm_nt(b_cat, jnp.concatenate([c_hi, c_hi], axis=1)) + mm_nt(b_hi, c_lo)
    scores_t = jnp.where(mask_t, scores_t, 0.0)
    step = step_r[...]
    last = la[Q - 1 : Q, :]
    tail = meta[:, 7:8]
    step_s = spread(step, heads)
    carry_s = spread(jnp.exp2(la) * meta[:, 8:9], heads)
    tail_s = spread(jnp.exp2(last - la) * tail, heads)
    decay = jnp.exp2(last) * meta[Q - 1 : Q, 8:9]
    enter = jnp.exp2(cum[0:1, :]) * meta[0:1, 9:10]
    decay_s = spread(jnp.broadcast_to(decay, (8, LANES)), heads)
    enter_s = spread(jnp.broadcast_to(enter, (8, LANES)), heads)
    lane = lane_iota(Q)
    left_half = lane < inner // heads
    zero = jnp.zeros((Q, LANES), bf16)

    dg_t = jnp.zeros((Q, Q), f32)
    dc = jnp.zeros((Q, 2 * state), f32)
    db = jnp.zeros((Q, 2 * state), f32)
    xdu = jnp.zeros((Q, LANES), f32)
    xacc = jnp.zeros((8, LANES), f32)
    for j in range(inner // LANES):
        cols = slice(j * LANES, (j + 1) * LANES)
        xv = x[:, cols]
        dy = dyr[:, cols]
        step_x = mm(step_s, expm[:, cols])
        carry_x = mm(carry_s, expm[:, cols])
        tail_x = mm(tail_s, expm[:, cols])
        u = xv * step_x
        u_hi, u_lo = split2(u)
        dy_hi, dy_lo = split2(dy)
        dy_cat = jnp.concatenate([dy_hi, dy_lo], axis=1)
        rows = []
        for e in range(2):
            keep = left_half if e == 0 else ~left_half
            rows.append(
                jnp.concatenate([jnp.where(keep, u_hi, zero), jnp.where(keep, u_lo, zero)], axis=1)
            )
        right = jnp.concatenate(
            [jnp.concatenate([dy_hi, dy_hi], axis=1), jnp.concatenate([dy_lo, dy_lo], axis=1)], axis=0
        )
        dw = mm_nt(jnp.concatenate(rows, axis=0), right)
        dw = dw[:, :Q] + dw[:, Q:]
        lefts = []
        for e in range(2):
            h = 2 * j + e
            gap = jnp.minimum(la_t[h : h + 1, :] - la[:, h : h + 1], 0.0)
            decays = jnp.exp2(gap)
            w_hi, w_lo = split2(scores_t * decays)
            lefts.append(jnp.concatenate([w_hi, w_lo], axis=1))
            dg_t = dg_t + dw[e * Q : (e + 1) * Q] * decays
        both = mm(jnp.concatenate(lefts, axis=0), jnp.concatenate([dy_cat, dy_cat], axis=0))
        both = both[:, :LANES] + both[:, LANES:]
        du = jnp.where(left_half, both[:Q], both[Q:])
        d_out = ds[:, cols]
        d_hi, d_lo = split2(d_out)
        du = du + tail_x * (mm(b_cat, jnp.concatenate([d_hi, d_hi], axis=0)) + mm(b_hi, d_lo))
        xdu = xdu + head_sums(xv * du, red[cols, :])
        dx = dsk[:, cols] * dy + step_x * du
        cgx[0:Q, cols] = dx * dsil[:, cols]
        enter_x = mm(enter_s, expm[:, cols])[0:1]
        s_true = sloc[0, :, cols] + enter_x * s_in[:, cols]
        s_hi, s_lo = split2(s_true)
        v_hi, v_lo = split2(carry_x * dy)
        t_hi, t_lo = split2(tail_x * u)
        s_cat = jnp.concatenate([s_hi, s_lo], axis=0)
        d_cat = jnp.concatenate([d_hi, d_lo], axis=0)
        dc = dc + mm_nt(v_hi, s_cat) + mm_nt(v_lo, s_cat)
        db = db + mm_nt(t_hi, d_cat) + mm_nt(t_lo, d_cat)
        decay_x = mm(decay_s, expm[:, cols])[0:1]
        d_new = d_out * decay_x + prod3(ct_hi, ct_lo, v_hi, v_lo)
        ds[:, cols] = d_new
        total = jnp.sum(d_new * s_true, axis=0, keepdims=True)
        xacc = xacc + head_sums(jnp.broadcast_to(total, (8, LANES)), red[cols, :])

    g_hi, g_lo = split2(jnp.where(mask_t, dg_t, 0.0))
    db_all = db[:, :state] + db[:, state:] + (
        mm(g_hi, c_hi) + mm(g_lo, c_hi) + mm(g_hi, c_lo)
    )
    dc_all = dc[:, :state] + dc[:, state:] + (
        mm_tn(g_hi, b_hi) + mm_tn(g_lo, b_hi) + mm_tn(g_hi, b_lo)
    )
    cgx[0:Q, inner : inner + state] = db_all * dsil[:, inner : inner + state]
    cgx[0:Q, inner + state :] = dc_all * dsil[:, inner + state :]

    flow = rowdot[...] - step * xdu
    g = mask_mm(mask_t.astype(bf16), flow) + tail * xb[0:1, :]
    g = g * meta[:, 10:11]
    rate = jnp.exp(alog[...])
    dt = (xdu - g * rate) * sig[...]
    dt_o[...] = dt.astype(bf16)
    small_o[0:1, :] += jnp.sum(-g * step * rate, axis=0, keepdims=True)
    small_o[1:2, :] += jnp.sum(dt, axis=0, keepdims=True)
    xb[...] = xacc

    m1, m2, m3 = meta[:, 4:5], meta[:, 5:6], meta[:, 6:7]
    width = 128
    for k in range(channels // width):
        cols = slice(k * width, (k + 1) * width)
        e0 = cgx[0:Q, cols]
        e1 = cgx[1 : Q + 1, cols] * m1
        e2 = cgx[2 : Q + 2, cols] * m2
        e3 = cgx[3 : Q + 3, cols] * m3
        grad = cw[3:4, cols] * e0 + cw[2:3, cols] * e1 + cw[1:2, cols] * e2 + cw[0:1, cols] * e3
        pg_o[:, cols] = grad.astype(bf16)
        xf = xbc[:, cols].astype(f32)
        for tap, e in ((3, e0), (2, e1), (1, e2), (0, e3)):
            dcw_o[tap : tap + 1, cols] += jnp.sum(xf * e, axis=0, keepdims=True)
        dcw_o[4:5, cols] += jnp.sum(e0, axis=0, keepdims=True)

        @pl.when(step_id == 0)
        def _():
            tail_o[:, cols] = grad[Q - 8 :, :]

    @pl.when(step_id == pl.num_programs(0) - 1)
    def _():
        first_o[...] = cgx[0:8, :]


def chain_kernel(backward, pieces, out):
    count = pieces.shape[0]
    rows = out.shape[1]

    def turn(i, run):
        k = count - 1 - i if backward else i
        out[k] = run
        return run * pieces[k, rows : rows + 1, :] + pieces[k, 0:rows, :]

    lax.fori_loop(0, count, turn, jnp.zeros(out.shape[1:], f32))


def params(**more):
    return pltpu.CompilerParams(vmem_limit_bytes=VMEM_BYTES, **more)


def exchange(local, decay, backward):
    count = lax.axis_size("seq")
    rows, lanes = local.shape
    split = max(1, count // rows)
    per, width = rows * split // count, lanes // split
    parts = local.reshape(count, per, width)
    decays = jnp.tile(decay.reshape(split, 1, width), (count // split, 1, 1))
    parts = jnp.concatenate([parts, decays], axis=1)
    got = lax.all_to_all(parts, "seq", 0, 0, tiled=True)
    out = pl.pallas_call(
        functools.partial(chain_kernel, backward),
        out_shape=jax.ShapeDtypeStruct((count, per, width), f32),
        compiler_params=params(),
    )(got)
    return lax.all_to_all(out, "seq", 0, 0, tiled=True).reshape(rows, lanes)


def from_behind(value, steps):
    count = lax.axis_size("seq")
    first, last = max(0, -steps), min(count, count - steps)
    return lax.ppermute(value, "seq", [(s, s + steps) for s in range(first, last)])


def body(
    hidden, scene_lengths, norm_gain, w_in, conv_weight, conv_bias, dt_bias, a_log, d_skip,
    gate_gain, w_out, out_grad,
):
    tokens, model = hidden.shape
    heads = a_log.shape[0]
    inner = gate_gain.shape[0]
    channels = conv_bias.shape[0]
    state = (channels - inner) // 2
    chunks = tokens // Q
    repeat = LANES // heads
    columns = w_in.shape[1]

    scenes = scene_lengths.shape[0]
    order = jnp.arange(scenes)
    starts = jnp.sum(jnp.where(order[None, :] < order[:, None], scene_lengths[None, :], 0), axis=1)
    dev_start = lax.axis_index("seq") * tokens
    wide_pos = dev_start + jnp.arange(tokens + 8, dtype=jnp.int32)
    begin_all = jnp.max(jnp.where(starts[None, :] <= wide_pos[:, None], starts[None, :], 0), axis=1)
    begin, pos = begin_all[:tokens], wide_pos[:tokens]
    chunk_last = jnp.repeat(begin.reshape(chunks, Q)[:, -1], Q)
    chunk_start = pos // Q * Q
    inside = jnp.arange(tokens)
    notes = [
        begin,
        pos - 1 >= begin,
        pos - 2 >= begin,
        pos - 3 >= begin,
        (begin_all[1 : tokens + 1] <= pos) & (inside + 1 < tokens),
        (begin_all[2 : tokens + 2] <= pos) & (inside + 2 < tokens),
        (begin_all[3 : tokens + 3] <= pos) & (inside + 3 < tokens),
        begin == chunk_last,
        begin < chunk_start,
        begin < dev_start,
        begin != pos,
    ]
    meta = jnp.stack([n.astype(f32) for n in notes] + [jnp.zeros((tokens,), f32)] * (16 - len(notes)), axis=1)
    brow = begin.astype(f32).reshape(chunks, 1, Q)

    head_of = jnp.arange(inner) // (inner // heads)
    expm = (jnp.arange(LANES)[:, None] % heads == head_of[None, :]).astype(bf16)
    red = expm.T

    def four(v):
        return jnp.tile(v, repeat).reshape(1, LANES)

    gain_row = norm_gain.reshape(1, model)
    w_dt = jnp.tile(w_in[:, inner + channels :], (1, repeat))
    dsk = jnp.repeat(d_skip, inner // heads).reshape(1, inner)
    cb = conv_bias.reshape(1, channels)
    gate_row = gate_gain.reshape(1, inner)

    edge = hidden[tokens - 8 :].astype(f32)
    edge_low = (
        edge * lax.rsqrt(jnp.mean(edge * edge, axis=1, keepdims=True) + EPS) * norm_gain
    ).astype(bf16)
    edge_xbc = jnp.dot(
        edge_low, w_in[:, inner : inner + channels], preferred_element_type=f32
    ).astype(bf16)
    rim = from_behind(edge_xbc, 1).astype(f32)

    tb = 2 * Q
    whole = lambda shape: pl.BlockSpec(shape, lambda i: (0,) * len(shape), pipeline_mode=pl.Buffered(1))
    rowsb = lambda n, width: pl.BlockSpec((n, width), lambda i: (i, 0))
    sds = jax.ShapeDtypeStruct
    (nl, xbc, x, bc, dsil, step, sig, la, cum, sloc, dev_state, dev_decay) = pl.pallas_call(
        functools.partial(project_kernel, heads, inner, state),
        grid=(tokens // tb,),
        in_specs=[
            rowsb(tb, model), whole((8, channels)), whole((1, model)),
            pl.BlockSpec((model, inner), lambda i: (0, 1), pipeline_mode=pl.Buffered(1)),
            pl.BlockSpec((model, 2 * state), lambda i: (0, 2 * inner // (2 * state)), pipeline_mode=pl.Buffered(1)),
            whole((model, LANES)), whole((4, channels)), whole((1, channels)), whole((1, LANES)),
            whole((1, LANES)), rowsb(tb, 16), whole((LANES, inner)),
        ],
        out_specs=[
            rowsb(tb, model), rowsb(tb, channels), rowsb(tb, inner), rowsb(tb, 2 * state),
            rowsb(tb, channels), rowsb(tb, LANES), rowsb(tb, LANES), rowsb(tb, LANES),
            rowsb(tb // Q * 8, LANES), pl.BlockSpec((tb // Q, state, inner), lambda i: (i, 0, 0)),
            pl.BlockSpec((state, inner), lambda i: (0, 0)), pl.BlockSpec((8, inner), lambda i: (0, 0)),
        ],
        out_shape=[
            sds((tokens, model), bf16), sds((tokens, channels), bf16), sds((tokens, inner), f32),
            sds((tokens, 2 * state), f32), sds((tokens, channels), f32), sds((tokens, LANES), f32),
            sds((tokens, LANES), f32), sds((tokens, LANES), f32), sds((chunks * 8, LANES), f32),
            sds((chunks, state, inner), f32), sds((state, inner), f32), sds((8, inner), f32),
        ],
        scratch_shapes=[
            pltpu.VMEM((tb + 8, channels), f32), pltpu.VMEM((state, inner), f32), pltpu.VMEM((8, LANES), f32),
        ],
        compiler_params=params(),
    )(hidden, rim, gain_row, w_in, w_in, w_dt, conv_weight, cb, four(dt_bias), four(a_log), meta, expm)

    state_in = exchange(dev_state, dev_decay[0:1], False)

    yss, z = pl.pallas_call(
        functools.partial(scan_kernel, heads, inner, state),
        grid=(chunks,),
        in_specs=[
            rowsb(Q, inner), rowsb(Q, 2 * state), rowsb(Q, LANES), rowsb(Q, LANES), rowsb(Q, 16),
            pl.BlockSpec((1, 1, Q), lambda i: (i, 0, 0)),
            pl.BlockSpec((1, state, inner), lambda i: (i, 0, 0)),
            rowsb(Q, model), whole((model, inner)), whole((LANES, inner)),
        ],
        out_specs=[rowsb(Q, inner), rowsb(Q, inner)],
        out_shape=[sds((tokens, inner), f32), sds((tokens, inner), f32)],
        scratch_shapes=[pltpu.VMEM((8, LANES), f32)],
        compiler_params=params(),
    )(x, bc, step, la, meta, brow, sloc, nl, w_in, expm)

    gate_low, dy, gz, rowdot, state_in_grad, dgain, dskip = pl.pallas_call(
        functools.partial(gate_kernel, heads, inner, state),
        grid=(chunks,),
        in_specs=[
            rowsb(Q, inner), rowsb(Q, inner), rowsb(Q, inner), rowsb(Q, model), whole((inner, model)),
            whole((state, inner)), rowsb(Q, 2 * state), rowsb(Q, LANES), rowsb(8, LANES), rowsb(Q, 16),
            whole((1, inner)), whole((1, inner)), whole((LANES, inner)), whole((inner, LANES)),
        ],
        out_specs=[
            rowsb(Q, inner), rowsb(Q, inner), rowsb(Q, inner), rowsb(Q, LANES),
            pl.BlockSpec((state, inner), lambda i: (0, 0)), pl.BlockSpec((8, inner), lambda i: (0, 0)),
            pl.BlockSpec((8, inner), lambda i: (0, 0)),
        ],
        out_shape=[
            sds((tokens, inner), bf16), sds((tokens, inner), f32), sds((tokens, inner), bf16),
            sds((tokens, LANES), f32), sds((state, inner), f32), sds((8, inner), f32), sds((8, inner), f32),
        ],
        scratch_shapes=[
            pltpu.VMEM((Q, inner), f32), pltpu.VMEM((Q, inner), f32), pltpu.VMEM((Q, inner), f32),
            pltpu.VMEM((3 * state, inner), bf16),
        ],
        compiler_params=params(),
    )(yss, x, z, out_grad, w_out, state_in, bc, la, cum, meta, dsk, gate_row, expm, red)

    state_out_grad = exchange(state_in_grad, dev_decay[0:1], True)
    state_out = dev_state + dev_decay[0:1] * state_in

    mixed_out = (hidden.astype(f32) + jnp.dot(gate_low, w_out, preferred_element_type=f32)).astype(bf16)
    w_out_part = jnp.einsum("tk,ti->ki", out_grad, gate_low, preferred_element_type=f32)
    w_out_grad = lax.psum_scatter(w_out_part, "seq", scatter_dimension=0, tiled=True).T

    final = chunks - 1
    back = lambda n, width: pl.BlockSpec((n, width), lambda i: (final - i, 0))
    pg, dt_grad, first, tail, dcw, small = pl.pallas_call(
        functools.partial(back_kernel, heads, inner, state),
        grid=(chunks,),
        in_specs=[
            back(Q, inner), back(Q, 2 * state), back(Q, LANES), back(Q, LANES), back(Q, LANES),
            back(8, LANES), back(Q, 16), pl.BlockSpec((1, 1, Q), lambda i: (final - i, 0, 0)),
            pl.BlockSpec((1, state, inner), lambda i: (final - i, 0, 0)), whole((state, inner)),
            back(Q, inner), back(Q, LANES), back(Q, channels), back(Q, channels),
            whole((state, inner)), whole((state, inner)), whole((1, inner)), whole((4, channels)),
            whole((1, LANES)), whole((LANES, inner)), whole((inner, LANES)),
        ],
        out_specs=[
            back(Q, channels), back(Q, LANES),
            pl.BlockSpec((8, channels), lambda i: (0, 0)), pl.BlockSpec((8, channels), lambda i: (0, 0)),
            pl.BlockSpec((8, channels), lambda i: (0, 0)), pl.BlockSpec((8, LANES), lambda i: (0, 0)),
        ],
        out_shape=[
            sds((tokens, channels), bf16), sds((tokens, LANES), bf16), sds((8, channels), f32),
            sds((8, channels), f32), sds((8, channels), f32), sds((8, LANES), f32),
        ],
        scratch_shapes=[
            pltpu.VMEM((state, inner), f32), pltpu.VMEM((Q + 8, channels), f32), pltpu.VMEM((8, LANES), f32),
            pltpu.VMEM((8, LANES), f32),
        ],
        compiler_params=params(),
    )(
        x, bc, step, sig, la, cum, meta, brow, sloc, state_in, dy, rowdot, dsil, xbc,
        state_out_grad, state_out, dsk, conv_weight, four(a_log), expm, red,
    )

    rim_grad = from_behind(first, -1)
    last_pos = wide_pos[tokens - 3 : tokens]
    last_low = xbc[tokens - 3 :].astype(f32)
    cross = jnp.zeros((3, channels), f32)
    cross_taps = [jnp.zeros((channels,), f32)]
    for j in (3, 2, 1):
        count = j
        rows_here = jnp.arange(3 - count, 3)
        ok = (begin_all[tokens - 3 + 3 - count + j : tokens + j] <= last_pos[3 - count :]).astype(f32)
        e = rim_grad[0:count] * ok[:, None]
        cross = cross.at[3 - count :].add(conv_weight[3 - j] * e)
        cross_taps.append(jnp.sum(last_low[3 - count :] * e, axis=0))
    conv_weight_part = dcw[0:4] + jnp.stack(cross_taps[1:] + cross_taps[:1], axis=0)
    is_last = lax.axis_index("seq") == lax.axis_size("seq") - 1
    fixed = (tail + jnp.pad(cross, ((5, 0), (0, 0)))).astype(bf16)
    pg = lax.dynamic_update_slice(pg, jnp.where(is_last, tail.astype(bf16), fixed), (tokens - 8, 0))

    projected_grad = jnp.concatenate([gz, pg, dt_grad[:, :heads]], axis=1)
    normed_grad = jnp.einsum("te,de->td", projected_grad, w_in, preferred_element_type=f32)
    w_in_part = jnp.einsum("tk,te->ke", nl, projected_grad, preferred_element_type=f32)
    w_in_grad = lax.psum_scatter(w_in_part, "seq", scatter_dimension=0, tiled=True)

    hv = hidden.astype(f32)
    s = lax.rsqrt(jnp.mean(hv * hv, axis=1, keepdims=True) + EPS)
    gained = normed_grad * norm_gain
    inner_mean = jnp.mean(gained * hv, axis=1, keepdims=True)
    hidden_grad = out_grad.astype(f32) + s * gained - hv * (s * s * s * inner_mean)
    norm_gain_part = jnp.sum(normed_grad * hv * s, axis=0)

    dskip_part = jnp.sum(dskip[0].reshape(heads, inner // heads), axis=1)
    summed = lax.psum(
        (norm_gain_part, conv_weight_part, dcw[4], small[1, :heads], small[0, :heads], dskip_part, dgain[0]),
        "seq",
    )
    return (
        mixed_out, hidden_grad, summed[0], w_in_grad, summed[1], summed[2], summed[3], summed[4],
        summed[5], summed[6], w_out_grad,
    )


def solution(mesh):
    rep = P()
    return jax.shard_map(
        body,
        mesh=mesh,
        in_specs=(P("seq", None),) + (rep,) * 10 + (P("seq", None),),
        out_specs=(P("seq", None), P("seq", None), rep, P("seq", None), rep, rep, rep, rep, rep, rep, P(None, "seq")),
        check_vma=False,
    )
```

time: 1630 us -> 843 us (0.52)
  matrix products: 597 us -> 86.3 us
  other arithmetic: 474 us -> 24.2 us
  Pallas kernels: 0 us -> 355 us
  local copies, waits for them, and re-layouts: 194 us -> 38 us
  waiting for transfers between devices: 240 us -> 131 us
  blocking collectives: 88.2 us -> 171 us
    dot_general x18 -> x5, matrix products: 597 us -> 86.3 us  [the longest x1 28 us: body(): jnp.einsum('tk,te->ke', nl, projected_grad, preferred_element_type=f32)]
    pallas_call x0 -> x6, Pallas kernels: none -> 355 us  [the longest x1 174 us: body(): pl.pallas_call(functools.partial(back_kernel, heads, inner, state), grid=...]
    reduce_sum x26 -> x6, other arithmetic: 153 us -> 5.84 us  [the longest x1 3.13 us: body(): s = lax.rsqrt(jnp.mean(hv * hv, axis=1, keepdims=True) + EPS)]
    all_gather x2 -> x0, waiting for transfers between devices: 141 us -> none  [entering_2(): pieces = jax.tree.map(lambda part: lax.all_gather(part, axis), value)]
    all_to_all x0 -> x2, blocking collectives: none -> 123 us  [exchange(): got = lax.all_to_all(parts, 'seq', 0, 0, tiled=True)]
    select_n x63 -> x2, other arithmetic: 92.1 us -> 0.01 us  [the longest x1 0.01 us: body(): head_of = jnp.arange(inner) // (inner // heads)]
    mul x14 -> x2, other arithmetic: 79.2 us -> 0.82 us  [the longest x1 0.81 us: body(): cross_taps.append(jnp.sum(last_low[3 - count:] * e, axis=0))]
    unnamed x1 -> x0, blocking collectives: 43.6 us -> none
  transfers between devices with their start and end apart: 6 -> 6, of which waited for: 2 -> 3; matrix products, arithmetic and copies ran while one was open for 47% -> 14% of each run, Pallas kernels for 0% -> 28%
where the time goes in v1:
time: 843 us; the launch traced here: 835 us
  Pallas kernels  355 us (42%)
  blocking collectives  171 us (20%)
  waiting for transfers between devices  131 us (16%)
  matrix products  86.3 us (10%)
  local copies, waits for them, and re-layouts  38 us (5%)
  other arithmetic  24.2 us (3%)
  between operations  16.2 us (2%)
  starting transfers between devices  13.2 us (2%)
    pallas_call x1, Pallas kernels, body(): pl.pallas_call(functools.partial(back_kernel, heads, inner, state), grid=...  174 us
    all_to_all x2, blocking collectives, exchange(): got = lax.all_to_all(parts, 'seq', 0, 0, tiled=True)  123 us
    reduce_scatter x1, waiting for transfers between devices, body(): lax.psum_scatter(w_in_part, 'seq', scatter_dimension=0, tiled=True)  101 us
    pallas_call x1, Pallas kernels, body(): pl.pallas_call(functools.partial(gate_kernel, heads, inner, state), grid=...  72.1 us
    pallas_call x1, Pallas kernels, body(): pl.pallas_call(functools.partial(scan_kernel, heads, inner, state), grid=...  57.7 us
    psum x1, blocking collectives, body(): lax.psum((norm_gain_part, conv_weight_part, dcw[4], small[1, :heads], sma...  48.2 us
    pallas_call x1, Pallas kernels, body(): pl.pallas_call(functools.partial(project_kernel, heads, inner, state), gr...  44.7 us
    all_to_all x2, waiting for transfers between devices, exchange(): return lax.all_to_all(out, 'seq', 0, 0, tiled=True).reshape(rows, lanes)  28.3 us
  transfers between devices with their start and end apart: 6, of which 3 were waited for; matrix products, arithmetic and copies ran while one was open for 14% of the time, Pallas kernels for 28%

profile of v1, /device:TPU:0, one launch (start us, length us, event | category | flops | bytes accessed | tf_op | source)
XLA Modules:
  0.0 835.2 jit_solution(17720408110248932673)
XLA Ops:
  8.0 3.7 fusion.10
  11.7 2.4 collective-permute-start
  16.3 12.1 %copy.69.w_x.w_bc.w_z = bf16[1024,4384]{1,0:T(8,128)(2,1)} copy(bf16[1024,4384]{0,1:T(8,128)(2,1)} %param.23) | data formatting | bytes 17956864 | tf_op args[3]
  33.2 44.7 %shard_map.208 = (bf16[2048,1024]{1,0:T(8,128)(2,1)}, bf16[2048,2304]{1,0:T(8,128)(2,1)}, f32[2048,2048]{1,0:T(8,128)}, f32[2048,256]{1,0:T(8,128)}, f32[2048,23...) custom-call(bf16[2048,1024]{1,0:T(8,128)(2,1)} %hid.1, ...), custom_call_target="tpu_custom_call" | custom-call | tf_op jit(solution)/shard_map/pallas_call | solution.py:529
  80.9 55.7 %all_to_all.20.pieces = f32[32,5,2048]{2,1,0:T(8,128)} all-to-all(f32[32,5,2048]{2,1,0:T(8,128)S(1)} %pad_maximum_fusion.4), channel_id=1, replica_groups=mesh['seq'=32] {'seq'}, dimensions={0} | all-to-all | bytes 2621440 | tf_op jit(solution)/shard_map/all_to_all | solution.py:449
  136.6 3.0 shard_map.210
  139.6 3.7 all-to-all-start.1
  145.3 57.7 %shard_map.209 = (f32[2048,2048]{1,0:T(8,128)}, f32[2048,2048]{1,0:T(8,128)}) custom-call(f32[2048,2048]{1,0:T(8,128)} %get-tuple-element.82.x, f32[2048,256]{1,0:T(8,128)} %get-tuple-element.83.bc, f32[2048,128]{1,0:T(8,128)} %get-tuple-element.84.step.step_r, f32[2048,128]{1,0:T(8,128)} %get-tuple-element.85.la_r, f32[2048,16]{1,0:T(8,128)} %copy.72.meta, ...), custom_call_target="tpu_custom_call" | custom-call | tf_op jit(solution)/shard_map/pallas_call | solution.py:559
  204.3 72.1 %shard_map.211 = (bf16[2048,2048]{1,0:T(8,128)(2,1)}, f32[2048,2048]{1,0:T(8,128)}, bf16[2048,2048]{1,0:T(8,128)(2,1)}, f32[2048,128]{1,0:T(8,128)}, f32[128,204...) custom-call(f32[2048,2048]{1,0:T(8,128)} %get-tuple-element.88.yss, f32[2048,2048]{1,0:T(8,128)} %get-tuple-element.82.x, ...), custom_call_target="tpu_custom_call" | custom-call | tf_op jit(solution)/shard_map/pallas_call | solution.py:574
  276.4 14.6 %convolution_bitcast_fusion = f32[1024,2048]{0,1:T(8,128)} fusion(bf16[2048,2048]{1,0:T(8,128)(2,1)} %get-tuple-element.93, bf16[2048,1024]{1,0:T(8,128)(2,1)} %og.1), kind=kOutput, calls=%fused_computation.16 | convolution fusion | flops 8589934592 | bytes 20971520 | tf_op jit(solution)/shard_map/tk,ti->ki/dot_general | solution.py:602
  291.0 9.3 %copy.78 = f32[1024,2048]{1,0:T(8,128)} copy(f32[1024,2048]{0,1:T(8,128)} %convolution_bitcast_fusion) | data formatting | bytes 16777216
  300.4 1.7 reshape.219
  302.5 67.3 %all_to_all.21.pieces = f32[32,5,2048]{2,1,0:T(8,128)} all-to-all(f32[32,5,2048]{2,1,0:T(8,128)S(1)} %pad_maximum_fusion.3), channel_id=1, replica_groups=mesh['seq'=32] {'seq'}, dimensions={0} | all-to-all | bytes 2621440 | tf_op jit(solution)/shard_map/all_to_all | solution.py:449
  369.8 3.0 shard_map.212
  372.8 5.8 all-to-all-start.3
  382.4 28.3 %all-to-all-done.3 = f32[32,4,2048]{2,1,0:T(4,128)S(1)} async-done(((f32[32,4,2048]{2,1,0:T(4,128)}), f32[32,4,2048]{2,1,0:T(4,128)S(1)}, u32[]{:S(2)}, u32[]{:S(2)}) %all-to-all-start.3) | async-done | bytes 1048608 | tf_op jit(solution)/shard_map/all_to_all | solution.py:455
  412.1 174.5 %shard_map.213 = (bf16[2048,2304]{1,0:T(8,128)(2,1)}, bf16[2048,128]{1,0:T(8,128)(2,1)}, f32[8,2304]{1,0:T(8,128)}, f32[8,2304]{1,0:T(8,128)}, f32[8,2304]{1,0:T(8,128)}, /*index=5*/f32[8,128]{1,0:T(8,128)}) custom-call(f32[2048,2048]{1,0:T(8,128)} %get-tuple-element.82.x, f32[2048,256]{1,0:T(8,128)} %get-tuple-element.83.bc, ...), custom_call_target="tpu_custom_call" | custom-call | tf_op jit(solution)/shard_map/pallas_call | solution.py:607
  594.0 28.0 %fusion.6 = f32[1024,4384]{1,0:T(8,128)} fusion(bf16[2048,1024]{1,0:T(8,128)(2,1)} %get-tuple-element.87.nl, bf16[2048,32]{1,0:T(8,128)(2,1)} %bitcast.62, bf16[2048,2304]{1,0:T(8,128)(2,1)} %fusion.14, bf16[2048,2048]{1,0:T(8,128)(2,1)} %get-tuple-element.94), kind=kOutput, calls=%fused_computation.12 | convolution fusion | flops 18441699328 | bytes 40108032 | tf_op jit(solution)/shard_map/tk,te->ke/dot_general | solution.py:656
  622.1 3.1 fusion.1
  627.2 14.6 %fusion = bf16[2048,1024]{1,0:T(8,128)(2,1)} fusion(bf16[2048,1024]{1,0:T(8,128)(2,1)} %hid.1, bf16[2048,2048]{1,0:T(8,128)(2,1)} %get-tuple-element.93, bf16[2048,1024]{1,0:T(8,128)(2,1)} %w_out.1), kind=kOutput, calls=%fused_computation.6 | convolution fusion | flops 8596226048 | bytes 20971520 | tf_op jit(solution)/shard_map/dot_general | solution.py:601
  642.7 25.4 %fusion.5 = (f32[1024]{0:T(1024)S(1)}, f32[2048]{0:T(1024)S(1)}, f32[2048,1024]{1,0:T(8,128)}) fusion(bf16[2048,1024]{1,0:T(8,128)(2,1)S(1)} %copy-done, f32[2048]{0:T(1024)S(1)} %add_rsqrt_fusion, f32[1024]{0:T(1024)S(1)} %copy-done.5, bf16[1024,4384]{0,1:T(8,128)(2,1)S(1)} %bitcast.42, bf16[2048,32]{1,0:T(8,128)(2,1)S(1)} %bitcast.63, ...), kind=kOutput, calls=%fused_computation.11 | convolution fusion | flops 18456377344 | bytes 39542784 | tf_op jit(solution)/shard_map/te,de->td/dot_general | solution.py:655
  668.1 48.2 %all-reduce.1 = (f32[1024]{0:T(1024)}, f32[4,2304]{1,0:T(4,128)}, f32[2304]{0:T(1024)}, f32[32]{0:T(128)}, f32[32]{0:T(128)}, /*index=5*/f32[32]{0:T(128)}, f32[2048]{0:T(1024)}) all-reduce(f32[1024]{0:T(1024)S(1)} %get-tuple-element.164, f32[4,2304]{1,0:T(4,128)S(1)} %maximum_add_fusion, ...), channel_id=1, replica_groups=mesh['seq'=32] {'seq'}, use_global_device_ids=true, to_apply=%region_6.7 | all-reduce | flops 14688 | bytes 117504 | tf_op jit(solution)/shard_map/psum | solution.py:667
  716.3 10.1 %fusion.3 = f32[2048,1024]{1,0:T(8,128)} fusion(bf16[2048,1024]{1,0:T(8,128)(2,1)} %hid.1, bf16[2048,1024]{1,0:T(8,128)(2,1)} %og.1, f32[2048,1024]{1,0:T(8,128)} %get-tuple-element.194, f32[2048]{0:T(1024)S(1)} %fusion.27, f32[1024]{0:T(1024)S(1)} %copy-done.5, f32[2048]{0:T(1024)S(1)} %add_rsqrt_fusion), kind=kLoop, calls=%fused_computation.9 | loop fusion | flops 14680064 | bytes 25186304 | tf_op jit(solution)/shard_map/sub | solution.py:663
  726.4 101.5 %reduce-scatter.5.cloned.1.call-done = f32[32,4384]{1,0:T(8,128)} async-done(((f32[1024,4384]{1,0:T(8,128)}), f32[32,4384]{1,0:T(8,128)}) %reduce-scatter.5.cloned.1.call-update) | async-done | bytes 561168 | tf_op jit(solution)/shard_map/reduce_scatter | solution.py:657
  (101 shorter events, 28.6 us)
Async XLA Ops:
  11.7 20.9 %collective-permute-start = (bf16[8,2304]{1,0:T(8,128)(2,1)S(1)}, bf16[8,2304]{1,0:T(8,128)(2,1)S(1)}, u32[]{:S(2)}, u32[]{:S(2)}) collective-permute-start(bf16[8,2304]{1,0:T(8,128)(2,1)S(1)} %fusion.10), channel_id=1, source_target_pairs={{0,1},{1,2},{2,3},{3,4},{4,5},{5,6},{6,7},{7,8},{8,9},{9,10},{10,1... | collective-permute-start | bytes 110600 | tf_op jit(solution)/shard_map/ppermute | solution.py:461
  15.0 13.4 %copy-start.4 = (f32[2048]{0:T(1024)}, f32[2048]{0:T(1024)S(1)}, u32[]{:S(2)}) copy-start(f32[2048]{0:T(1024)S(1)} %get-tuple-element.191) | copy-start | bytes 24580
  16.3 13.7 %copy-start.8 = (f32[32]{0:T(128)S(1)}, f32[32]{0:T(128)}, u32[]{:S(2)}) copy-start(f32[32]{0:T(128)} %param.27) | copy-start | bytes 388
  16.3 14.2 %slice-start.3 = ((bf16[1024,4384]{0,1:T(8,128)(2,1)}), bf16[1024,32]{0,1:T(8,128)(2,1)S(1)}, s32[]{:S(2)}) async-start(bf16[1024,4384]{0,1:T(8,128)(2,1)} %param.23), calls=%async_computation.11 | async-start | bytes 131072 | tf_op jit(solution)/shard_map/slice | solution.py:511
  16.3 15.1 %copy-start.7 = (f32[2304]{0:T(1024)S(1)}, f32[2304]{0:T(1024)}, u32[]{:S(2)}) copy-start(f32[2304]{0:T(1024)} %param.25) | copy-start | bytes 27652
  16.3 15.7 %copy-start.9 = (f32[32]{0:T(128)S(1)}, f32[32]{0:T(128)}, u32[]{:S(2)}) copy-start(f32[32]{0:T(128)} %param.26) | copy-start | bytes 388
  77.9 65.4 %copy-start.10 = (f32[32]{0:T(128)S(1)}, f32[32]{0:T(128)}, u32[]{:S(2)}) copy-start(f32[32]{0:T(128)} %param.28) | copy-start | bytes 388
  139.6 63.3 %all-to-all-start.1 = ((f32[32,4,2048]{2,1,0:T(4,128)}), f32[32,4,2048]{2,1,0:T(4,128)S(1)}, u32[]{:S(2)}, u32[]{:S(2)}) async-start(f32[32,4,2048]{2,1,0:T(4,128)} %shard_map.210), calls=%async_computation.1 | async-start | bytes 2097152 | tf_op jit(solution)/shard_map/all_to_all | solution.py:455
  143.3 583.1 %reduce-scatter.7.cloned.1.call-start = ((), (), s32[]{:S(2)}) async-start(), calls=%async_computation.7 | async-start | bytes 8650752
  300.4 80.7 %copy-start.3 = (f32[4,2304]{1,0:T(4,128)S(1)}, f32[4,2304]{1,0:T(4,128)}, u32[]{:S(2)}) copy-start(f32[4,2304]{1,0:T(4,128)} %cw.3) | copy-start | bytes 110596
  300.4 80.9 %copy-start.1 = (f32[128,2048]{1,0:T(8,128)S(1)}, f32[128,2048]{1,0:T(8,128)}, u32[]{:S(2)}) copy-start(f32[128,2048]{1,0:T(8,128)} %reshape.217.s_in) | copy-start | bytes 3145732
  300.4 80.9 %copy-start.2 = (f32[128,2048]{1,0:T(8,128)S(1)}, f32[128,2048]{1,0:T(8,128)}, u32[]{:S(2)}) copy-start(f32[128,2048]{1,0:T(8,128)} %get-tuple-element.90) | copy-start | bytes 3145732
  372.8 37.9 %all-to-all-start.3 = ((f32[32,4,2048]{2,1,0:T(4,128)}), f32[32,4,2048]{2,1,0:T(4,128)S(1)}, u32[]{:S(2)}, u32[]{:S(2)}) async-start(f32[32,4,2048]{2,1,0:T(4,128)} %shard_map.212), calls=%async_computation.3 | async-start | bytes 2097152 | tf_op jit(solution)/shard_map/all_to_all | solution.py:455
  378.6 449.3 %reduce-scatter.5.cloned.1.call-start = ((), (), s32[]{:S(2)}) async-start(), calls=%async_computation.6 | async-start | bytes 18923520 | tf_op jit(solution)/shard_map/reduce_scatter | solution.py:657
  586.5 3.4 collective-permute-start.1
  622.0 20.7 %slice-start = ((s8[8978432]{0:T(1024)(128)(4,1)}), s8[589824]{0:T(1024)(128)(4,1)S(1)}, s32[]{:S(2)}) async-start(s8[8978432]{0:T(1024)(128)(4,1)} %bitcast.41), calls=%async_computation.8 | async-start | bytes 1179648
  627.1 14.6 %copy-start.6 = (f32[8,2304]{1,0:T(8,128)S(1)}, f32[8,2304]{1,0:T(8,128)}, u32[]{:S(2)}) copy-start(f32[8,2304]{1,0:T(8,128)} %get-tuple-element.105) | copy-start | bytes 221188
  627.1 15.5 %copy-start = (bf16[2048,1024]{1,0:T(8,128)(2,1)S(1)}, bf16[2048,1024]{1,0:T(8,128)(2,1)}, u32[]{:S(2)}) copy-start(bf16[2048,1024]{1,0:T(8,128)(2,1)} %hid.1) | copy-start | bytes 12582916
  627.1 15.5 %slice-start.1 = ((s8[8978432]{0:T(1024)(128)(4,1)}), s8[4194304]{0:T(1024)(128)(4,1)S(1)}, s32[]{:S(2)}) async-start(s8[8978432]{0:T(1024)(128)(4,1)} %bitcast.41), calls=%async_computation.9 | async-start | bytes 8388608
  627.1 15.5 %slice-start.2 = ((s8[8978432]{0:T(1024)(128)(4,1)}), s8[4194304]{0:T(1024)(128)(4,1)S(1)}, s32[]{:S(2)}) async-start(s8[8978432]{0:T(1024)(128)(4,1)} %bitcast.41), calls=%async_computation.10 | async-start | bytes 8388608
  627.1 15.5 %copy-start.5 = (f32[1024]{0:T(1024)S(1)}, f32[1024]{0:T(1024)}, u32[]{:S(2)}) copy-start(f32[1024]{0:T(1024)} %param.22) | copy-start | bytes 12292
  627.2 15.5 %copy-start.11 = (bf16[2048,128]{1,0:T(8,128)(2,1)S(1)}, bf16[2048,128]{1,0:T(8,128)(2,1)}, u32[]{:S(2)}) copy-start(bf16[2048,128]{1,0:T(8,128)(2,1)} %get-tuple-element.104) | copy-start | bytes 1572868
Sparse Core Ops, SparseCore 0:
  300.5 165.7 reduce-scatter.6
  622.1 205.7 reduce-scatter.4

commit v2 on v1

v2 whole, which is shorter than its diff:
```python
import functools

import jax
import jax.numpy as jnp
import numpy as np
from jax import lax
from jax.experimental import pallas as pl
from jax.experimental.pallas import tpu as pltpu
from jax.sharding import PartitionSpec as P

Q = 128
LANES = 128
EPS = 1e-05
LOG2E = 1.4426950408889634
f32 = jnp.float32
bf16 = jnp.bfloat16
VMEM_BYTES = 60 << 20
SUB = 2
WIDE = 256


def mm(a, b):
    return lax.dot_general(a, b, (((1,), (0,)), ((), ())), preferred_element_type=f32)


def mm_nt(a, b):
    return lax.dot_general(a, b, (((1,), (1,)), ((), ())), preferred_element_type=f32)


def mm_tn(a, b):
    return lax.dot_general(a, b, (((0,), (0,)), ((), ())), preferred_element_type=f32)


def split2(v):
    hi = v.astype(bf16)
    return hi, (v - hi.astype(f32)).astype(bf16)


def sigmoid(v):
    return jax.nn.sigmoid(v)


def lane_iota(rows):
    return lax.broadcasted_iota(jnp.int32, (rows, LANES), 1)


def spread(v, heads):
    hi = v.astype(bf16).astype(f32)
    rest = v - hi
    mid = rest.astype(bf16).astype(f32)
    low = rest - mid
    lane = lane_iota(v.shape[0])
    kept = jnp.where(lane < heads, hi, jnp.where(lane < 2 * heads, mid, low))
    return jnp.where(lane < 3 * heads, kept, 0.0).astype(bf16)


def exact3(v):
    hi = v.astype(bf16)
    rest = v - hi.astype(f32)
    mid = rest.astype(bf16)
    return hi, mid, (rest - mid.astype(f32)).astype(bf16)


def mask_mm(mask, v):
    hi, mid, low = exact3(v)
    return mm(mask, hi) + mm(mask, mid) + mm(mask, low)


def prod3(a_hi, a_lo, b_hi, b_lo):
    left = jnp.concatenate([a_hi, a_lo], axis=1)
    return mm(left, jnp.concatenate([b_hi, b_hi], axis=0)) + mm(a_hi, b_lo)


def head_sums(v, red):
    hi, lo = split2(v)
    return mm(hi, red) + mm(lo, red)


def tri_masks(begin_col, begin_row):
    row = lax.broadcasted_iota(jnp.int32, (Q, Q), 0)
    col = lax.broadcasted_iota(jnp.int32, (Q, Q), 1)
    same = jnp.broadcast_to(begin_col, (Q, Q)) == jnp.broadcast_to(begin_row, (Q, Q))
    return same & (row >= col), same & (row <= col)


def project_kernel(
    heads, inner, state,
    hid, rim, gain, w_x, w_bc, w_dt, cw, cb, dtb, alog, meta, expm,
    nl_o, xbc_o, x_o, bc_o, dsil_o, step_o, sig_o, la_o, cum_o, decay_o, sloc_o, dst_o,
    ext, srun, cum, msk,
):
    rows = hid.shape[0]
    channels = inner + 2 * state
    step_id = pl.program_id(0)

    @pl.when(step_id == 0)
    def _():
        ext[0:8, :] = rim[...]
        srun[...] = jnp.zeros_like(srun)
        cum[...] = jnp.zeros_like(cum)

    hv = hid[...].astype(f32)
    mean = jnp.mean(hv * hv, axis=1, keepdims=True)
    nl = (hv * lax.rsqrt(mean + EPS) * gain[...]).astype(bf16)
    nl_o[...] = nl

    v = mm(nl, w_dt[...]) + dtb[...]
    step = jnp.maximum(v, 0.0) + jnp.log1p(jnp.exp(-jnp.abs(v)))
    step_o[...] = step
    sig_o[...] = 1.0 / (1.0 + jnp.exp(-v))
    rate = -step * (jnp.exp(alog[...]) * LOG2E)

    for j in range(3):
        msk[j] = jnp.broadcast_to(meta[:, 1 + j : 2 + j], (rows, LANES))
    m1, m2, m3 = (jnp.concatenate([msk[j]] * (WIDE // LANES), axis=1) for j in range(3))
    for g in range(channels // WIDE):
        cols = slice(g * WIDE, (g + 1) * WIDE)
        weights = w_x[cols, :] if g * WIDE < inner else w_bc[...]
        low = mm_nt(nl, weights).astype(bf16)
        xbc_o[:, cols] = low
        ext[8 : 8 + rows, cols] = low.astype(f32)
        conv = cb[:, cols] + cw[3:4, cols] * ext[8 : 8 + rows, cols]
        conv = conv + cw[2:3, cols] * (ext[7 : 7 + rows, cols] * m1)
        conv = conv + cw[1:2, cols] * (ext[6 : 6 + rows, cols] * m2)
        conv = conv + cw[0:1, cols] * (ext[5 : 5 + rows, cols] * m3)
        gate = sigmoid(conv)
        act = conv * gate
        dsil_o[:, cols] = gate + act * (1.0 - gate)
        if g * WIDE < inner:
            x_o[:, cols] = act
        else:
            bc_o[...] = act
    ext[0:8, :] = ext[rows : rows + 8, :]

    row = lax.broadcasted_iota(jnp.int32, (Q, Q), 0)
    col = lax.broadcasted_iota(jnp.int32, (Q, Q), 1)
    tri = (row >= col).astype(bf16)
    for c in range(rows // Q):
        rs = slice(c * Q, (c + 1) * Q)
        la = mask_mm(tri, rate[rs])
        la_o[rs, :] = la
        enter = jnp.exp2(cum[...]) * meta[c * Q : c * Q + 1, 9:10]
        cum_o[c * 8 : (c + 1) * 8, :] = cum[...]
        last = la[Q - 1 : Q, :]
        cum[...] = cum[...] + last
        weight = jnp.exp2(last - la) * meta[rs, 7:8] * step[rs]
        decay = jnp.exp2(last) * meta[c * Q + Q - 1 : c * Q + Q, 8:9]
        sub = lax.broadcasted_iota(jnp.int32, (8, LANES), 0)
        both = jnp.where(sub == 0, jnp.broadcast_to(decay, (8, LANES)), enter)
        factors = jnp.concatenate([spread(weight, heads), spread(both, heads), jnp.zeros((8, LANES), bf16)], axis=0)
        b_t = bc_o[rs, :state].T
        bt_hi, bt_lo = split2(b_t)
        for g in range(inner // WIDE):
            cols = slice(g * WIDE, (g + 1) * WIDE)
            wide = mm(factors, expm[:, cols])
            decay_o[c * 8 : (c + 1) * 8, cols] = wide[Q : Q + 8]
            hi, lo = split2(x_o[rs, cols] * wide[:Q])
            new = prod3(bt_hi, bt_lo, hi, lo)
            old = srun[:, cols]
            sloc_o[c, :, cols] = old
            srun[:, cols] = old * wide[Q : Q + 1] + new
        if c == rows // Q - 1:
            @pl.when(step_id == pl.num_programs(0) - 1)
            def _():
                live = meta[c * Q + Q - 1 : c * Q + Q, 9:10]
                total = jnp.exp2(cum[...]) * live
                dst_o[:, :inner] = srun[...]
                dst_o[:, inner:] = jnp.broadcast_to(total[0:1], (state, LANES))


def over_heads(v, first, count, half):
    shape = (v.shape[0], LANES)
    column = lambda h: jnp.broadcast_to(v[:, h : h + 1], shape)
    pairs = [jnp.where(half, column(h), column(h + 1)) for h in range(first, first + count, 2)]
    return jnp.concatenate(pairs, axis=1)


def scan_kernel(heads, inner, state, x_r, bc_r, step_r, la_rows, meta_r, brow, sloc, expm, y_o):
    left_half = lane_iota(Q) < inner // heads
    for c in range(SUB):
        rs = slice(c * Q, (c + 1) * Q)
        la = la_rows[rs, :]
        la_t = la.T
        meta, step = meta_r[rs, :], step_r[rs, :]
        mask, _ = tri_masks(meta[:, 0:1], brow[c])
        b_hi, b_lo = split2(bc_r[rs, :state])
        c_hi, c_lo = split2(bc_r[rs, state:])
        c_cat = jnp.concatenate([c_hi, c_lo], axis=1)
        scores = mm_nt(c_cat, jnp.concatenate([b_hi, b_hi], axis=1)) + mm_nt(c_hi, b_lo)
        scores = jnp.where(mask, scores, 0.0)
        carry_s = spread(jnp.exp2(la) * meta[:, 8:9], heads)
        for k in range(inner // WIDE):
            wide_cols = slice(k * WIDE, (k + 1) * WIDE)
            first = k * WIDE * heads // inner
            s_hi, s_lo = split2(sloc[c, :, wide_cols])
            carried = mm(carry_s, expm[:, wide_cols]) * (
                mm(c_cat, jnp.concatenate([s_hi, s_hi], axis=0)) + mm(c_hi, s_lo)
            )
            step_x = over_heads(step, first, WIDE * heads // inner, left_half)
            all_hi, all_lo = split2(x_r[rs, wide_cols] * step_x)
            for p in range(WIDE // LANES):
                own = slice(p * LANES, (p + 1) * LANES)
                cols = slice(k * WIDE + p * LANES, k * WIDE + (p + 1) * LANES)
                u_cat = jnp.concatenate([all_hi[:, own], all_lo[:, own]], axis=1)
                right = jnp.concatenate([u_cat, u_cat], axis=0)
                lefts = []
                for e in range(2):
                    h = first + 2 * p + e
                    gap = jnp.minimum(la[:, h : h + 1] - la_t[h : h + 1, :], 0.0)
                    w_hi, w_lo = split2(scores * jnp.exp2(gap))
                    lefts.append(jnp.concatenate([w_hi, w_lo], axis=1))
                both = mm(jnp.concatenate(lefts, axis=0), right)
                both = both[:, :LANES] + both[:, LANES:]
                y_o[rs, cols] = jnp.where(left_half, both[:Q], both[Q:]) + carried[:, own]


def gate_kernel(
    heads, inner, state,
    yss, x, z, og, w_out, s_in, bc, la_r, cum, meta, dsk, gain, expm, red,
    gl_o, dy_o, gz_o, rowdot_o, sin_o, dgain_o, dskip_o,
    gsc, ysc, ssc, exs, grad, ogs,
):
    step_id = pl.program_id(0)
    rows = x.shape[0]

    @pl.when(step_id == 0)
    def _():
        sin_o[:, :inner] = jnp.zeros((state, inner), f32)
        dgain_o[...] = jnp.zeros_like(dgain_o)
        dskip_o[...] = jnp.zeros_like(dskip_o)
        ogs[...] = jnp.zeros_like(ogs)
        hi, lo = split2(s_in[...])
        ssc[0:state, :] = hi
        ssc[state : 2 * state, :] = hi
        ssc[2 * state :, :] = lo

    c_hi, c_lo = split2(bc[:, state:])
    c_cat = jnp.concatenate([c_hi, c_lo], axis=1)
    ct_hi, ct_lo = split2(bc[:, state:].T)
    before = jnp.concatenate(
        [jnp.broadcast_to(cum[8 * c : 8 * c + 1, :], (Q, LANES)) for c in range(rows // Q)], axis=0
    )
    enter_s = spread(jnp.exp2(la_r[...] + before) * meta[:, 9:10], heads)
    ogv = og[...]
    ogs[...] += eights(jnp.square(ogv.astype(f32)))
    sq = jnp.zeros((rows, LANES), f32)
    dotted = jnp.zeros((rows, LANES), f32)
    for g in range(inner // WIDE):
        cols = slice(g * WIDE, (g + 1) * WIDE)
        carried = mm(c_cat, ssc[0 : 2 * state, cols]) + mm(c_hi, ssc[2 * state :, cols])
        enter_x = mm(enter_s, expm[:, cols])
        exs[:, cols] = enter_x
        y = yss[:, cols] + carried * enter_x
        ysc[:, cols] = y
        zv = z[:, cols]
        gated = (y + dsk[:, cols] * x[:, cols]) * (zv * sigmoid(zv))
        gsc[:, cols] = gated
        s = gated * gated
        gg = mm_nt(ogv, w_out[cols, :])
        grad[:, cols] = gg
        d = gg * gain[:, cols] * gated
        for k in range(WIDE // LANES):
            sq = sq + s[:, k * LANES : (k + 1) * LANES]
            dotted = dotted + d[:, k * LANES : (k + 1) * LANES]
    mean = jnp.sum(sq, axis=1, keepdims=True) / inner
    r = lax.rsqrt(mean + EPS)
    m = jnp.sum(dotted, axis=1, keepdims=True) / inner
    coeff = r * r * r * m
    rowdot = jnp.zeros((2 * rows, LANES), f32)
    for g in range(inner // WIDE):
        cols = slice(g * WIDE, (g + 1) * WIDE)
        gated = gsc[:, cols]
        gg = grad[:, cols]
        gn = gated * r
        gl_o[:, cols] = (gn * gain[:, cols]).astype(bf16)
        dgain_o[0:1, cols] += jnp.sum(gg * gn, axis=0, keepdims=True)
        grad_gated = r * (gain[:, cols] * gg) - gated * coeff
        zv = z[:, cols]
        sg = sigmoid(zv)
        sz = zv * sg
        dy = grad_gated * sz
        dy_o[:, cols] = dy
        ys = ysc[:, cols]
        xv = x[:, cols]
        gz = grad_gated * (ys + dsk[:, cols] * xv) * (sg + sz * (1.0 - sg))
        gz_o[:, cols] = gz.astype(bf16)
        dgain_o[1:2, cols] += jnp.sum(gz * gz, axis=0, keepdims=True)
        rowdot = rowdot + mm(jnp.concatenate(split2(dy * ys), axis=0), red[cols, :])
        dskip_o[0:1, cols] += jnp.sum(dy * xv, axis=0, keepdims=True)
        hi, lo = split2(dy * exs[:, cols])
        sin_o[:, cols] += mm(ct_hi, hi) + mm(ct_lo, hi) + mm(ct_hi, lo)
    rowdot_o[...] = rowdot[:rows] + rowdot[rows:]

    @pl.when(step_id == pl.num_programs(0) - 1)
    def _():
        most = jnp.max(dgain_o[1:2, :], axis=1, keepdims=True)
        og_most = jnp.max(jnp.sum(ogs[...], axis=0, keepdims=True), axis=1, keepdims=True)
        sin_o[:, inner:] = jnp.where(lane_iota(state) < LANES // 2, most, og_most)


def back_kernel(
    heads, head_width, state, first_head, started, into, last_one,
    x, bc, step_r, la_r, decay, meta, brow, sloc, s_in, dyr, dsil, xbc,
    d_in, s_out, dsk, cw, expm, red, *rest,
):
    if started:
        acc_in, rest = rest[:2], rest[2:]
    if last_one:
        (sig, rowdot, alog), rest = rest[:3], rest[3:]
    if into:
        rest = rest[1:]
    if last_one:
        pg_o, par_o, first_o, tail_o, dcw_o, ds, cgx, tot, msk = rest
    else:
        pg_o, dcb_o, small_o, first_o, tail_o, dcw_o, ds, cgx, tot, msk = rest
    step_id = pl.program_id(0)
    width = x.shape[1]
    rows = SUB * Q

    @pl.when(step_id == 0)
    def _():
        ds[...] = d_in[...]
        cgx[0:8, :] = jnp.zeros_like(cgx[0:8, :])
        dcw_o[...] = jnp.zeros_like(dcw_o)
        if last_one:
            par_o[...] = jnp.zeros_like(par_o)
        for p in range(width // LANES):
            cols = slice(p * LANES, (p + 1) * LANES)
            tot[p : p + 1, :] = jnp.sum(d_in[:, cols] * s_out[:, cols], axis=0, keepdims=True)

    cgx[rows:, :] = cgx[0:8, :]
    pairs = width // LANES
    left_half = lane_iota(Q) < head_width
    zero = jnp.zeros((Q, LANES), bf16)
    lane8 = lane_iota(8)
    pair8 = lax.broadcasted_iota(jnp.int32, (8, LANES), 0)
    for c in reversed(range(SUB)):
        rs = slice(c * Q, (c + 1) * Q)
        part = tot[0:8, :]
        halves = [
            jnp.sum(jnp.where(side, part, 0.0), axis=1, keepdims=True)
            for side in (lane8 < head_width, lane8 >= head_width)
        ]
        ends = jnp.zeros((8, LANES), f32)
        for e in range(2):
            here = (lane8 % heads == first_head + 2 * pair8 + e) & (pair8 < pairs)
            ends = ends + jnp.where(here, halves[e], 0.0)
        ends = jnp.sum(ends, axis=0, keepdims=True)

        la = la_r[rs, :]
        la_t = la.T
        notes = meta[rs, :]
        for j in range(3):
            msk[j] = jnp.broadcast_to(notes[:, 4 + j : 5 + j], (Q, LANES))
        _, mask_t = tri_masks(notes[:, 0:1], brow[c])
        b_hi, b_lo = split2(bc[rs, :state])
        c32 = bc[rs, state:]
        c_hi, c_lo = split2(c32)
        b_cat = jnp.concatenate([b_hi, b_lo], axis=1)
        ct_hi, ct_lo = split2(c32.T)
        scores_t = mm_nt(b_cat, jnp.concatenate([c_hi, c_hi], axis=1)) + mm_nt(b_hi, c_lo)
        scores_t = jnp.where(mask_t, scores_t, 0.0)
        last = la[Q - 1 : Q, :]
        tail = notes[:, 7:8]
        step = step_r[rs, :]
        tail_v = jnp.exp2(last - la) * tail
        factors = jnp.concatenate(
            [spread(step, heads), spread(jnp.exp2(la) * notes[:, 8:9], heads)], axis=0
        )

        dg_t = jnp.zeros((Q, Q), f32)
        dc = jnp.zeros((Q, state), f32)
        db = jnp.zeros((Q, state), f32)
        xdu = jnp.zeros((Q, LANES), f32)
        for lo_col in range(0, width, WIDE):
            wd = min(WIDE, width - lo_col)
            wcols = slice(lo_col, lo_col + wd)
            first = first_head + lo_col // head_width
            wide = mm(factors, expm[:, wcols])
            step_x, carry_x = wide[:Q], wide[Q:]
            tail_x = over_heads(tail_v, first, wd // head_width, left_half)
            xv = x[rs, wcols]
            dy = dyr[rs, wcols]
            u = xv * step_x
            u_hi, u_lo = split2(u)
            dy_hi, dy_lo = split2(dy)
            d_out = ds[:, wcols]
            d_hi, d_lo = split2(d_out)
            through = tail_x * (mm(b_cat, jnp.concatenate([d_hi, d_hi], axis=0)) + mm(b_hi, d_lo))
            insides = []
            for p in range(wd // LANES):
                own = slice(p * LANES, (p + 1) * LANES)
                uh, ul, yh, yl = u_hi[:, own], u_lo[:, own], dy_hi[:, own], dy_lo[:, own]
                sides = []
                for e in range(2):
                    keep = left_half if e == 0 else ~left_half
                    sides.append(
                        jnp.concatenate([jnp.where(keep, uh, zero), jnp.where(keep, ul, zero)], axis=1)
                    )
                right = jnp.concatenate(
                    [jnp.concatenate([yh, yh], axis=1), jnp.concatenate([yl, yl], axis=1)], axis=0
                )
                dw = mm_nt(jnp.concatenate(sides, axis=0), right)
                dw = dw[:, :Q] + dw[:, Q:]
                lefts = []
                for e in range(2):
                    h = first + 2 * p + e
                    gap = jnp.minimum(la_t[h : h + 1, :] - la[:, h : h + 1], 0.0)
                    decays = jnp.exp2(gap)
                    w_hi, w_lo = split2(scores_t * decays)
                    lefts.append(jnp.concatenate([w_hi, w_lo], axis=1))
                    dg_t = dg_t + dw[e * Q : (e + 1) * Q] * decays
                y_cat = jnp.concatenate([yh, yl], axis=1)
                both = mm(jnp.concatenate(lefts, axis=0), jnp.concatenate([y_cat, y_cat], axis=0))
                both = both[:, :LANES] + both[:, LANES:]
                insides.append(jnp.where(left_half, both[:Q], both[Q:]))
            du = through + (jnp.concatenate(insides, axis=1) if len(insides) > 1 else insides[0])
            sums = mm(jnp.concatenate(split2(xv * du), axis=0), red[wcols, :])
            xdu = xdu + sums[:Q] + sums[Q:]
            cgx[rs, wcols] = (dsk[:, wcols] * dy + step_x * du) * dsil[rs, wcols]
            s_true = sloc[c, :, wcols] + decay[8 * c + 1 : 8 * c + 2, wcols] * s_in[:, wcols]
            s_hi, s_lo = split2(s_true)
            v_hi, v_lo = split2(carry_x * dy)
            t_hi, t_lo = split2(tail_x * u)
            res = mm_nt(jnp.concatenate([v_hi, v_lo], axis=0), jnp.concatenate([s_hi, s_lo], axis=0))
            dc = dc + (res[:Q, :state] + res[:Q, state:] + res[Q:, :state])
            res = mm_nt(jnp.concatenate([t_hi, t_lo], axis=0), jnp.concatenate([d_hi, d_lo], axis=0))
            db = db + (res[:Q, :state] + res[:Q, state:] + res[Q:, :state])
            d_new = d_out * decay[8 * c : 8 * c + 1, wcols] + prod3(ct_hi, ct_lo, v_hi, v_lo)
            ds[:, wcols] = d_new
            total = jnp.sum(d_new * s_true, axis=0, keepdims=True)
            for p in range(wd // LANES):
                row = lo_col // LANES + p
                tot[row : row + 1, :] = total[:, p * LANES : (p + 1) * LANES]
            conv_back(c, wcols, msk, cgx, cw, xbc, pg_o, dcw_o, tail_o)

        parts = [dg_t, dc, db, xdu]
        if started:
            parts = [v + acc_in[0][rs, i * LANES : (i + 1) * LANES] for i, v in enumerate(parts)]
            ends = ends + acc_in[1][8 * c : 8 * c + 1, :]
        if not last_one:
            for i, value in enumerate(parts):
                dcb_o[rs, i * LANES : (i + 1) * LANES] = value
            small_o[8 * c : 8 * c + 8, :] = jnp.broadcast_to(ends, (8, LANES))
            continue
        dg_t, dc, db, xdu = parts
        g_hi, g_lo = split2(jnp.where(mask_t, dg_t, 0.0))
        dc = dc + mm_tn(g_hi, b_hi) + mm_tn(g_lo, b_hi) + mm_tn(g_hi, b_lo)
        db = db + mm(g_hi, c_hi) + mm(g_lo, c_hi) + mm(g_hi, c_lo)
        cgx[rs, width : width + state] = db * dsil[rs, width : width + state]
        cgx[rs, width + state :] = dc * dsil[rs, width + state :]
        flow = rowdot[rs, :] - step * xdu
        g = mask_mm(mask_t.astype(bf16), flow) + tail * ends
        g = g * notes[:, 10:11]
        rate = jnp.exp(alog[...])
        dt = (xdu - g * rate) * sig[rs, :]
        used = cgx.shape[1]
        pg_o[rs, used : used + LANES] = jnp.where(lane_iota(Q) < heads, dt, 0.0).astype(bf16)
        pg_o[rs, used + LANES :] = jnp.zeros((Q, pg_o.shape[1] - used - LANES), bf16)
        par_o[0:1, :] += jnp.sum(-g * step * rate, axis=0, keepdims=True)
        par_o[1:2, :] += jnp.sum(dt, axis=0, keepdims=True)
        par_o[2:3, :] += jnp.sum(dt * dt, axis=0, keepdims=True)
        conv_back(c, slice(width, width + 2 * state), msk, cgx, cw, xbc, pg_o, dcw_o, tail_o)
    first_o[...] = cgx[0:8, :]


def eights(v):
    return jnp.sum(v.reshape(v.shape[0] // 8, 8, v.shape[1]), axis=0)


def conv_back(c, which, msk, cgx, cw, xbc, pg_o, dcw_o, tail_o):
    at = c * Q
    for start in range(which.start, which.stop, LANES):
        cols = slice(start, start + LANES)
        e0 = cgx[at : at + Q, cols]
        e1 = cgx[at + 1 : at + Q + 1, cols] * msk[0]
        e2 = cgx[at + 2 : at + Q + 2, cols] * msk[1]
        e3 = cgx[at + 3 : at + Q + 3, cols] * msk[2]
        grad = cw[3:4, cols] * e0 + cw[2:3, cols] * e1 + cw[1:2, cols] * e2 + cw[0:1, cols] * e3
        pg_o[at : at + Q, cols] = grad.astype(bf16)
        xf = xbc[at : at + Q, cols].astype(f32)
        for tap, e in ((3, e0), (2, e1), (1, e2), (0, e3)):
            dcw_o[8 * tap : 8 * tap + 8, cols] += eights(xf * e)
        dcw_o[32:40, cols] += eights(e0)
        dcw_o[40:48, cols] += eights(grad * grad)
        if c == SUB - 1:
            tail_o[:, cols] = jnp.where(pl.program_id(0) == 0, grad[Q - 8 :, :], tail_o[:, cols])


def edge_kernel(count, ok, piece, *refs):
    ins, piece_o, outs, ext = refs[: 5 * count], refs[5 * count], refs[5 * count + 1 : 6 * count + 1], refs[-1]
    near_o = refs[-2]
    near = jnp.zeros((1, 1), f32)
    piece_o[...] = piece[...]
    group = piece.shape[1] // 2
    for k in range(count):
        tail, rim, cw, xbc, dcw = ins[5 * k : 5 * k + 5]
        dcw_o = outs[k]
        width = tail.shape[1]
        ext[0:8, 0:width] = jnp.zeros((8, width), f32)
        ext[8:16, 0:width] = rim[...]
        last = xbc[...].astype(f32)[8:16]
        grad = tail[...]
        for k8 in range(6):
            dcw_o[k8 : k8 + 1, :] = jnp.sum(dcw[8 * k8 : 8 * k8 + 8, :], axis=0, keepdims=True)
        dcw_o[6:8, :] = jnp.zeros((2, width), f32)
        for j in (1, 2, 3):
            e = ext[j : j + 8, 0:width] * ok[:, j : j + 1]
            grad = grad + cw[3 - j : 4 - j, :] * e
            dcw_o[3 - j : 4 - j, :] += jnp.sum(last * e, axis=0, keepdims=True)
        dcw_o[5:6, :] += jnp.sum(grad * grad, axis=0, keepdims=True)
        near = jnp.maximum(near, jnp.max(dcw_o[5:6, :], axis=1, keepdims=True))
        cols = slice(k * group, k * group + width)
        old = piece[:, cols].astype(f32)
        piece_o[:, cols] = jnp.concatenate([old[0:8], grad], axis=0).astype(bf16)
    near_o[...] = jnp.broadcast_to(near, (8, LANES))


def chain_kernel(backward, pieces, decays, out):
    count, _, width = out.shape

    def turn(i, run):
        k = count - 1 - i if backward else i
        out[k] = run
        return run * decays[k] + pieces[k, :, :width]

    lax.fori_loop(0, count, turn, jnp.zeros(out.shape[1:], f32))


def cost(us):
    return pl.CostEstimate(flops=int(us * 1e9), bytes_accessed=1 << 20, transcendentals=0)


def params(**more):
    return pltpu.CompilerParams(vmem_limit_bytes=VMEM_BYTES, **more)


def to_all(local, lanes):
    count = lax.axis_size("seq")
    rows = local.shape[0]
    if count <= rows:
        got = lax.all_to_all(local.reshape(count, rows // count, lanes + LANES), "seq", 0, 0, tiled=True)
        return got, got[:, 0, lanes:]
    split = count // rows
    got = lax.all_to_all(local[:, :lanes].reshape(count, 1, lanes // split), "seq", 0, 0, tiled=True)
    notes = jnp.broadcast_to(local[0:8, lanes:][None], (count, 8, LANES))
    return got, lax.all_to_all(notes, "seq", 0, 0, tiled=True)[:, 0]


def chain(got, decays, lanes, backward):
    count, per, width = got.shape
    if width > lanes:
        width = lanes
    own = decays[:, None, :]
    if width < lanes:
        split = lanes // width
        own = lax.dynamic_slice_in_dim(own, lax.axis_index("seq") % split * width, width, axis=2)
    out = pl.pallas_call(
        functools.partial(chain_kernel, backward),
        out_shape=jax.ShapeDtypeStruct((count, per, width), f32),
        compiler_params=params(),
    )(got, own)
    return lax.all_to_all(out, "seq", 0, 0, tiled=True).reshape(-1, lanes)


def swap(value, k):
    return lax.ppermute(value, "seq", [(i, i ^ k) for i in range(lax.axis_size("seq"))])


def trade(value):
    return lax.all_to_all(value, "seq", 0, 0, tiled=True)


def sum_all(flat):
    count = lax.axis_size("seq")
    rows = -(-flat.shape[0] // (count * LANES))
    pieces = jnp.pad(flat, (0, count * rows * LANES - flat.shape[0])).reshape(count, rows, LANES)
    mine = jnp.sum(trade(pieces), axis=0)
    return trade(jnp.broadcast_to(mine[None], pieces.shape)).reshape(-1)[: flat.shape[0]]


def sum_all_once(flat):
    count = lax.axis_size("seq")
    wide = flat.reshape(-1, LANES)
    return jnp.sum(trade(jnp.broadcast_to(wide[None], (count,) + wide.shape)), axis=0).reshape(-1)


HALF = jnp.float16
TOP = 32768.0


def tie(*values):
    return lax.optimization_barrier(values)


def chip_scatter(product, cols_mine, cols_other, near, bound, first_bits):
    scale = TOP / jnp.maximum(bound, 1e-30)
    count = lax.axis_size("seq")
    chips = count // 2
    chip = lax.axis_index("seq") // 2
    near = jnp.broadcast_to(jnp.maximum(near, 1e-30), (8, LANES))
    away = swap((product(cols_other) * (TOP / near[0, 0])).astype(HALF), 1).astype(f32)
    acc = (product(cols_mine) + away * (swap(near, 1)[0, 0] * (1.0 / TOP))) * scale
    rows, width = acc.shape
    bits = chips.bit_length() - 1
    acc = acc.reshape((2,) * bits + (rows // chips, width))
    left = list(range(bits))[::-1]
    order = [b for b in first_bits if b < bits]
    order = order + [b for b in range(bits) if b not in order]
    for b in order:
        axis = left.index(b)
        left.remove(b)
        mine = (chip >> b) & 1
        away = lax.dynamic_index_in_dim(acc, 1 - mine, axis, keepdims=False).astype(HALF)
        acc = lax.dynamic_index_in_dim(acc, mine, axis, keepdims=False)
        away, acc = yield away, acc
        arrived = yield swap(away, 2 << b)
        acc = acc + arrived.astype(f32)
    return acc * (1.0 / scale)


class Flow:
    def __init__(self, steps):
        self.steps, self.result = steps, None
        self.value = next(steps)

    def push(self, value):
        try:
            self.value = self.steps.send(value)
        except StopIteration as end:
            self.result = end.value

    def finish(self):
        while self.result is None:
            self.push(self.value)
        return self.result


def beside(flows, operand, kernel):
    flows = [f for f in flows if f.result is None]
    pairs = [f.value for f in flows]
    flat = tie(operand, *[v for p in pairs for v in p])
    for k, f in enumerate(flows):
        f.push((flat[1 + 2 * k], flat[2 + 2 * k]))
    results = kernel(flat[0])
    flat = tie(results[0], *[f.value for f in flows])
    for k, f in enumerate(flows):
        f.push(flat[1 + k])
    return (flat[0],) + tuple(results[1:])


def both_cores(part):
    core = lax.axis_index("seq") % 2
    rows = part.shape[0] // 2
    mine = lax.dynamic_slice_in_dim(part, core * rows, rows, 0)
    other = swap(lax.dynamic_slice_in_dim(part, (1 - core) * rows, rows, 0), 1)
    return jnp.where(core == 0, mine, other), jnp.where(core == 0, other, mine)


def from_behind(value, steps):
    count = lax.axis_size("seq")
    first, last = max(0, -steps), min(count, count - steps)
    return lax.ppermute(value, "seq", [(s, s + steps) for s in range(first, last)])


def body(
    hidden, scene_lengths, norm_gain, w_in, conv_weight, conv_bias, dt_bias, a_log, d_skip,
    gate_gain, w_out, out_grad,
):
    tokens, model = hidden.shape
    heads = a_log.shape[0]
    inner = gate_gain.shape[0]
    channels = conv_bias.shape[0]
    state = (channels - inner) // 2
    chunks = tokens // Q
    repeat = LANES // heads
    columns = w_in.shape[1]

    scenes = scene_lengths.shape[0]
    order = jnp.arange(scenes)
    starts = jnp.sum(jnp.where(order[None, :] < order[:, None], scene_lengths[None, :], 0), axis=1)
    dev_start = lax.axis_index("seq") * tokens
    wide_pos = dev_start + jnp.arange(tokens + 8, dtype=jnp.int32)
    begin_all = jnp.max(jnp.where(starts[None, :] <= wide_pos[:, None], starts[None, :], 0), axis=1)
    begin, pos = begin_all[:tokens], wide_pos[:tokens]
    chunk_last = jnp.repeat(begin.reshape(chunks, Q)[:, -1], Q)
    chunk_start = pos // Q * Q
    inside = jnp.arange(tokens)
    notes = [
        begin,
        pos - 1 >= begin,
        pos - 2 >= begin,
        pos - 3 >= begin,
        (begin_all[1 : tokens + 1] <= pos) & (inside + 1 < tokens),
        (begin_all[2 : tokens + 2] <= pos) & (inside + 2 < tokens),
        (begin_all[3 : tokens + 3] <= pos) & (inside + 3 < tokens),
        begin == chunk_last,
        begin < chunk_start,
        begin < dev_start,
        begin != pos,
    ]
    meta = jnp.stack([n.astype(f32) for n in notes] + [jnp.zeros((tokens,), f32)] * (16 - len(notes)), axis=1)
    brow = begin.astype(f32).reshape(chunks, 1, Q)

    head_of = np.arange(inner) // (inner // heads)
    expand = np.arange(LANES)[:, None] % heads == head_of[None, :]
    expm, red = jnp.asarray(expand, bf16), jnp.asarray(expand.T, bf16)

    def four(v):
        return jnp.tile(v, repeat).reshape(1, LANES)

    gain_row = norm_gain.reshape(1, model)
    w_t = w_in.T
    w_dt = jnp.tile(w_t[inner + channels :], (repeat, 1)).T
    dsk = jnp.repeat(d_skip, inner // heads).reshape(1, inner)
    cb = conv_bias.reshape(1, channels)
    gate_row = gate_gain.reshape(1, inner)

    edge = hidden[tokens - 8 :].astype(f32)
    edge_low = (
        edge * lax.rsqrt(jnp.mean(edge * edge, axis=1, keepdims=True) + EPS) * norm_gain
    ).astype(bf16)
    edge_xbc = jnp.dot(
        edge_low, w_in[:, inner : inner + channels], preferred_element_type=f32
    ).astype(bf16)
    rim = from_behind(edge_xbc, 1).astype(f32)

    tb = SUB * Q
    whole = lambda shape: pl.BlockSpec(shape, lambda i: (0,) * len(shape), pipeline_mode=pl.Buffered(1))
    rowsb = lambda n, width: pl.BlockSpec((n, width), lambda i: (i, 0))
    sds = jax.ShapeDtypeStruct
    (nl, xbc, x, bc, dsil, step, sig, la, cum, decay, sloc, dev_state) = pl.pallas_call(
        functools.partial(project_kernel, heads, inner, state),
        grid=(tokens // tb,),
        in_specs=[
            rowsb(tb, model), whole((8, channels)), whole((1, model)),
            pl.BlockSpec((inner, model), lambda i: (1, 0), pipeline_mode=pl.Buffered(1)),
            pl.BlockSpec((2 * state, model), lambda i: (2 * inner // (2 * state), 0), pipeline_mode=pl.Buffered(1)),
            whole((model, LANES)), whole((4, channels)), whole((1, channels)), whole((1, LANES)),
            whole((1, LANES)), rowsb(tb, 16), whole((LANES, inner)),
        ],
        out_specs=[
            rowsb(tb, model), rowsb(tb, channels), rowsb(tb, inner), rowsb(tb, 2 * state),
            rowsb(tb, channels), rowsb(tb, LANES), rowsb(tb, LANES), rowsb(tb, LANES),
            rowsb(tb // Q * 8, LANES), rowsb(tb // Q * 8, inner),
            pl.BlockSpec((tb // Q, state, inner), lambda i: (i, 0, 0)),
            pl.BlockSpec((state, inner + LANES), lambda i: (0, 0)),
        ],
        out_shape=[
            sds((tokens, model), bf16), sds((tokens, channels), bf16), sds((tokens, inner), f32),
            sds((tokens, 2 * state), f32), sds((tokens, channels), f32), sds((tokens, LANES), f32),
            sds((tokens, LANES), f32), sds((tokens, LANES), f32), sds((chunks * 8, LANES), f32),
            sds((chunks * 8, inner), f32),
            sds((chunks, state, inner), f32), sds((state, inner + LANES), f32),
        ],
        scratch_shapes=[
            pltpu.VMEM((tb + 8, channels), f32), pltpu.VMEM((state, inner), f32), pltpu.VMEM((8, LANES), f32),
            pltpu.VMEM((3, tb, LANES), f32),
        ],
        compiler_params=params(),
        cost_estimate=cost(44),
    )(hidden, rim, gain_row, w_t, w_t, w_dt, conv_weight, cb, four(dt_bias), four(a_log), meta, expm)

    to_lanes = lambda d: jnp.repeat(d[..., :heads], inner // heads, axis=-1)
    got, notes = to_all(dev_state, inner)
    decays = to_lanes(notes)
    state_in = chain(got, decays, inner, False)

    z = jnp.dot(nl, w_in[:, :inner], preferred_element_type=f32)
    yss = pl.pallas_call(
        functools.partial(scan_kernel, heads, inner, state),
        grid=(chunks // SUB,),
        in_specs=[
            rowsb(tb, inner), rowsb(tb, 2 * state), rowsb(tb, LANES), rowsb(tb, LANES), rowsb(tb, 16),
            pl.BlockSpec((SUB, 1, Q), lambda i: (i, 0, 0)),
            pl.BlockSpec((SUB, state, inner), lambda i: (i, 0, 0)), whole((LANES, inner)),
        ],
        out_specs=rowsb(tb, inner),
        out_shape=sds((tokens, inner), f32),
        compiler_params=params(),
        cost_estimate=cost(41),
    )(x, bc, step, la, meta, brow, sloc, expm)

    gate_low, dy, gz, rowdot, state_in_grad, dgain, dskip = pl.pallas_call(
        functools.partial(gate_kernel, heads, inner, state),
        grid=(tokens // tb,),
        in_specs=[
            rowsb(tb, inner), rowsb(tb, inner), rowsb(tb, inner), rowsb(tb, model), whole((inner, model)),
            whole((state, inner)), rowsb(tb, 2 * state), rowsb(tb, LANES), rowsb(8 * SUB, LANES), rowsb(tb, 16),
            whole((1, inner)), whole((1, inner)), whole((LANES, inner)), whole((inner, LANES)),
        ],
        out_specs=[
            rowsb(tb, inner), rowsb(tb, inner), rowsb(tb, inner), rowsb(tb, LANES),
            pl.BlockSpec((state, inner + LANES), lambda i: (0, 0)), pl.BlockSpec((8, inner), lambda i: (0, 0)),
            pl.BlockSpec((8, inner), lambda i: (0, 0)),
        ],
        out_shape=[
            sds((tokens, inner), bf16), sds((tokens, inner), f32), sds((tokens, inner), bf16),
            sds((tokens, LANES), f32), sds((state, inner + LANES), f32), sds((8, inner), f32), sds((8, inner), f32),
        ],
        scratch_shapes=[
            pltpu.VMEM((tb, inner), f32), pltpu.VMEM((tb, inner), f32), pltpu.VMEM((3 * state, inner), bf16),
            pltpu.VMEM((tb, inner), f32), pltpu.VMEM((tb, inner), f32), pltpu.VMEM((8, model), f32),
        ],
        compiler_params=params(),
        cost_estimate=cost(50),
    )(yss, x, z, out_grad, w_out, state_in, bc, la, cum, meta, dsk, gate_row, expm, red)

    got, bounds = to_all(state_in_grad, inner)
    mixed_out = (hidden.astype(f32) + jnp.dot(gate_low, w_out, preferred_element_type=f32)).astype(bf16)
    normed_grad = jnp.einsum("te,de->td", gz, w_in[:, :inner], preferred_element_type=f32)
    state_out_grad = chain(got, decays, inner, True)
    state_out = dev_state[:, :inner] + to_lanes(dev_state[0:1, inner:]) * state_in

    core = lax.axis_index("seq") % 2
    contract = lambda left: lambda right: lax.dot_general(
        left, right, (((0,), (0,)), ((), ())), preferred_element_type=f32
    )
    halfc = inner // 2
    at = lambda v, c: lax.dynamic_slice_in_dim(v, c * halfc, halfc, 1)
    low_most = 1.02 * jnp.sqrt(jnp.float32(inner * tokens)) * jnp.max(jnp.abs(gate_gain))
    nl_most = 1.02 * jnp.sqrt(jnp.float32(model * tokens)) * jnp.max(jnp.abs(norm_gain))
    gz_bounds = jnp.sqrt(bounds[:, 0]) * nl_most
    og_bounds = jnp.sqrt(bounds[:, LANES - 1]) * low_most
    me = lax.axis_index("seq")
    flows = [
        Flow(chip_scatter(contract(out_grad), at(gate_low, core), at(gate_low, 1 - core), og_bounds[me], jnp.sum(og_bounds), (0, 1))),
        Flow(chip_scatter(contract(nl), at(gz, core), at(gz, 1 - core), gz_bounds[me], jnp.sum(gz_bounds), (1, 0))),
    ]

    final = chunks // SUB - 1
    width = 5 * LANES
    full = inner // width
    left_cols = inner - full * width
    conv_left = channels - full * width
    back = lambda n, cols: pl.BlockSpec((n, cols), lambda i: (final - i, 0))
    still = lambda shape: pl.BlockSpec(shape, lambda i: (0,) * len(shape))
    brow_spec = pl.BlockSpec((SUB, 1, Q), lambda i: (final - i, 0, 0))
    acc_specs = [back(tb, 4 * LANES), back(8 * SUB, LANES)]
    acc_shapes = [sds((tokens, 4 * LANES), f32), sds((chunks * 8, LANES), f32)]

    def back_group(g, dsk, acc, into):
        last_one = g == full
        w, wc = (left_cols, conv_left) if last_one else (width, width)
        b, bcv = (full * width // w, full * width // wc)if last_one else (g, g)
        chunk_cols = lambda n: pl.BlockSpec((n, w), lambda i: (final - i, b))
        conv_cols = lambda n: pl.BlockSpec((n, wc), lambda i: (final - i, bcv))
        fixed = lambda n, cols, block: pl.BlockSpec((n, cols), lambda i: (0, block), pipeline_mode=pl.Buffered(1))
        ins = [
            x, bc, step, la, decay, meta, brow, sloc, state_in, dy, dsil, xbc, state_out_grad,
            state_out, dsk, conv_weight, expm, red, *acc,
        ]
        specs = [
            chunk_cols(tb), back(tb, 2 * state), back(tb, LANES), back(tb, LANES), chunk_cols(8 * SUB),
            back(tb, 16), brow_spec, pl.BlockSpec((SUB, state, w), lambda i: (final - i, 0, b)),
            fixed(state, w, b), chunk_cols(tb), conv_cols(tb), conv_cols(tb), fixed(state, w, b),
            fixed(state, w, b), fixed(1, w, b), fixed(4, wc, bcv), fixed(LANES, w, b),
            pl.BlockSpec((w, LANES), lambda i: (b, 0), pipeline_mode=pl.Buffered(1)),
        ] + (acc_specs if acc else [])
        if last_one:
            ins += [sig, rowdot, four(a_log)]
            specs += [back(tb, LANES), back(tb, LANES), still((1, LANES))]
        aliases = {}
        if into is not None:
            aliases[len(ins)] = 0
            ins.append(into)
            specs.append(pl.BlockSpec(memory_space=pl.ANY))
        pg_spec = pl.BlockSpec((tb, width), lambda i: (final - i, g % 2))
        mid_specs, mid_shapes = (
            ([still((8, LANES))], [sds((8, LANES), f32)]) if last_one else (acc_specs, acc_shapes)
        )
        return pl.pallas_call(
            functools.partial(
                back_kernel, heads, inner // heads, state, g * width // (inner // heads), bool(acc),
                into is not None, last_one,
            ),
            grid=(chunks // SUB,),
            in_specs=specs,
            out_specs=[pg_spec] + mid_specs + [still((8, wc)), still((8, wc)), still((48, wc))],
            out_shape=[sds((tokens, 2 * width), bf16)]
            + mid_shapes
            + [sds((8, wc), f32), sds((8, wc), f32), sds((48, wc), f32)],
            scratch_shapes=[
                pltpu.VMEM((state, w), f32), pltpu.VMEM((tb + 8, wc), f32), pltpu.VMEM((8, LANES), f32),
                pltpu.VMEM((3, Q, LANES), f32),
            ],
            input_output_aliases=aliases,
            compiler_params=params(),
            cost_estimate=cost(20 if last_one else 38),
        )(*ins)

    ok_notes = jnp.stack(
        [(begin_all[tokens - 8 + j : tokens + j] <= wide_pos[tokens - 8 : tokens]).astype(f32) for j in range(4)], axis=1
    )

    def fix(part, rims, tails, sums, groups):
        at_last = pl.BlockSpec((16, 2 * width), lambda i: (tokens // 16 - 1, 0))
        ins, specs = [ok_notes, part], [whole((8, 4)), at_last]
        out_specs, shapes = [at_last], [sds(part.shape, bf16)]
        for rim_grad, tail, dcw, g in zip(rims, tails, sums, groups):
            w = tail.shape[1]
            b = g * width // w
            ins += [tail, rim_grad, conv_weight, xbc, dcw]
            specs += [
                whole((8, w)), whole((8, w)), pl.BlockSpec((4, w), lambda i, b=b: (0, b)),
                pl.BlockSpec((16, w), lambda i, b=b: (tokens // 16 - 1, b)), whole((48, w)),
            ]
            out_specs.append(pl.BlockSpec((8, w), lambda i: (0, 0)))
            shapes.append(sds((8, w), f32))
        out_specs.append(pl.BlockSpec((8, LANES), lambda i: (0, 0)))
        shapes.append(sds((8, LANES), f32))
        res = pl.pallas_call(
            functools.partial(edge_kernel, len(groups)), grid=(1,), in_specs=specs, out_specs=out_specs,
            out_shape=shapes, scratch_shapes=[pltpu.VMEM((16, width), f32)], input_output_aliases={1: 0},
            compiler_params=params(),
        )(*ins)
        return res[0], list(res[1:-1]), res[-1]

    reorder2 = lambda r: (r[1], r[0]) + tuple(r[2:])
    reorder = lambda r: (r[2],) + (r[0], r[1]) + tuple(r[3:])
    restore = lambda r: (r[1], r[2], r[0]) + tuple(r[3:])
    parts, rims, tails, sums = [], [], [], []
    acc, into = (), None
    for g in range(full):
        res = beside(flows, dsk, lambda m: reorder(back_group(g, m, acc, into)))
        part, a0, a1, first_g, tail_g, dcw_g = restore(res)
        acc = (a0, a1)
        rims.append(from_behind(first_g, -1))
        tails.append(tail_g)
        sums.append(dcw_g)
        into = part if g % 2 == 0 else None
        if g % 2 == 1:
            parts.append(part)
    part_a, dcws, near_a = fix(parts[0], rims[0:2], tails[0:2], sums[0:2], (0, 1))

    def bound_of(near):
        near = jnp.sqrt(near) * nl_most
        return near[0, 0], jnp.sum(trade(jnp.broadcast_to(near, (lax.axis_size("seq"), 8, LANES)))[:, 0, 0])

    own = lambda v, c: lax.dynamic_slice_in_dim(v, c * width, width, 1)
    flow_a = Flow(
        chip_scatter(contract(nl), own(part_a, core), own(part_a, 1 - core), *bound_of(near_a), (0, 1))
    )
    flows.append(flow_a)
    res = beside(flows, dsk, lambda m: reorder2(back_group(full, m, acc, into)))
    small, part, first_g, tail_g, dcw_g = res
    rims.append(from_behind(first_g, -1))
    part_b, dcw_b, near_b = fix(part, rims[2:], tails[2:] + [tail_g], sums[2:] + [dcw_g], (2, 3))
    bound_b = bound_of(jnp.maximum(near_b, jnp.max(small[2])))
    flow_b = Flow(
        chip_scatter(contract(nl), own(part_b, core), own(part_b, 1 - core), *bound_b, (1, 0))
    )
    dcw = jnp.concatenate(dcws + dcw_b, axis=1)

    (away, kept) = flow_b.value
    part_a2, part_b2, dcw, small, out_done, z_done, a_away, a_kept, away, kept = tie(
        part_a, part_b, dcw, small, flows[0].finish(), flows[1].finish(), *flow_a.value, away, kept
    )
    flow_a.push((a_away, a_kept))
    conv_weight_part = dcw[0:4]
    flow_b.push((away, kept))
    cut = inner + 2 * width
    normed_grad = (
        normed_grad
        + jnp.dot(part_a2, w_t[inner:cut], preferred_element_type=f32)
        + jnp.dot(part_b2[:, : columns - cut], w_t[cut:], preferred_element_type=f32)
    )
    out_rows = jnp.concatenate(both_cores(out_done), axis=1)
    w_out_grad = out_rows.T
    z_rows = both_cores(z_done)
    a_rows = both_cores(flow_a.finish())
    b_rows = both_cores(flow_b.finish())
    w_in_grad = jnp.concatenate(list(z_rows) + list(a_rows) + list(b_rows), axis=1)[:, :columns]

    hv = hidden.astype(f32)
    s = lax.rsqrt(jnp.mean(hv * hv, axis=1, keepdims=True) + EPS)
    gained = normed_grad * norm_gain
    inner_mean = jnp.mean(gained * hv, axis=1, keepdims=True)
    hidden_grad = out_grad.astype(f32) + s * gained - hv * (s * s * s * inner_mean)
    norm_gain_part = jnp.sum(normed_grad * hv * s, axis=0)

    dskip_part = jnp.sum(dskip[0].reshape(heads, inner // heads), axis=1)
    early = (conv_weight_part.reshape(-1), dcw[4], small[1, :heads], small[0, :heads], dskip_part, dgain[0])
    total = sum_all(jnp.concatenate(early))
    summed, start = [], 0
    for part in early:
        summed.append(total[start : start + part.shape[0]])
        start += part.shape[0]
    norm_gain_grad = sum_all_once(norm_gain_part)
    return (
        mixed_out, hidden_grad, norm_gain_grad, w_in_grad, summed[0].reshape(conv_weight.shape), summed[1],
        summed[2], summed[3], summed[4], summed[5], w_out_grad,
    )


def solution(mesh):
    rep = P()
    return jax.shard_map(
        body,
        mesh=mesh,
        in_specs=(P("seq", None),) + (rep,) * 10 + (P("seq", None),),
        out_specs=(P("seq", None), P("seq", None), rep, P("seq", None), rep, rep, rep, rep, rep, rep, P(None, "seq")),
        check_vma=False,
    )
```

time: 843 us -> 625 us (0.74)
  blocking collectives: 171 us -> 0 us
  Pallas kernels: 355 us -> 251 us
  waiting for transfers between devices: 131 us -> 62.9 us
  starting transfers between devices: 13.2 us -> 74.9 us
  matrix products: 86.3 us -> 133 us
  other arithmetic: 24.2 us -> 41.1 us
    all_to_all x2 -> x0, blocking collectives: 123 us -> none  [exchange(): got = lax.all_to_all(parts, 'seq', 0, 0, tiled=True)]
    reduce_scatter x1 -> x0, waiting for transfers between devices: 101 us -> none  [body(): lax.psum_scatter(w_in_part, 'seq', scatter_dimension=0, tiled=True)]
    pallas_call x3 -> x8, Pallas kernels: 180 us -> 124 us  [the longest x4 115 us: back_group(): pl.pallas_call(functools.partial(back_kernel, heads, inner // heads, stat...]
    dot_general x3 -> x12, matrix products: 68 us -> 117 us  [the longest x8 63.6 us: body(): lax.dot_general(left, right, (((0,), (0,)), ((), ())), preferred_element_...]
    psum x1 -> x0, blocking collectives: 48.2 us -> none  [body(): lax.psum((norm_gain_part, conv_weight_part, dcw[4], small[1, :heads], sma...]
    all_to_all x2 -> x9, starting transfers between devices: 9.46 us -> 43.1 us  [the longest x5 22.2 us: trade(): return lax.all_to_all(value, 'seq', 0, 0, tiled=True)]
    pallas_call x1, Pallas kernels: 57.7 us -> 29.3 us  [body(): pl.pallas_call(functools.partial(scan_kernel, heads, inner, state), grid=...]
    ppermute x0 -> x28, starting transfers between devices: none -> 23.8 us  [swap(): lax.ppermute(value, 'seq', [(i, i ^ k) for i in range(lax.axis_size('seq'...]
  transfers between devices with their start and end apart: 6 -> 42, of which waited for: 3 -> 10; matrix products, arithmetic and copies ran while one was open for 14% -> 27% of each run, Pallas kernels for 28% -> 24%
where the time goes in v2:
time: 625 us; the launch traced here: 615 us
  Pallas kernels  251 us (40%)
  matrix products  133 us (21%)
  starting transfers between devices  74.9 us (12%)
  waiting for transfers between devices  62.9 us (10%)
  other arithmetic  41.1 us (7%)
  local copies, waits for them, and re-layouts  40.7 us (7%)
  between operations  11.7 us (2%)
    pallas_call x4, Pallas kernels, back_group(): pl.pallas_call(functools.partial(back_kernel, heads, inner // heads, stat...  115 us
    dot_general x8, matrix products, body(): lax.dot_general(left, right, (((0,), (0,)), ((), ())), preferred_element_...  63.6 us
    pallas_call x1, Pallas kernels, body(): pl.pallas_call(functools.partial(gate_kernel, heads, inner, state), grid=...  53.3 us
    pallas_call x1, Pallas kernels, body(): pl.pallas_call(functools.partial(project_kernel, heads, inner, state), gr...  44.3 us
    pallas_call x1, Pallas kernels, body(): pl.pallas_call(functools.partial(scan_kernel, heads, inner, state), grid=...  29.3 us
    ppermute x28, starting transfers between devices, swap(): lax.ppermute(value, 'seq', [(i, i ^ k) for i in range(lax.axis_size('seq'...  23.8 us
    all_to_all x5, starting transfers between devices, trade(): return lax.all_to_all(value, 'seq', 0, 0, tiled=True)  22.2 us
    all_to_all x2, waiting for transfers between devices, to_all(): lax.all_to_all(local.reshape(count, rows // count, lanes + LANES), 'seq',...  18.6 us
  transfers between devices with their start and end apart: 42, of which 10 were waited for; matrix products, arithmetic and copies ran while one was open for 27% of the time, Pallas kernels for 24%

profile of v2, /device:TPU:0, one launch (start us, length us, event | category | flops | bytes accessed | tf_op | source)
XLA Modules:
  0.0 615.1 jit_solution(1134452582492240125)
XLA Ops:
  15.0 44.3 %shard_map.221 = (bf16[2048,1024]{1,0:T(8,128)(2,1)}, bf16[2048,2304]{1,0:T(8,128)(2,1)}, f32[2048,2048]{1,0:T(8,128)}, f32[2048,256]{1,0:T(8,128)}, f32[2048,23...) custom-call(bf16[2048,1024]{1,0:T(8,128)(2,1)} %hid.1, ...), custom_call_target="tpu_custom_call" | custom-call | flops 44000002048 | bytes 1048576 | tf_op jit(solution)/shard_map/pallas_call | solution.py:732
  61.9 7.1 %all-to-all-start = ((f32[32,4,2176]{2,1,0:T(4,128)}), f32[32,4,2176]{2,1,0:T(4,128)S(1)}, u32[]{:S(2)}, u32[]{:S(2)}) async-start(f32[32,4,2176]{2,1,0:T(4,128)} %reshape.185), calls=%async_computation | async-start | bytes 2228224 | tf_op jit(solution)/shard_map/all_to_all | solution.py:542
  69.0 29.3 %shard_map.222.yss = f32[2048,2048]{1,0:T(8,128)} custom-call(f32[2048,2048]{1,0:T(8,128)} %get-tuple-element.106.x_r.x, f32[2048,256]{1,0:T(8,128)} %get-tuple-element.107.bc_r.bc, f32[2048,128]{1,0:T(8,128)} %get-tuple-element.108.step_r, f32[2048,128]{1,0:T(8,128)} %get-tuple-element.109.la_rows.la_r, f32[2048,16]{1,0:T(8,128)} %copy.166.meta.meta_r, ...), custom_call_target="tpu_custom_call" | custom-call | flops 41000001536 | bytes 1048576 | tf_op jit(solution)/shard_map/pallas_call | solution.py:770
  102.1 6.0 all-to-all-start.1
  108.2 15.4 %fusion.21.z = f32[2048,2048]{1,0:T(8,128)} fusion(bf16[2048,1024]{1,0:T(8,128)(2,1)} %get-tuple-element.111, bf16[1024,4384]{0,1:T(8,128)(2,1)} %param.17), kind=kOutput, calls=%fused_computation.31 | convolution fusion | flops 8589934592 | bytes 25165824 | tf_op jit(solution)/shard_map/dot_general | solution.py:769
  123.6 10.8 %all-to-all-done.1 = f32[32,4,2048]{2,1,0:T(4,128)S(1)} async-done(((f32[32,4,2048]{2,1,0:T(4,128)}), f32[32,4,2048]{2,1,0:T(4,128)S(1)}, u32[]{:S(2)}, u32[]{:S(2)}) %all-to-all-start.1) | async-done | bytes 1048608 | tf_op jit(solution)/shard_map/all_to_all | solution.py:563
  135.7 53.3 %shard_map.224 = (bf16[2048,2048]{1,0:T(8,128)(2,1)}, f32[2048,2048]{1,0:T(8,128)}, bf16[2048,2048]{1,0:T(8,128)(2,1)}, f32[2048,128]{1,0:T(8,128)}, f32[128,217...) custom-call(f32[2048,2048]{1,0:T(8,128)} %shard_map.222.yss, f32[2048,2048]{1,0:T(8,128)} %get-tuple-element.106.x_r.x, ...), custom_call_target="tpu_custom_call" | custom-call | flops 49999998976 | bytes 1048576 | tf_op jit(solution)/shard_map/pallas_call | solution.py:784
  204.7 18.6 %all-to-all-done.2.pieces = f32[32,4,2176]{2,1,0:T(4,128)S(1)} async-done(((f32[32,4,2176]{2,1,0:T(4,128)}), f32[32,4,2176]{2,1,0:T(4,128)S(1)}, u32[]{:S(2)}, u32[]{:S(2)}) %all-to-all-start.2) | async-done | bytes 1114144 | tf_op jit(solution)/shard_map/all_to_all | solution.py:542
  233.4 9.6 %multiply_convert_fusion = f16[1024,1024]{1,0:T(8,128)(2,1)} fusion(bf16[2048,1024]{1,0:T(8,128)(2,1)} %get-tuple-element.111, bf16[2048,2048]{1,0:T(8,128)(2,1)} %get-tuple-element.115, s32[]{:T(128)S(6)} %select_n.170, f32[]{:T(128)S(6)} %div.79), kind=kOutput, calls=%fused_computation.19 | convolution fusion | flops 4297064448 | bytes 10485768 | tf_op jit(solution)/shard_map/dot_general | solution.py:816
  243.2 12.8 %fusion = bf16[2048,1024]{1,0:T(8,128)(2,1)} fusion(bf16[2048,1024]{1,0:T(8,128)(2,1)S(1)} %copy-done, bf16[2048,2048]{1,0:T(8,128)(2,1)} %get-tuple-element.114, bf16[2048,1024]{1,0:T(8,128)(2,1)S(1)} %copy-done.29), kind=kOutput, calls=%fused_computation.5 | convolution fusion | flops 8596226048 | bytes 20971520 | tf_op jit(solution)/shard_map/dot_general | solution.py:810
  259.8 9.4 %fusion.40 = f16[1024,1024]{1,0:T(8,128)(2,1)} fusion(f32[]{:T(128)S(6)} %div.74, bf16[2048,1024]{1,0:T(8,128)(2,1)} %og.1, bf16[2048,2048]{1,0:T(8,128)(2,1)} %get-tuple-element.114, s32[]{:T(128)S(6)} %select_n.170), kind=kOutput, calls=%fused_computation.48 | convolution fusion | flops 4297064448 | bytes 10485768 | tf_op jit(solution)/shard_map/dot_general | solution.py:816
  274.6 8.8 %add_multiply_fusion = f32[1024,1024]{1,0:T(8,128)S(1)} fusion(f16[1024,1024]{1,0:T(8,128)(2,1)} %collective-permute-done.3, bf16[2048,1024]{1,0:T(8,128)(2,1)} %get-tuple-element.111, bf16[2048,2048]{1,0:T(8,128)(2,1)} %get-tuple-element.115, s32[]{:T(128)S(6)} %select_n.169, f32[]{:T(128)S(6)} %div.80, f32[]{:T(128)} %bitcast.34), kind=kOutput, calls=%fused_computation.18 | convolution fusion | flops 4299161600 | bytes 14680584 | tf_op jit(solution)/shard_map/dot_general | solution.py:816
  286.2 8.2 %fusion.10 = f32[1024,1024]{1,0:T(8,128)S(1)} fusion(f16[1024,1024]{1,0:T(8,128)(2,1)} %collective-permute-done.1, f32[]{:T(128)S(6)} %div.75, f32[]{:T(128)} %bitcast.29, bf16[2048,1024]{1,0:T(8,128)(2,1)S(1)} %copy-done.6, bf16[2048,2048]{1,0:T(8,128)(2,1)} %get-tuple-element.114, s32[]{:T(128)S(6)} %select_n.169), kind=kOutput, calls=%fused_computation.17 | convolution fusion | flops 4299161600 | bytes 14680584 | tf_op jit(solution)/shard_map/dot_general | solution.py:816
  300.8 32.9 %shard_map.226 = (bf16[2048,1280]{1,0:T(8,128)(2,1)}, f32[2048,512]{1,0:T(8,128)}, f32[128,128]{1,0:T(8,128)}, f32[8,640]{1,0:T(8,128)}, f32[8,640]{1,0:T(8,128)}, /*index=5*/f32[48,640]{1,0:T(8,128)}) custom-call(f32[2048,2048]{1,0:T(8,128)} %get-tuple-element.106.x_r.x, f32[2048,256]{1,0:T(8,128)} %get-tuple-element.107.bc_r.bc, ...), custom_call_target="tpu_custom_call" | custom-call | flops 38000001024 | bytes 1048576 | tf_op jit(solution)/shard_map/pallas_call | solution.py:872
  340.7 33.0 %shard_map.227 = (bf16[2048,1280]{1,0:T(8,128)(2,1)}, f32[2048,512]{1,0:T(8,128)}, f32[128,128]{1,0:T(8,128)}, f32[8,640]{1,0:T(8,128)}, f32[8,640]{1,0:T(8,128)}, /*index=5*/f32[48,640]{1,0:T(8,128)}) custom-call(f32[2048,2048]{1,0:T(8,128)} %get-tuple-element.106.x_r.x, f32[2048,256]{1,0:T(8,128)} %get-tuple-element.107.bc_r.bc, ...), custom_call_target="tpu_custom_call", output_to_operand_aliasing={{0}: (20, {})} | custom-call | flops 38000001024 | bytes 1048576 | tf_op jit(solution)/shard_map/pallas_call | solution.py:872
  375.0 14.5 %fusion.19 = f32[2048,1024]{1,0:T(8,128)} fusion(bf16[2048,2048]{1,0:T(8,128)(2,1)} %get-tuple-element.115, bf16[1024,4384]{0,1:T(8,128)(2,1)} %param.17), kind=kOutput, calls=%fused_computation.29 | convolution fusion | flops 8589934592 | bytes 20971520 | tf_op jit(solution)/shard_map/te,de->td/dot_general | solution.py:811
  403.6 7.6 %multiply_convert_fusion.3 = f16[1024,640]{1,0:T(8,128)(2,1)} fusion(bf16[2048,1024]{1,0:T(8,128)(2,1)} %get-tuple-element.111, bf16[2048,1280]{1,0:T(8,128)(2,1)} %get-tuple-element.189, s32[]{:T(128)S(6)} %select_n.182, f32[]{:T(128)S(6)} %div.81), kind=kOutput, calls=%fused_computation.42 | convolution fusion | flops 2685665280 | bytes 8126472 | tf_op jit(solution)/shard_map/dot_general | solution.py:816
  417.7 31.9 %shard_map.229 = (bf16[2048,1280]{1,0:T(8,128)(2,1)}, f32[2048,512]{1,0:T(8,128)}, f32[128,128]{1,0:T(8,128)}, f32[8,640]{1,0:T(8,128)}, f32[8,640]{1,0:T(8,128)}, /*index=5*/f32[48,640]{1,0:T(8,128)}) custom-call(f32[2048,2048]{1,0:T(8,128)} %get-tuple-element.106.x_r.x, f32[2048,256]{1,0:T(8,128)} %get-tuple-element.107.bc_r.bc, ...), custom_call_target="tpu_custom_call" | custom-call | flops 38000001024 | bytes 1048576 | tf_op jit(solution)/shard_map/pallas_call | solution.py:872
  463.8 16.8 %shard_map.230 = (bf16[2048,1280]{1,0:T(8,128)(2,1)}, f32[8,128]{1,0:T(8,128)}, f32[8,384]{1,0:T(8,128)}, f32[8,384]{1,0:T(8,128)}, f32[48,384]{1,0:T(8,128)}) custom-call(f32[2048,2048]{1,0:T(8,128)} %get-tuple-element.106.x_r.x, f32[2048,256]{1,0:T(8,128)} %get-tuple-element.107.bc_r.bc, ...), custom_call_target="tpu_custom_call", output_to_operand_aliasing={{0}: (23, {})} | custom-call | flops 20000000000 | bytes 1048576 | tf_op jit(solution)/shard_map/pallas_call | solution.py:872
  491.4 7.6 %multiply_convert_fusion.2 = f16[1024,640]{1,0:T(8,128)(2,1)} fusion(bf16[2048,1024]{1,0:T(8,128)(2,1)} %get-tuple-element.111, bf16[2048,1280]{1,0:T(8,128)(2,1)} %get-tuple-element.190, s32[]{:T(128)S(6)} %select_n.182, f32[]{:T(128)S(6)} %div.85), kind=kOutput, calls=%fused_computation.36 | convolution fusion | flops 2685665280 | bytes 8126472 | tf_op jit(solution)/shard_map/dot_general | solution.py:816
  500.9 6.4 %all-to-all-start.5 = ((f32[32,8,128]{2,1,0:T(8,128)}), f32[32,8,128]{2,1,0:T(8,128)S(1)}, u32[]{:S(2)}, u32[]{:S(2)}) async-start(f32[32,8,128]{2,1,0:T(8,128)} %broadcast_in_dim.94), calls=%async_computation.5 | async-start | bytes 262144 | tf_op jit(solution)/shard_map/all_to_all | solution.py:571
  516.9 6.9 %add_multiply_fusion.1 = f32[1024,640]{1,0:T(8,128)S(1)} fusion(f16[1024,640]{1,0:T(8,128)(2,1)} %collective-permute-done.20, bf16[2048,1024]{1,0:T(8,128)(2,1)} %get-tuple-element.111, bf16[2048,1280]{1,0:T(8,128)(2,1)} %get-tuple-element.190, s32[]{:T(128)S(6)} %select_n.181, f32[]{:T(128)S(6)} %div.86, f32[]{:T(128)} %bitcast.58), kind=kOutput, calls=%fused_computation.35 | convolution fusion | flops 2686976000 | bytes 10748424 | tf_op jit(solution)/shard_map/dot_general | solution.py:816
  533.0 10.1 %fusion.6 = f32[2048,1024]{1,0:T(8,128)} fusion(bf16[2048,1280]{1,0:T(8,128)(2,1)} %get-tuple-element.190, bf16[4384,1024]{1,0:T(8,128)(2,1)} %bitcast.163), kind=kOutput, calls=%fused_computation.12 | convolution fusion | flops 4429185024 | bytes 15269888 | tf_op jit(solution)/shard_map/dot_general | solution.py:966
  543.2 13.2 %fusion.5 = (f32[1024]{0:T(1024)S(1)}, f32[2048]{0:T(1024)S(1)}, f32[2048,1024]{1,0:T(8,128)S(1)}) fusion(bf16[2048,1024]{1,0:T(8,128)(2,1)S(1)} %copy-done.1, f32[2048]{0:T(1024)S(1)} %copy-done.16, f32[1024]{0:T(1024)S(1)} %copy-done.15, f32[2048,1024]{1,0:T(8,128)} %fusion.6, f32[2048,1024]{1,0:T(8,128)} %fusion.19, ...), kind=kOutput, calls=%fused_computation.10 | convolution fusion | flops 5387580416 | bytes 37249024 | tf_op jit(solution)/shard_map/dot_general | solution.py:965
  (289 shorter events, 189.0 us)
Async XLA Ops:
  61.9 36.4 %all-to-all-start = ((f32[32,4,2176]{2,1,0:T(4,128)}), f32[32,4,2176]{2,1,0:T(4,128)S(1)}, u32[]{:S(2)}, u32[]{:S(2)}) async-start(f32[32,4,2176]{2,1,0:T(4,128)} %reshape.185), calls=%async_computation | async-start | bytes 2228224 | tf_op jit(solution)/shard_map/all_to_all | solution.py:542
  102.1 32.3 %all-to-all-start.1 = ((f32[32,4,2048]{2,1,0:T(4,128)}), f32[32,4,2048]{2,1,0:T(4,128)S(1)}, u32[]{:S(2)}, u32[]{:S(2)}) async-start(f32[32,4,2048]{2,1,0:T(4,128)} %shard_map.223), calls=%async_computation.1 | async-start | bytes 2097152 | tf_op jit(solution)/shard_map/all_to_all | solution.py:563
  191.7 31.7 %all-to-all-start.2 = ((f32[32,4,2176]{2,1,0:T(4,128)}), f32[32,4,2176]{2,1,0:T(4,128)S(1)}, u32[]{:S(2)}, u32[]{:S(2)}) async-start(f32[32,4,2176]{2,1,0:T(4,128)} %reshape.188), calls=%async_computation.2 | async-start | bytes 2228224 | tf_op jit(solution)/shard_map/all_to_all | solution.py:542
  226.9 46.3 %all-to-all-start.3 = ((f32[32,4,2048]{2,1,0:T(4,128)}), f32[32,4,2048]{2,1,0:T(4,128)S(1)}, u32[]{:S(2)}, u32[]{:S(2)}) async-start(f32[32,4,2048]{2,1,0:T(4,128)} %shard_map.225), calls=%async_computation.3 | async-start | bytes 2097152 | tf_op jit(solution)/shard_map/all_to_all | solution.py:563
  242.9 31.7 %collective-permute-start.3 = (f16[1024,1024]{1,0:T(8,128)(2,1)}, f16[1024,1024]{1,0:T(8,128)(2,1)}, u32[]{:S(2)}, u32[]{:S(2)}) collective-permute-start(f16[1024,1024]{1,0:T(8,128)(2,1)} %multiply_convert_fusion), channel_id=1, source_target_pairs={{0,1},{1,0},{2,3},{3,2},{4,5},{5,4},{6,7},{7,6},{8,9},{9,8},{10,11... | collective-permute-start | bytes 6291464 | tf_op jit(solution)/shard_map/ppermute | solution.py:567
  297.6 37.4 %collective-permute-start.5 = (f16[2,2,2,64,1024]{4,3,0,1,2:T(8,128)(2,1)}, f16[2,2,2,64,1024]{4,3,0,1,2:T(8,128)(2,1)}, u32[]{:S(2)}, u32[]{:S(2)}) collective-permute-start(f16[2,2,2,64,1024]{4,3,0,1,2:T(8,128)(2,1)} %fusion.51), channel_id=1, source_target_pairs={{0,2},{1,3},{2,0},{3,1},{4,6},{5,7},{6,4},{7,5},{8,10},{9,11},{10,... | collective-permute-start | bytes 3145736 | tf_op jit(solution)/shard_map/ppermute | solution.py:567
  299.3 35.6 %collective-permute-start.6 = (f16[2,2,2,64,1024]{4,3,0,1,2:T(8,128)(2,1)S(1)}, f16[2,2,2,64,1024]{4,3,0,1,2:T(8,128)(2,1)}, u32[]{:S(2)}, u32[]{:S(2)}) collective-permute-start(f16[2,2,2,64,1024]{4,3,0,1,2:T(8,128)(2,1)S(1)} %fusion.52), channel_id=1, source_target_pairs={{0,4},{1,5},{2,6},{3,7},{4,0},{5,1},{6,2},{7,3},{8,12},{9,13},{10,... | collective-permute-start | bytes 3145736 | tf_op jit(solution)/shard_map/ppermute | solution.py:567
  333.7 59.8 %collective-permute-start.7 = (f32[8,640]{1,0:T(8,128)}, f32[8,640]{1,0:T(8,128)S(1)}, u32[]{:S(2)}, u32[]{:S(2)}) collective-permute-start(f32[8,640]{1,0:T(8,128)} %get-tuple-element.135), channel_id=1, source_target_pairs={{1,0},{2,1},{3,2},{4,3},{5,4},{6,5},{7,6},{8,7},{9,8},{10,9},{11,1... | collective-permute-start | bytes 61448 | tf_op jit(solution)/shard_map/ppermute | solution.py:663
  373.7 19.7 %collective-permute-start.8 = (f32[8,640]{1,0:T(8,128)}, f32[8,640]{1,0:T(8,128)S(1)}, u32[]{:S(2)}, u32[]{:S(2)}) collective-permute-start(f32[8,640]{1,0:T(8,128)} %get-tuple-element.138), channel_id=1, source_target_pairs={{1,0},{2,1},{3,2},{4,3},{5,4},{6,5},{7,6},{8,7},{9,8},{10,9},{11,1... | collective-permute-start | bytes 61448 | tf_op jit(solution)/shard_map/ppermute | solution.py:663
  389.5 24.6 %collective-permute-start.9 = (f16[2,2,64,1024]{3,2,0,1:T(8,128)(2,1)}, f16[2,2,64,1024]{3,2,0,1:T(8,128)(2,1)S(1)}, u32[]{:S(2)}, u32[]{:S(2)}) collective-permute-start(f16[2,2,64,1024]{3,2,0,1:T(8,128)(2,1)} %get-tuple-element.143), channel_id=1, source_target_pairs={{0,4},{1,5},{2,6},{3,7},{4,0},{5,1},{6,2},{7,3},{8,12},{9,13},{10,... | collective-permute-start | bytes 1572872 | tf_op jit(solution)/shard_map/ppermute | solution.py:567
  392.9 21.2 %collective-permute-start.10 = (f16[2,2,64,1024]{3,2,0,1:T(8,128)(2,1)}, f16[2,2,64,1024]{3,2,0,1:T(8,128)(2,1)}, u32[]{:S(2)}, u32[]{:S(2)}) collective-permute-start(f16[2,2,64,1024]{3,2,0,1:T(8,128)(2,1)} %get-tuple-element.144), channel_id=1, source_target_pairs={{0,2},{1,3},{2,0},{3,1},{4,6},{5,7},{6,4},{7,5},{8,10},{9,11},{10,... | collective-permute-start | bytes 1572872 | tf_op jit(solution)/shard_map/ppermute | solution.py:567
  411.2 41.2 %collective-permute-start.13 = (f16[1024,640]{1,0:T(8,128)(2,1)}, f16[1024,640]{1,0:T(8,128)(2,1)}, u32[]{:S(2)}, u32[]{:S(2)}) collective-permute-start(f16[1024,640]{1,0:T(8,128)(2,1)} %multiply_convert_fusion.3), channel_id=1, source_target_pairs={{0,1},{1,0},{2,3},{3,2},{4,5},{5,4},{6,7},{7,6},{8,9},{9,8},{10,11... | collective-permute-start | bytes 3932168 | tf_op jit(solution)/shard_map/ppermute | solution.py:567
  415.6 35.8 %collective-permute-start.11 = (f16[2,64,1024]{2,1,0:T(8,128)(2,1)S(1)}, f16[2,64,1024]{2,1,0:T(8,128)(2,1)S(1)}, u32[]{:S(2)}, u32[]{:S(2)}) collective-permute-start(f16[2,64,1024]{2,1,0:T(8,128)(2,1)S(1)} %get-tuple-element.153), channel_id=1, source_target_pairs={{0,8},{1,9},{2,10},{3,11},{4,12},{5,13},{6,14},{7,15},{8,0},{9,1},... | collective-permute-start | bytes 786440 | tf_op jit(solution)/shard_map/ppermute | solution.py:567
  417.4 34.1 %collective-permute-start.12 = (f16[2,64,1024]{2,1,0:T(8,128)(2,1)S(1)}, f16[2,64,1024]{2,1,0:T(8,128)(2,1)S(1)}, u32[]{:S(2)}, u32[]{:S(2)}) collective-permute-start(f16[2,64,1024]{2,1,0:T(8,128)(2,1)S(1)} %get-tuple-element.154), channel_id=1, source_target_pairs={{0,8},{1,9},{2,10},{3,11},{4,12},{5,13},{6,14},{7,15},{8,0},{9,1},... | collective-permute-start | bytes 786440 | tf_op jit(solution)/shard_map/ppermute | solution.py:567
  449.7 35.9 %collective-permute-start.15 = (f32[8,640]{1,0:T(8,128)}, f32[8,640]{1,0:T(8,128)}, u32[]{:S(2)}, u32[]{:S(2)}) collective-permute-start(f32[8,640]{1,0:T(8,128)} %get-tuple-element.167), channel_id=1, source_target_pairs={{1,0},{2,1},{3,2},{4,3},{5,4},{6,5},{7,6},{8,7},{9,8},{10,9},{11,1... | collective-permute-start | bytes 61448 | tf_op jit(solution)/shard_map/ppermute | solution.py:663
  458.5 29.0 %collective-permute-start.17 = (f16[64,1024]{1,0:T(8,128)(2,1)S(1)}, f16[64,1024]{1,0:T(8,128)(2,1)S(1)}, u32[]{:S(2)}, u32[]{:S(2)}) collective-permute-start(f16[64,1024]{1,0:T(8,128)(2,1)S(1)} %get-tuple-element.178), channel_id=1, source_target_pairs={{0,16},{1,17},{2,18},{3,19},{4,20},{5,21},{6,22},{7,23},{8,24},{9,... | collective-permute-start | bytes 393224 | tf_op jit(solution)/shard_map/ppermute | solution.py:567
  463.5 24.0 %collective-permute-start.18 = (f16[64,1024]{1,0:T(8,128)(2,1)}, f16[64,1024]{1,0:T(8,128)(2,1)S(1)}, u32[]{:S(2)}, u32[]{:S(2)}) collective-permute-start(f16[64,1024]{1,0:T(8,128)(2,1)} %get-tuple-element.179), channel_id=1, source_target_pairs={{0,16},{1,17},{2,18},{3,19},{4,20},{5,21},{6,22},{7,23},{8,24},{9,... | collective-permute-start | bytes 393224 | tf_op jit(solution)/shard_map/ppermute | solution.py:567
  463.6 23.9 %collective-permute-start.19 = (f16[2,2,2,64,640]{4,3,0,1,2:T(8,128)(2,1)S(1)}, f16[2,2,2,64,640]{4,3,0,1,2:T(8,128)(2,1)S(1)}, u32[]{:S(2)}, u32[]{:S(2)}) collective-permute-start(f16[2,2,2,64,640]{4,3,0,1,2:T(8,128)(2,1)S(1)} %fusion.53), channel_id=1, source_target_pairs={{0,2},{1,3},{2,0},{3,1},{4,6},{5,7},{6,4},{7,5},{8,10},{9,11},{10,... | collective-permute-start | bytes 1966088 | tf_op jit(solution)/shard_map/ppermute | solution.py:567
  499.0 17.9 %collective-permute-start.20 = (f16[1024,640]{1,0:T(8,128)(2,1)}, f16[1024,640]{1,0:T(8,128)(2,1)}, u32[]{:S(2)}, u32[]{:S(2)}) collective-permute-start(f16[1024,640]{1,0:T(8,128)(2,1)} %multiply_convert_fusion.2), channel_id=1, source_target_pairs={{0,1},{1,0},{2,3},{3,2},{4,5},{5,4},{6,7},{7,6},{8,9},{9,8},{10,11... | collective-permute-start | bytes 3932168 | tf_op jit(solution)/shard_map/ppermute | solution.py:567
  526.6 35.8 %all-to-all-start.7 = ((f32[32,4,128]{2,1,0:T(4,128)}), f32[32,4,128]{2,1,0:T(4,128)S(1)}, u32[]{:S(2)}, u32[]{:S(2)}) async-start(f32[32,4,128]{2,1,0:T(4,128)} %bitcast.77), calls=%async_computation.7 | async-start | bytes 131072 | tf_op jit(solution)/shard_map/all_to_all | solution.py:571
  530.5 49.1 %collective-permute-start.22 = (f32[32,1024]{1,0:T(8,128)}, f32[32,1024]{1,0:T(8,128)}, u32[]{:S(2)}, u32[]{:S(2)}) collective-permute-start(f32[32,1024]{1,0:T(8,128)} %constant_dynamic-slice_fusion.3), channel_id=1, source_target_pairs={{0,1},{1,0},{2,3},{3,2},{4,5},{5,4},{6,7},{7,6},{8,9},{9,8},{10,11... | collective-permute-start | bytes 393224 | tf_op jit(solution)/shard_map/ppermute | solution.py:567
  530.6 38.3 %collective-permute-start.32 = (f32[32,1024]{1,0:T(8,128)}, f32[32,1024]{1,0:T(8,128)}, u32[]{:S(2)}, u32[]{:S(2)}) collective-permute-start(f32[32,1024]{1,0:T(8,128)} %constant_dynamic-slice_fusion), channel_id=1, source_target_pairs={{0,1},{1,0},{2,3},{3,2},{4,5},{5,4},{6,7},{7,6},{8,9},{9,8},{10,11... | collective-permute-start | bytes 393224 | tf_op jit(solution)/shard_map/ppermute | solution.py:567
  531.0 58.0 %collective-permute-start.23 = (f16[2,2,64,640]{3,2,0,1:T(8,128)(2,1)}, f16[2,2,64,640]{3,2,0,1:T(8,128)(2,1)}, u32[]{:S(2)}, u32[]{:S(2)}) collective-permute-start(f16[2,2,64,640]{3,2,0,1:T(8,128)(2,1)} %get-tuple-element.193), channel_id=1, source_target_pairs={{0,4},{1,5},{2,6},{3,7},{4,0},{5,1},{6,2},{7,3},{8,12},{9,13},{10,... | collective-permute-start | bytes 983048 | tf_op jit(solution)/shard_map/ppermute | solution.py:567
  532.7 58.1 %collective-permute-start.27 = (f16[2,2,2,64,640]{4,3,0,1,2:T(8,128)(2,1)}, f16[2,2,2,64,640]{4,3,0,1,2:T(8,128)(2,1)}, u32[]{:S(2)}, u32[]{:S(2)}) collective-permute-start(f16[2,2,2,64,640]{4,3,0,1,2:T(8,128)(2,1)} %fusion.54), channel_id=1, source_target_pairs={{0,4},{1,5},{2,6},{3,7},{4,0},{5,1},{6,2},{7,3},{8,12},{9,13},{10,... | collective-permute-start | bytes 1966088 | tf_op jit(solution)/shard_map/ppermute | solution.py:567
  (50 other events, 451.5 us)

commit v3 on v2

--- a/solution.py
+++ b/solution.py
@@ -952,32 +952,36 @@
     )
     dcw = jnp.concatenate(dcws + dcw_b, axis=1)
 
-    (away, kept) = flow_b.value
-    part_a2, part_b2, dcw, small, out_done, z_done, a_away, a_kept, away, kept = tie(
-        part_a, part_b, dcw, small, flows[0].finish(), flows[1].finish(), *flow_a.value, away, kept
+    cut = inner + 2 * width
+    late = [flow_b, flow_a]
+    part_a, part_b, away, kept = tie(part_a, part_b, *flow_b.value)
+    flow_b.value = (away, kept)
+    rest_of = lambda v: (
+        normed_grad
+        + jnp.dot(part_a, w_t[inner:cut], preferred_element_type=f32)
+        + jnp.dot(v[:, : columns - cut], w_t[cut:], preferred_element_type=f32),
     )
-    flow_a.push((a_away, a_kept))
+    (normed_all,) = beside(late, part_b, rest_of)
+    normed_all, dcw, small, out_done, z_done = tie(
+        normed_all, dcw, small, flows[0].finish(), flows[1].finish()
+    )
     conv_weight_part = dcw[0:4]
-    flow_b.push((away, kept))
-    cut = inner + 2 * width
-    normed_grad = (
-        normed_grad
-        + jnp.dot(part_a2, w_t[inner:cut], preferred_element_type=f32)
-        + jnp.dot(part_b2[:, : columns - cut], w_t[cut:], preferred_element_type=f32)
-    )
+
+    def into_hidden(normed_grad):
+        hv = hidden.astype(f32)
+        s = lax.rsqrt(jnp.mean(hv * hv, axis=1, keepdims=True) + EPS)
+        gained = normed_grad * norm_gain
+        inner_mean = jnp.mean(gained * hv, axis=1, keepdims=True)
+        hidden_grad = out_grad.astype(f32) + s * gained - hv * (s * s * s * inner_mean)
+        return jnp.sum(normed_grad * hv * s, axis=0), hidden_grad
+
+    norm_gain_part, hidden_grad = beside(late, normed_all, into_hidden)
     out_rows = jnp.concatenate(both_cores(out_done), axis=1)
     w_out_grad = out_rows.T
     z_rows = both_cores(z_done)
     a_rows = both_cores(flow_a.finish())
     b_rows = both_cores(flow_b.finish())
     w_in_grad = jnp.concatenate(list(z_rows) + list(a_rows) + list(b_rows), axis=1)[:, :columns]
-
-    hv = hidden.astype(f32)
-    s = lax.rsqrt(jnp.mean(hv * hv, axis=1, keepdims=True) + EPS)
-    gained = normed_grad * norm_gain
-    inner_mean = jnp.mean(gained * hv, axis=1, keepdims=True)
-    hidden_grad = out_grad.astype(f32) + s * gained - hv * (s * s * s * inner_mean)
-    norm_gain_part = jnp.sum(normed_grad * hv * s, axis=0)
 
     dskip_part = jnp.sum(dskip[0].reshape(heads, inner // heads), axis=1)
     early = (conv_weight_part.reshape(-1), dcw[4], small[1, :heads], small[0, :heads], dskip_part, dgain[0])

time: 625 us -> 617 us (0.987)
  waiting for transfers between devices: 62.9 us -> 53.7 us
    reduce_sum x1 -> x2, other arithmetic: 3.07 us -> 10.1 us  [the longest x1 7.03 us: into_hidden(): return (jnp.sum(normed_grad * hv * s, axis=0), hidden_grad)]
    ppermute x28, waiting for transfers between devices: 18.1 us -> 11.7 us  [swap(): lax.ppermute(value, 'seq', [(i, i ^ k) for i in range(lax.axis_size('seq'...]
  transfers between devices with their start and end apart: 42 -> 42, of which waited for: 10 -> 9; matrix products, arithmetic and copies ran while one was open for 27% -> 27% of each run, Pallas kernels for 24% -> 24%
where the time goes in v3:
time: 617 us; the launch traced here: 607 us
  Pallas kernels  251 us (41%)
  matrix products  131 us (21%)
  starting transfers between devices  77.8 us (13%)
  waiting for transfers between devices  53.7 us (9%)
  other arithmetic  42.7 us (7%)
  local copies, waits for them, and re-layouts  39.4 us (6%)
  between operations  11.8 us (2%)
    pallas_call x4, Pallas kernels, back_group(): pl.pallas_call(functools.partial(back_kernel, heads, inner // heads, stat...  115 us
    dot_general x8, matrix products, body(): lax.dot_general(left, right, (((0,), (0,)), ((), ())), preferred_element_...  63.7 us
    pallas_call x1, Pallas kernels, body(): pl.pallas_call(functools.partial(gate_kernel, heads, inner, state), grid=...  53.3 us
    pallas_call x1, Pallas kernels, body(): pl.pallas_call(functools.partial(project_kernel, heads, inner, state), gr...  44.3 us
    pallas_call x1, Pallas kernels, body(): pl.pallas_call(functools.partial(scan_kernel, heads, inner, state), grid=...  29.3 us
    ppermute x28, starting transfers between devices, swap(): lax.ppermute(value, 'seq', [(i, i ^ k) for i in range(lax.axis_size('seq'...  28.5 us
    all_to_all x5, starting transfers between devices, trade(): return lax.all_to_all(value, 'seq', 0, 0, tiled=True)  20.5 us
    all_to_all x2, waiting for transfers between devices, to_all(): lax.all_to_all(local.reshape(count, rows // count, lanes + LANES), 'seq',...  18.6 us
  transfers between devices with their start and end apart: 42, of which 9 were waited for; matrix products, arithmetic and copies ran while one was open for 27% of the time, Pallas kernels for 24%

profile of v3, /device:TPU:0, one launch (start us, length us, event | category | flops | bytes accessed | tf_op | source)
XLA Modules:
  0.0 607.2 jit_solution(11995289116632002206)
XLA Ops:
  15.0 44.3 %shard_map.221 = (bf16[2048,1024]{1,0:T(8,128)(2,1)}, bf16[2048,2304]{1,0:T(8,128)(2,1)}, f32[2048,2048]{1,0:T(8,128)}, f32[2048,256]{1,0:T(8,128)}, f32[2048,23...) custom-call(bf16[2048,1024]{1,0:T(8,128)(2,1)} %hid.1, ...), custom_call_target="tpu_custom_call" | custom-call | flops 44000002048 | bytes 1048576 | tf_op jit(solution)/shard_map/pallas_call | solution.py:732
  61.9 7.1 %all-to-all-start = ((f32[32,4,2176]{2,1,0:T(4,128)}), f32[32,4,2176]{2,1,0:T(4,128)S(1)}, u32[]{:S(2)}, u32[]{:S(2)}) async-start(f32[32,4,2176]{2,1,0:T(4,128)} %reshape.185), calls=%async_computation | async-start | bytes 2228224 | tf_op jit(solution)/shard_map/all_to_all | solution.py:542
  69.0 29.3 %shard_map.222.yss = f32[2048,2048]{1,0:T(8,128)} custom-call(f32[2048,2048]{1,0:T(8,128)} %get-tuple-element.121.x_r.x, f32[2048,256]{1,0:T(8,128)} %get-tuple-element.122.bc_r.bc, f32[2048,128]{1,0:T(8,128)} %get-tuple-element.123.step_r, f32[2048,128]{1,0:T(8,128)} %get-tuple-element.124.la_rows.la_r, f32[2048,16]{1,0:T(8,128)} %copy.166.meta.meta_r, ...), custom_call_target="tpu_custom_call" | custom-call | flops 41000001536 | bytes 1048576 | tf_op jit(solution)/shard_map/pallas_call | solution.py:770
  108.2 15.3 %fusion.21.z = f32[2048,2048]{1,0:T(8,128)} fusion(bf16[2048,1024]{1,0:T(8,128)(2,1)} %get-tuple-element.126, bf16[1024,4384]{0,1:T(8,128)(2,1)} %param.17), kind=kOutput, calls=%fused_computation.31 | convolution fusion | flops 8589934592 | bytes 25165824 | tf_op jit(solution)/shard_map/dot_general | solution.py:769
  123.5 10.9 %all-to-all-done.1 = f32[32,4,2048]{2,1,0:T(4,128)S(1)} async-done(((f32[32,4,2048]{2,1,0:T(4,128)}), f32[32,4,2048]{2,1,0:T(4,128)S(1)}, u32[]{:S(2)}, u32[]{:S(2)}) %all-to-all-start.1) | async-done | bytes 1048608 | tf_op jit(solution)/shard_map/all_to_all | solution.py:563
  135.8 53.3 %shard_map.224 = (bf16[2048,2048]{1,0:T(8,128)(2,1)}, f32[2048,2048]{1,0:T(8,128)}, bf16[2048,2048]{1,0:T(8,128)(2,1)}, f32[2048,128]{1,0:T(8,128)}, f32[128,217...) custom-call(f32[2048,2048]{1,0:T(8,128)} %shard_map.222.yss, f32[2048,2048]{1,0:T(8,128)} %get-tuple-element.121.x_r.x, ...), custom_call_target="tpu_custom_call" | custom-call | flops 49999998976 | bytes 1048576 | tf_op jit(solution)/shard_map/pallas_call | solution.py:784
  204.8 18.6 %all-to-all-done.2.pieces = f32[32,4,2176]{2,1,0:T(4,128)S(1)} async-done(((f32[32,4,2176]{2,1,0:T(4,128)}), f32[32,4,2176]{2,1,0:T(4,128)S(1)}, u32[]{:S(2)}, u32[]{:S(2)}) %all-to-all-start.2) | async-done | bytes 1114144 | tf_op jit(solution)/shard_map/all_to_all | solution.py:542
  233.4 9.6 %multiply_convert_fusion = f16[1024,1024]{1,0:T(8,128)(2,1)} fusion(bf16[2048,1024]{1,0:T(8,128)(2,1)} %get-tuple-element.126, bf16[2048,2048]{1,0:T(8,128)(2,1)} %get-tuple-element.130, s32[]{:T(128)S(6)} %select_n.170, f32[]{:T(128)S(6)} %div.79), kind=kOutput, calls=%fused_computation.19 | convolution fusion | flops 4297064448 | bytes 10485768 | tf_op jit(solution)/shard_map/dot_general | solution.py:816
  243.3 12.8 %fusion = bf16[2048,1024]{1,0:T(8,128)(2,1)} fusion(bf16[2048,1024]{1,0:T(8,128)(2,1)S(1)} %copy-done, bf16[2048,2048]{1,0:T(8,128)(2,1)} %get-tuple-element.129, bf16[2048,1024]{1,0:T(8,128)(2,1)S(1)} %copy-done.30), kind=kOutput, calls=%fused_computation.5 | convolution fusion | flops 8596226048 | bytes 20971520 | tf_op jit(solution)/shard_map/dot_general | solution.py:810
  259.9 9.4 %fusion.40 = f16[1024,1024]{1,0:T(8,128)(2,1)} fusion(f32[]{:T(128)S(6)} %div.74, bf16[2048,1024]{1,0:T(8,128)(2,1)} %og.1, bf16[2048,2048]{1,0:T(8,128)(2,1)} %get-tuple-element.129, s32[]{:T(128)S(6)} %select_n.170), kind=kOutput, calls=%fused_computation.48 | convolution fusion | flops 4297064448 | bytes 10485768 | tf_op jit(solution)/shard_map/dot_general | solution.py:816
  274.7 8.8 %add_multiply_fusion = f32[1024,1024]{1,0:T(8,128)S(1)} fusion(f16[1024,1024]{1,0:T(8,128)(2,1)} %collective-permute-done.3, bf16[2048,1024]{1,0:T(8,128)(2,1)} %get-tuple-element.126, bf16[2048,2048]{1,0:T(8,128)(2,1)} %get-tuple-element.130, s32[]{:T(128)S(6)} %select_n.169, f32[]{:T(128)S(6)} %div.80, f32[]{:T(128)} %bitcast.34), kind=kOutput, calls=%fused_computation.18 | convolution fusion | flops 4299161600 | bytes 14680584 | tf_op jit(solution)/shard_map/dot_general | solution.py:816
  286.3 8.2 %fusion.10 = f32[1024,1024]{1,0:T(8,128)S(1)} fusion(f16[1024,1024]{1,0:T(8,128)(2,1)} %collective-permute-done.1, f32[]{:T(128)S(6)} %div.75, f32[]{:T(128)} %bitcast.29, bf16[2048,1024]{1,0:T(8,128)(2,1)S(1)} %copy-done.6, bf16[2048,2048]{1,0:T(8,128)(2,1)} %get-tuple-element.129, s32[]{:T(128)S(6)} %select_n.169), kind=kOutput, calls=%fused_computation.17 | convolution fusion | flops 4299161600 | bytes 14680584 | tf_op jit(solution)/shard_map/dot_general | solution.py:816
  301.0 32.8 %shard_map.226 = (bf16[2048,1280]{1,0:T(8,128)(2,1)}, f32[2048,512]{1,0:T(8,128)}, f32[128,128]{1,0:T(8,128)}, f32[8,640]{1,0:T(8,128)}, f32[8,640]{1,0:T(8,128)}, /*index=5*/f32[48,640]{1,0:T(8,128)}) custom-call(f32[2048,2048]{1,0:T(8,128)} %get-tuple-element.121.x_r.x, f32[2048,256]{1,0:T(8,128)} %get-tuple-element.122.bc_r.bc, ...), custom_call_target="tpu_custom_call" | custom-call | flops 38000001024 | bytes 1048576 | tf_op jit(solution)/shard_map/pallas_call | solution.py:872
  340.8 33.0 %shard_map.227 = (bf16[2048,1280]{1,0:T(8,128)(2,1)}, f32[2048,512]{1,0:T(8,128)}, f32[128,128]{1,0:T(8,128)}, f32[8,640]{1,0:T(8,128)}, f32[8,640]{1,0:T(8,128)}, /*index=5*/f32[48,640]{1,0:T(8,128)}) custom-call(f32[2048,2048]{1,0:T(8,128)} %get-tuple-element.121.x_r.x, f32[2048,256]{1,0:T(8,128)} %get-tuple-element.122.bc_r.bc, ...), custom_call_target="tpu_custom_call", output_to_operand_aliasing={{0}: (20, {})} | custom-call | flops 38000001024 | bytes 1048576 | tf_op jit(solution)/shard_map/pallas_call | solution.py:872
  375.1 14.5 %fusion.19 = f32[2048,1024]{1,0:T(8,128)} fusion(bf16[2048,2048]{1,0:T(8,128)(2,1)} %get-tuple-element.130, bf16[1024,4384]{0,1:T(8,128)(2,1)} %param.17), kind=kOutput, calls=%fused_computation.29 | convolution fusion | flops 8589934592 | bytes 20971520 | tf_op jit(solution)/shard_map/te,de->td/dot_general | solution.py:811
  403.7 7.6 %multiply_convert_fusion.3 = f16[1024,640]{1,0:T(8,128)(2,1)} fusion(bf16[2048,1024]{1,0:T(8,128)(2,1)} %get-tuple-element.126, bf16[2048,1280]{1,0:T(8,128)(2,1)} %get-tuple-element.194, s32[]{:T(128)S(6)} %select_n.182, f32[]{:T(128)S(6)} %div.81), kind=kOutput, calls=%fused_computation.42 | convolution fusion | flops 2685665280 | bytes 8126472 | tf_op jit(solution)/shard_map/dot_general | solution.py:816
  417.8 31.9 %shard_map.229 = (bf16[2048,1280]{1,0:T(8,128)(2,1)}, f32[2048,512]{1,0:T(8,128)}, f32[128,128]{1,0:T(8,128)}, f32[8,640]{1,0:T(8,128)}, f32[8,640]{1,0:T(8,128)}, /*index=5*/f32[48,640]{1,0:T(8,128)}) custom-call(f32[2048,2048]{1,0:T(8,128)} %get-tuple-element.121.x_r.x, f32[2048,256]{1,0:T(8,128)} %get-tuple-element.122.bc_r.bc, ...), custom_call_target="tpu_custom_call" | custom-call | flops 38000001024 | bytes 1048576 | tf_op jit(solution)/shard_map/pallas_call | solution.py:872
  463.9 16.7 %shard_map.230 = (bf16[2048,1280]{1,0:T(8,128)(2,1)}, f32[8,128]{1,0:T(8,128)}, f32[8,384]{1,0:T(8,128)}, f32[8,384]{1,0:T(8,128)}, f32[48,384]{1,0:T(8,128)}) custom-call(f32[2048,2048]{1,0:T(8,128)} %get-tuple-element.121.x_r.x, f32[2048,256]{1,0:T(8,128)} %get-tuple-element.122.bc_r.bc, ...), custom_call_target="tpu_custom_call", output_to_operand_aliasing={{0}: (23, {})} | custom-call | flops 20000000000 | bytes 1048576 | tf_op jit(solution)/shard_map/pallas_call | solution.py:872
  491.5 7.6 %multiply_convert_fusion.2 = f16[1024,640]{1,0:T(8,128)(2,1)} fusion(bf16[2048,1024]{1,0:T(8,128)(2,1)} %get-tuple-element.126, bf16[2048,1280]{1,0:T(8,128)(2,1)} %get-tuple-element.200, s32[]{:T(128)S(6)} %select_n.182, f32[]{:T(128)S(6)} %div.83), kind=kOutput, calls=%fused_computation.36 | convolution fusion | flops 2685665280 | bytes 8126472 | tf_op jit(solution)/shard_map/dot_general | solution.py:816
  517.0 6.9 %add_multiply_fusion.1 = f32[1024,640]{1,0:T(8,128)S(1)} fusion(f16[1024,640]{1,0:T(8,128)(2,1)} %collective-permute-done.20, bf16[2048,1024]{1,0:T(8,128)(2,1)} %get-tuple-element.126, bf16[2048,1280]{1,0:T(8,128)(2,1)} %get-tuple-element.200, s32[]{:T(128)S(6)} %select_n.181, f32[]{:T(128)S(6)} %div.84, f32[]{:T(128)} %bitcast.56), kind=kOutput, calls=%fused_computation.35 | convolution fusion | flops 2686976000 | bytes 10748424 | tf_op jit(solution)/shard_map/dot_general | solution.py:816
  526.5 10.2 %fusion.6 = f32[2048,1024]{1,0:T(8,128)} fusion(bf16[2048,1280]{1,0:T(8,128)(2,1)S(1)} %bitcast.153, bf16[4384,1024]{1,0:T(8,128)(2,1)} %bitcast.167), kind=kOutput, calls=%fused_computation.12 | convolution fusion | flops 4429185024 | bytes 15269888 | tf_op jit(solution)/shard_map/dot_general | solution.py:962
  536.7 11.1 %add_add_fusion = f32[2048,1024]{1,0:T(8,128)} fusion(f32[2048,1024]{1,0:T(8,128)} %fusion.6, f32[2048,1024]{1,0:T(8,128)S(1)} %bitcast.198, bf16[2048,1280]{1,0:T(8,128)(2,1)S(1)} %bitcast.159, bf16[4384,1024]{1,0:T(8,128)(2,1)} %bitcast.168), kind=kOutput, calls=%fused_computation.11 | convolution fusion | flops 5372903424 | bytes 33030144 | tf_op jit(solution)/shard_map/dot_general | solution.py:961
  552.9 7.0 %fusion.5 = (f32[1024]{0:T(1024)S(1)}, f32[2048]{0:T(1024)S(1)}) fusion(f32[2048,1024]{1,0:T(8,128)} %add_add_fusion, bf16[2048,1024]{1,0:T(8,128)(2,1)} %hid.1, f32[2048]{0:T(1024)S(1)} %copy-done.14, f32[1024]{0:T(1024)S(1)} %copy-done.17), kind=kLoop, calls=%fused_computation.10 | loop fusion | flops 14676992 | bytes 12607488 | tf_op jit(solution)/shard_map/reduce_sum | solution.py:976
  560.2 6.7 %fusion.3 = f32[2048,1024]{1,0:T(8,128)} fusion(bf16[2048,1024]{1,0:T(8,128)(2,1)S(1)} %copy-done.1, bf16[2048,1024]{1,0:T(8,128)(2,1)S(1)} %copy-done.7, f32[2048,1024]{1,0:T(8,128)} %add_add_fusion, f32[2048]{0:T(1024)S(1)} %fusion.91, f32[1024]{0:T(1024)S(1)} %copy-done.17, f32[2048]{0:T(1024)S(1)} %copy-done.14), kind=kLoop, calls=%fused_computation.8 | loop fusion | flops 14680064 | bytes 25186304 | tf_op jit(solution)/shard_map/sub | solution.py:975
  (308 shorter events, 181.6 us)
Async XLA Ops:
  61.9 36.4 %all-to-all-start = ((f32[32,4,2176]{2,1,0:T(4,128)}), f32[32,4,2176]{2,1,0:T(4,128)S(1)}, u32[]{:S(2)}, u32[]{:S(2)}) async-start(f32[32,4,2176]{2,1,0:T(4,128)} %reshape.185), calls=%async_computation | async-start | bytes 2228224 | tf_op jit(solution)/shard_map/all_to_all | solution.py:542
  102.2 32.3 %all-to-all-start.1 = ((f32[32,4,2048]{2,1,0:T(4,128)}), f32[32,4,2048]{2,1,0:T(4,128)S(1)}, u32[]{:S(2)}, u32[]{:S(2)}) async-start(f32[32,4,2048]{2,1,0:T(4,128)} %shard_map.223), calls=%async_computation.1 | async-start | bytes 2097152 | tf_op jit(solution)/shard_map/all_to_all | solution.py:563
  191.8 31.7 %all-to-all-start.2 = ((f32[32,4,2176]{2,1,0:T(4,128)}), f32[32,4,2176]{2,1,0:T(4,128)S(1)}, u32[]{:S(2)}, u32[]{:S(2)}) async-start(f32[32,4,2176]{2,1,0:T(4,128)} %reshape.188), calls=%async_computation.2 | async-start | bytes 2228224 | tf_op jit(solution)/shard_map/all_to_all | solution.py:542
  227.0 46.4 %all-to-all-start.3 = ((f32[32,4,2048]{2,1,0:T(4,128)}), f32[32,4,2048]{2,1,0:T(4,128)S(1)}, u32[]{:S(2)}, u32[]{:S(2)}) async-start(f32[32,4,2048]{2,1,0:T(4,128)} %shard_map.225), calls=%async_computation.3 | async-start | bytes 2097152 | tf_op jit(solution)/shard_map/all_to_all | solution.py:563
  243.0 31.7 %collective-permute-start.3 = (f16[1024,1024]{1,0:T(8,128)(2,1)}, f16[1024,1024]{1,0:T(8,128)(2,1)}, u32[]{:S(2)}, u32[]{:S(2)}) collective-permute-start(f16[1024,1024]{1,0:T(8,128)(2,1)} %multiply_convert_fusion), channel_id=1, source_target_pairs={{0,1},{1,0},{2,3},{3,2},{4,5},{5,4},{6,7},{7,6},{8,9},{9,8},{10,11... | collective-permute-start | bytes 6291464 | tf_op jit(solution)/shard_map/ppermute | solution.py:567
  297.7 37.4 %collective-permute-start.5 = (f16[2,2,2,64,1024]{4,3,0,1,2:T(8,128)(2,1)}, f16[2,2,2,64,1024]{4,3,0,1,2:T(8,128)(2,1)}, u32[]{:S(2)}, u32[]{:S(2)}) collective-permute-start(f16[2,2,2,64,1024]{4,3,0,1,2:T(8,128)(2,1)} %fusion.51), channel_id=1, source_target_pairs={{0,2},{1,3},{2,0},{3,1},{4,6},{5,7},{6,4},{7,5},{8,10},{9,11},{10,... | collective-permute-start | bytes 3145736 | tf_op jit(solution)/shard_map/ppermute | solution.py:567
  299.5 35.6 %collective-permute-start.6 = (f16[2,2,2,64,1024]{4,3,0,1,2:T(8,128)(2,1)S(1)}, f16[2,2,2,64,1024]{4,3,0,1,2:T(8,128)(2,1)}, u32[]{:S(2)}, u32[]{:S(2)}) collective-permute-start(f16[2,2,2,64,1024]{4,3,0,1,2:T(8,128)(2,1)S(1)} %fusion.52), channel_id=1, source_target_pairs={{0,4},{1,5},{2,6},{3,7},{4,0},{5,1},{6,2},{7,3},{8,12},{9,13},{10,... | collective-permute-start | bytes 3145736 | tf_op jit(solution)/shard_map/ppermute | solution.py:567
  333.8 59.7 %collective-permute-start.7 = (f32[8,640]{1,0:T(8,128)}, f32[8,640]{1,0:T(8,128)S(1)}, u32[]{:S(2)}, u32[]{:S(2)}) collective-permute-start(f32[8,640]{1,0:T(8,128)} %get-tuple-element.150), channel_id=1, source_target_pairs={{1,0},{2,1},{3,2},{4,3},{5,4},{6,5},{7,6},{8,7},{9,8},{10,9},{11,1... | collective-permute-start | bytes 61448 | tf_op jit(solution)/shard_map/ppermute | solution.py:663
  373.8 19.7 %collective-permute-start.8 = (f32[8,640]{1,0:T(8,128)}, f32[8,640]{1,0:T(8,128)S(1)}, u32[]{:S(2)}, u32[]{:S(2)}) collective-permute-start(f32[8,640]{1,0:T(8,128)} %get-tuple-element.153), channel_id=1, source_target_pairs={{1,0},{2,1},{3,2},{4,3},{5,4},{6,5},{7,6},{8,7},{9,8},{10,9},{11,1... | collective-permute-start | bytes 61448 | tf_op jit(solution)/shard_map/ppermute | solution.py:663
  389.6 24.6 %collective-permute-start.9 = (f16[2,2,64,1024]{3,2,0,1:T(8,128)(2,1)}, f16[2,2,64,1024]{3,2,0,1:T(8,128)(2,1)S(1)}, u32[]{:S(2)}, u32[]{:S(2)}) collective-permute-start(f16[2,2,64,1024]{3,2,0,1:T(8,128)(2,1)} %get-tuple-element.158), channel_id=1, source_target_pairs={{0,4},{1,5},{2,6},{3,7},{4,0},{5,1},{6,2},{7,3},{8,12},{9,13},{10,... | collective-permute-start | bytes 1572872 | tf_op jit(solution)/shard_map/ppermute | solution.py:567
  393.0 21.2 %collective-permute-start.10 = (f16[2,2,64,1024]{3,2,0,1:T(8,128)(2,1)}, f16[2,2,64,1024]{3,2,0,1:T(8,128)(2,1)}, u32[]{:S(2)}, u32[]{:S(2)}) collective-permute-start(f16[2,2,64,1024]{3,2,0,1:T(8,128)(2,1)} %get-tuple-element.159), channel_id=1, source_target_pairs={{0,2},{1,3},{2,0},{3,1},{4,6},{5,7},{6,4},{7,5},{8,10},{9,11},{10,... | collective-permute-start | bytes 1572872 | tf_op jit(solution)/shard_map/ppermute | solution.py:567
  411.3 41.2 %collective-permute-start.13 = (f16[1024,640]{1,0:T(8,128)(2,1)}, f16[1024,640]{1,0:T(8,128)(2,1)}, u32[]{:S(2)}, u32[]{:S(2)}) collective-permute-start(f16[1024,640]{1,0:T(8,128)(2,1)} %multiply_convert_fusion.3), channel_id=1, source_target_pairs={{0,1},{1,0},{2,3},{3,2},{4,5},{5,4},{6,7},{7,6},{8,9},{9,8},{10,11... | collective-permute-start | bytes 3932168 | tf_op jit(solution)/shard_map/ppermute | solution.py:567
  415.8 35.8 %collective-permute-start.11 = (f16[2,64,1024]{2,1,0:T(8,128)(2,1)S(1)}, f16[2,64,1024]{2,1,0:T(8,128)(2,1)S(1)}, u32[]{:S(2)}, u32[]{:S(2)}) collective-permute-start(f16[2,64,1024]{2,1,0:T(8,128)(2,1)S(1)} %get-tuple-element.168), channel_id=1, source_target_pairs={{0,8},{1,9},{2,10},{3,11},{4,12},{5,13},{6,14},{7,15},{8,0},{9,1},... | collective-permute-start | bytes 786440 | tf_op jit(solution)/shard_map/ppermute | solution.py:567
  417.5 34.1 %collective-permute-start.12 = (f16[2,64,1024]{2,1,0:T(8,128)(2,1)S(1)}, f16[2,64,1024]{2,1,0:T(8,128)(2,1)S(1)}, u32[]{:S(2)}, u32[]{:S(2)}) collective-permute-start(f16[2,64,1024]{2,1,0:T(8,128)(2,1)S(1)} %get-tuple-element.169), channel_id=1, source_target_pairs={{0,8},{1,9},{2,10},{3,11},{4,12},{5,13},{6,14},{7,15},{8,0},{9,1},... | collective-permute-start | bytes 786440 | tf_op jit(solution)/shard_map/ppermute | solution.py:567
  449.8 35.8 %collective-permute-start.15 = (f32[8,640]{1,0:T(8,128)}, f32[8,640]{1,0:T(8,128)}, u32[]{:S(2)}, u32[]{:S(2)}) collective-permute-start(f32[8,640]{1,0:T(8,128)} %get-tuple-element.182), channel_id=1, source_target_pairs={{1,0},{2,1},{3,2},{4,3},{5,4},{6,5},{7,6},{8,7},{9,8},{10,9},{11,1... | collective-permute-start | bytes 61448 | tf_op jit(solution)/shard_map/ppermute | solution.py:663
  458.6 29.0 %collective-permute-start.17 = (f16[64,1024]{1,0:T(8,128)(2,1)S(1)}, f16[64,1024]{1,0:T(8,128)(2,1)S(1)}, u32[]{:S(2)}, u32[]{:S(2)}) collective-permute-start(f16[64,1024]{1,0:T(8,128)(2,1)S(1)} %get-tuple-element.190), channel_id=1, source_target_pairs={{0,16},{1,17},{2,18},{3,19},{4,20},{5,21},{6,22},{7,23},{8,24},{9,... | collective-permute-start | bytes 393224 | tf_op jit(solution)/shard_map/ppermute | solution.py:567
  463.6 24.0 %collective-permute-start.18 = (f16[64,1024]{1,0:T(8,128)(2,1)}, f16[64,1024]{1,0:T(8,128)(2,1)S(1)}, u32[]{:S(2)}, u32[]{:S(2)}) collective-permute-start(f16[64,1024]{1,0:T(8,128)(2,1)} %get-tuple-element.191), channel_id=1, source_target_pairs={{0,16},{1,17},{2,18},{3,19},{4,20},{5,21},{6,22},{7,23},{8,24},{9,... | collective-permute-start | bytes 393224 | tf_op jit(solution)/shard_map/ppermute | solution.py:567
  463.7 23.9 %collective-permute-start.19 = (f16[2,2,2,64,640]{4,3,0,1,2:T(8,128)(2,1)S(1)}, f16[2,2,2,64,640]{4,3,0,1,2:T(8,128)(2,1)S(1)}, u32[]{:S(2)}, u32[]{:S(2)}) collective-permute-start(f16[2,2,2,64,640]{4,3,0,1,2:T(8,128)(2,1)S(1)} %fusion.53), channel_id=1, source_target_pairs={{0,2},{1,3},{2,0},{3,1},{4,6},{5,7},{6,4},{7,5},{8,10},{9,11},{10,... | collective-permute-start | bytes 1966088 | tf_op jit(solution)/shard_map/ppermute | solution.py:567
  499.2 17.8 %collective-permute-start.20 = (f16[1024,640]{1,0:T(8,128)(2,1)}, f16[1024,640]{1,0:T(8,128)(2,1)}, u32[]{:S(2)}, u32[]{:S(2)}) collective-permute-start(f16[1024,640]{1,0:T(8,128)(2,1)} %multiply_convert_fusion.2), channel_id=1, source_target_pairs={{0,1},{1,0},{2,3},{3,2},{4,5},{5,4},{6,7},{7,6},{8,9},{9,8},{10,11... | collective-permute-start | bytes 3932168 | tf_op jit(solution)/shard_map/ppermute | solution.py:567
  524.4 23.5 %collective-permute-start.23 = (f16[2,2,64,640]{3,2,0,1:T(8,128)(2,1)S(1)}, f16[2,2,64,640]{3,2,0,1:T(8,128)(2,1)S(1)}, u32[]{:S(2)}, u32[]{:S(2)}) collective-permute-start(f16[2,2,64,640]{3,2,0,1:T(8,128)(2,1)S(1)} %get-tuple-element.202), channel_id=1, source_target_pairs={{0,4},{1,5},{2,6},{3,7},{4,0},{5,1},{6,2},{7,3},{8,12},{9,13},{10,... | collective-permute-start | bytes 983048 | tf_op jit(solution)/shard_map/ppermute | solution.py:567
  525.1 23.2 %collective-permute-start.22 = (f16[2,2,2,64,640]{4,3,0,1,2:T(8,128)(2,1)S(1)}, f16[2,2,2,64,640]{4,3,0,1,2:T(8,128)(2,1)S(1)}, u32[]{:S(2)}, u32[]{:S(2)}) collective-permute-start(f16[2,2,2,64,640]{4,3,0,1,2:T(8,128)(2,1)S(1)} %fusion.54), channel_id=1, source_target_pairs={{0,4},{1,5},{2,6},{3,7},{4,0},{5,1},{6,2},{7,3},{8,12},{9,13},{10,... | collective-permute-start | bytes 1966088 | tf_op jit(solution)/shard_map/ppermute | solution.py:567
  550.3 20.3 %all-to-all-start.7 = ((f32[32,4,128]{2,1,0:T(4,128)}), f32[32,4,128]{2,1,0:T(4,128)S(1)}, u32[]{:S(2)}, u32[]{:S(2)}) async-start(f32[32,4,128]{2,1,0:T(4,128)} %bitcast.77), calls=%async_computation.7 | async-start | bytes 131072 | tf_op jit(solution)/shard_map/all_to_all | solution.py:571
  567.4 17.6 %collective-permute-start.25 = (f16[2,64,640]{2,1,0:T(8,128)(2,1)S(1)}, f16[2,64,640]{2,1,0:T(8,128)(2,1)S(1)}, u32[]{:S(2)}, u32[]{:S(2)}) collective-permute-start(f16[2,64,640]{2,1,0:T(8,128)(2,1)S(1)} %get-tuple-element.219), channel_id=1, source_target_pairs={{0,8},{1,9},{2,10},{3,11},{4,12},{5,13},{6,14},{7,15},{8,0},{9,1},... | collective-permute-start | bytes 491528 | tf_op jit(solution)/shard_map/ppermute | solution.py:567
  586.5 18.2 %all-to-all-start.6 = ((f32[32,8,128]{2,1,0:T(8,128)}), f32[32,8,128]{2,1,0:T(8,128)S(1)}, u32[]{:S(2)}, u32[]{:S(2)}) async-start(f32[32,8,128]{2,1,0:T(8,128)} %broadcast_in_dim.96), calls=%async_computation.6 | async-start | bytes 262144 | tf_op jit(solution)/shard_map/all_to_all | solution.py:571
  (58 other events, 537.5 us)
